TPU v7x, 512 devices: a whole 4x8x8 slice. The times are simulated.
512 devices in a mesh: ctx: 16 (over z_hi, y), dp: 32 (over z_lo, x, core).
Axes of the slice: x: 4, y: 8, z: 8 (z_hi: 2, z_lo: 4; z = z_hi * 4 + z_lo), core: 2. Of those that a mesh axis runs over, the one named last changes fastest.
Arguments:
- item_first: int32 [32, 2048], P('dp', 'ctx'), may hold values from 0 to 127
- item_second: int32 [32, 2048], P('dp', 'ctx'), may hold values from 0 to 127
- lengths: int32 [32, 2], P('dp'), may hold values from 512 to 1536, as said below
- block_mask: int32 [32, 16, 16], P('dp', 'ctx'), may hold values 0 or 1
- core_first: bfloat16 [128, 1024], P('dp'), may hold values from -6 to 6
- core_second: bfloat16 [128, 1024], P('dp'), may hold values from -1 to 1
- w_proj: bfloat16 [1024, 2048], P(None, 'dp'), may hold values from -0.1875 to 0.1875
- w_out: bfloat16 [512, 1024], P(None, 'dp'), may hold values from -0.25 to 0.25
- cotangent: bfloat16 [32, 2048, 1024], P('dp', 'ctx'), may hold values from -1 to 1
Outputs:
- layer_out: bfloat16 [32, 2048, 1024], P('dp', 'ctx')
- grad_first: float32 [128, 1024], P('dp')
- grad_second: float32 [128, 1024], P('dp')
Inputs may be any that keep to these rules, and one draw needn't show every extreme that they name: A pair's two lengths sum to 2048; the first user's events come first.
All inputs are finite; a program needn't handle non-finite values. No bound on the sum of `block_mask` on one device may be relied on, other than what follows from the above.
Results may differ from a plain program's by a relative error of at most 0.022.
Values may be sent and summed in bfloat16 or wider, within the bound.
No kernel may reach another device: no remote copies, remote signals or barrier semaphores. Data moves between devices by JAX's collectives and lax.ppermute only.
A program may use at most 64 MiB of HBM per device.

v0:
```python
import jax
import jax.numpy as jnp
from jax import lax
from jax.sharding import PartitionSpec as P

DA = 32
DB = 32
R = 32
ROWS = 128
H = 4
HD = 128
E = 512
BLK = 128


epsilon = 1e-05


def normalize(values):
    average = jnp.mean(values, axis=-1, keepdims=True)
    centred = values - average
    inv_scale = lax.rsqrt(jnp.mean(centred * centred, axis=-1, keepdims=True) + epsilon)
    return (centred * inv_scale, inv_scale)


def norm_back(upstream, normed, inv_scale):
    return (
        upstream
        - jnp.mean(upstream, axis=-1, keepdims=True)
        - normed * jnp.mean(upstream * normed, axis=-1, keepdims=True)
    ) * inv_scale


def silu_slope(values):
    sigmoid_vals = jax.nn.sigmoid(values)
    return sigmoid_vals * (1.0 + values * (1.0 - sigmoid_vals))


def tile_terms(queries, key_rows, query_start, key_start, bitmap, pair_lengths):
    query_count = queries.shape[0]
    key_count = key_rows.shape[0]
    scores = jnp.einsum(
        "qhd,khd->hqk",
        queries.reshape(query_count, H, HD),
        key_rows.reshape(key_count, H, HD),
        preferred_element_type=jnp.float32,
    ) * HD ** (-0.5)
    query_pos = query_start + jnp.arange(query_count, dtype=jnp.int32)
    key_pos = key_start + jnp.arange(key_count, dtype=jnp.int32)
    query_user = query_pos >= pair_lengths[0]
    key_user = key_pos >= pair_lengths[0]
    block_rows = lax.dynamic_slice(
        bitmap, (query_start // BLK, key_start // BLK), (query_count // BLK, key_count // BLK)
    )
    block_keep = jnp.repeat(jnp.repeat(block_rows, BLK, axis=0), BLK, axis=1) == 1
    keeping = (
        (key_pos[None, :] >= query_pos[:, None])
        & (query_user[:, None] == key_user[None, :])
        & block_keep
    )
    user_length = jnp.where(query_user, pair_lengths[1], pair_lengths[0]).astype(jnp.float32)
    scaling = jnp.where(keeping, 1.0 / user_length[:, None], 0.0)
    sigmoid_vals = jax.nn.sigmoid(scores)
    attention = scores * sigmoid_vals * scaling[None]
    slopes = sigmoid_vals * (1.0 + scores * (1.0 - sigmoid_vals)) * scaling[None]
    return (attention, slopes)


def sweep(running, row_count, tile_width, advance):

    def turn(position, partial_value):
        offset = position * tile_width
        return advance(partial_value, offset)

    return lax.fori_loop(0, row_count // tile_width, turn, running)


def tile_span():
    return 512


def local(
    item_first, item_second, lengths, block_mask, core_first, core_second, w_proj, w_out, cotangent
):
    highest = lax.Precision.HIGHEST
    table_first, table_second = (
        lax.all_gather(core_first, "dp", axis=0, tiled=True),
        lax.all_gather(core_second, "dp", axis=0, tiled=True),
    )
    token_count = item_first.shape[1]
    row_ids = jnp.arange(ROWS, dtype=jnp.int32)
    picks_first = (item_first[0][:, None] == row_ids[None, :]).astype(jnp.bfloat16)
    picks_second = (item_second[0][:, None] == row_ids[None, :]).astype(jnp.bfloat16)
    rows_first = (
        jnp.dot(picks_first, table_first, preferred_element_type=jnp.float32)
        .astype(jnp.bfloat16)
        .reshape(token_count, DA, R)
    )
    rows_second = (
        jnp.dot(picks_second, table_second, preferred_element_type=jnp.float32)
        .astype(jnp.bfloat16)
        .reshape(token_count, R, DB)
    )
    embedded = (
        jnp.einsum("tar,trb->tab", rows_first, rows_second, preferred_element_type=jnp.float32)
        .reshape(token_count, DA * DB)
        .astype(jnp.bfloat16)
    )
    x_normed, x_scale = normalize(embedded.astype(jnp.float32))
    normed = x_normed.astype(jnp.bfloat16)
    proj_full, out_full = (
        lax.all_gather(w_proj, "dp", axis=1, tiled=True),
        lax.all_gather(w_out, "dp", axis=1, tiled=True),
    )
    pre_act = jnp.dot(normed, proj_full, preferred_element_type=jnp.float32)
    activated = jax.nn.silu(pre_act).astype(jnp.bfloat16)
    update_gate = activated[:, :E]
    value_rows = activated[:, E : 2 * E]
    query_rows = activated[:, 2 * E : 3 * E]
    key_rows = activated[:, 3 * E :]
    key_all, value_all, bitmap = (
        lax.all_gather(key_rows, "ctx", axis=0, tiled=True),
        lax.all_gather(value_rows, "ctx", axis=0, tiled=True),
        lax.all_gather(block_mask[0], "ctx", axis=0, tiled=True),
    )
    own_start = lax.axis_index("ctx") * token_count
    pair_lengths = lengths[0]
    key_total = key_all.shape[0]
    key_width = tile_span()

    def forward_tile(partial_value, offset):
        key_block = lax.dynamic_slice_in_dim(key_all, offset, key_width, 0)
        value_block = lax.dynamic_slice_in_dim(value_all, offset, key_width, 0)
        attention, unused = tile_terms(
            query_rows, key_block, own_start, offset, bitmap, pair_lengths
        )
        return partial_value + jnp.einsum(
            "hqk,khd->qhd",
            attention.astype(jnp.bfloat16),
            value_block.reshape(key_width, H, HD),
            preferred_element_type=jnp.float32,
        )

    zero_heads = jnp.zeros((token_count, H, HD), jnp.float32)
    mixed = sweep(zero_heads, key_total, key_width, forward_tile)
    mixed_normed, mixed_scale = normalize(mixed.reshape(token_count, E))
    hidden = (mixed_normed * update_gate.astype(jnp.float32)).astype(jnp.bfloat16)
    layer_out = (
        embedded.astype(jnp.float32) + jnp.dot(hidden, out_full, preferred_element_type=jnp.float32)
    ).astype(jnp.bfloat16)
    upstream = cotangent[0]
    hidden_grad = lax.dot_general(
        upstream, out_full, (((1,), (1,)), ((), ())), preferred_element_type=jnp.float32
    )
    gate_grad = hidden_grad * mixed_normed
    mixed_grad = norm_back(
        hidden_grad * update_gate.astype(jnp.float32), mixed_normed, mixed_scale
    ).astype(jnp.bfloat16)
    grad_heads = mixed_grad.reshape(token_count, H, HD)

    def query_tile(partial_value, offset):
        key_block = lax.dynamic_slice_in_dim(key_all, offset, key_width, 0)
        value_block = lax.dynamic_slice_in_dim(value_all, offset, key_width, 0)
        unused, slopes = tile_terms(query_rows, key_block, own_start, offset, bitmap, pair_lengths)
        pressure = jnp.einsum(
            "qhd,khd->hqk",
            grad_heads,
            value_block.reshape(key_width, H, HD),
            preferred_element_type=jnp.float32,
        )
        score_grad = (pressure * slopes).astype(jnp.bfloat16)
        return partial_value + jnp.einsum(
            "hqk,khd->qhd",
            score_grad,
            key_block.reshape(key_width, H, HD),
            preferred_element_type=jnp.float32,
        ) * HD ** (-0.5)

    query_grad = sweep(zero_heads, key_total, key_width, query_tile)
    own_values = value_rows.reshape(token_count, H, HD)
    remote_queries = lax.all_gather(query_rows, "ctx", axis=0, tiled=True)
    remote_grads = lax.all_gather(mixed_grad, "ctx", axis=0, tiled=True)
    row_count = remote_queries.shape[0]
    query_width = tile_span()

    def key_tile(partial_value, inner_offset):
        query_block = lax.dynamic_slice_in_dim(remote_queries, inner_offset, query_width, 0)
        grad_block = lax.dynamic_slice_in_dim(remote_grads, inner_offset, query_width, 0).reshape(
            query_width, H, HD
        )
        attention, slopes = tile_terms(
            query_block, key_rows, inner_offset, own_start, bitmap, pair_lengths
        )
        value_update = jnp.einsum(
            "hqk,qhd->khd",
            attention.astype(jnp.bfloat16),
            grad_block,
            preferred_element_type=jnp.float32,
        )
        pressure = jnp.einsum(
            "qhd,khd->hqk", grad_block, own_values, preferred_element_type=jnp.float32
        )
        score_grad = (pressure * slopes).astype(jnp.bfloat16)
        key_update = jnp.einsum(
            "hqk,qhd->khd",
            score_grad,
            query_block.reshape(query_width, H, HD),
            preferred_element_type=jnp.float32,
        ) * HD ** (-0.5)
        return (partial_value[0] + key_update, partial_value[1] + value_update)

    key_grad, value_grad = sweep((zero_heads, zero_heads), row_count, query_width, key_tile)
    joined = jnp.concatenate(
        [
            gate_grad,
            value_grad.reshape(token_count, E),
            query_grad.reshape(token_count, E),
            key_grad.reshape(token_count, E),
        ],
        axis=1,
    )
    pre_grad = (joined * silu_slope(pre_act)).astype(jnp.bfloat16)
    normed_grad = lax.dot_general(
        pre_grad, proj_full, (((1,), (1,)), ((), ())), preferred_element_type=jnp.float32
    )
    input_grad = upstream.astype(jnp.float32) + norm_back(normed_grad, x_normed, x_scale)
    embed_grad = input_grad.reshape(token_count, DA, DB)
    first_terms = jnp.einsum(
        "tab,trb->tar", embed_grad, rows_second.astype(jnp.float32), precision=highest
    ).reshape(token_count, DA * R)
    second_terms = jnp.einsum(
        "tar,tab->trb", rows_first.astype(jnp.float32), embed_grad, precision=highest
    ).reshape(token_count, R * DB)
    partial_first = lax.dot_general(
        picks_first.astype(jnp.float32), first_terms, (((0,), (0,)), ((), ())), precision=highest
    )
    partial_second = lax.dot_general(
        picks_second.astype(jnp.float32), second_terms, (((0,), (0,)), ((), ())), precision=highest
    )
    group_first, group_second = lax.psum((partial_first, partial_second), "ctx")
    grad_first, grad_second = (
        lax.psum_scatter(group_first, "dp", scatter_dimension=0, tiled=True),
        lax.psum_scatter(group_second, "dp", scatter_dimension=0, tiled=True),
    )
    return (layer_out[None], grad_first, grad_second)


def solution(mesh):
    placed = (
        P("dp", "ctx"),
        P("dp", "ctx"),
        P("dp", None),
        P("dp", "ctx", None),
        P("dp", None),
        P("dp", None),
        P(None, "dp"),
        P(None, "dp"),
        P("dp", "ctx", None),
    )
    return jax.shard_map(
        local,
        mesh=mesh,
        in_specs=placed,
        out_specs=(P("dp", "ctx", None), P("dp", None), P("dp", None)),
        check_vma=False,
    )
```

profile of v0, /device:TPU:1, one launch (start us, length us, event | category | flops | bytes accessed | tf_op | source)
XLA Modules:
  0.0 1020.9 jit_solution(5410425710702116445)
XLA Ops:
  8.0 48.2 %all-gather.2 = bf16[32,4,1024]{2,1,0:T(4,128)(2,1)S(1)} all-gather(bf16[1,4,1024]{2,1,0:T(4,128)(2,1)} %bitcast.252), channel_id=1, replica_groups=mesh['ctx'=16,'dp'=32] {'dp'}, dimensions={0}, use_global_device_ids=true | all-gather | bytes 270336 | tf_op jit(solution)/shard_map/all_gather | solution.py:88
  56.2 0.9 convolution_convert_fusion.1
  57.3 1.5 copy.108
  58.8 38.7 %all-gather.1 = bf16[32,4,1024]{2,1,0:T(4,128)(2,1)S(1)} all-gather(bf16[1,4,1024]{2,1,0:T(4,128)(2,1)S(1)} %bitcast.253), channel_id=1, replica_groups=mesh['ctx'=16,'dp'=32] {'dp'}, dimensions={0}, use_global_device_ids=true | all-gather | bytes 270336 | tf_op jit(solution)/shard_map/all_gather | solution.py:87
  98.0 2.6 copy.129
  100.6 2.8 fusion.88
  103.4 1.3 copy.109
  104.9 1.9 multiply_reduce_fusion
  106.9 4.7 multiply_convert_fusion.3
  113.9 47.1 %all-gather = s32[16,1,16]{2,1,0:T(1,128)S(1)} all-gather(s32[1,1,16]{2,1,0:T(1,128)S(1)} %copy-done.30), channel_id=2, replica_groups=mesh['ctx'=16,'dp'=32] {'ctx'}, dimensions={0}, use_global_device_ids=true | all-gather | bytes 1088 | tf_op jit(solution)/shard_map/all_gather | solution.py:124
  161.8 53.7 %all-gather.14.cloned.1.call-done = bf16[2048,512]{1,0:T(8,128)(2,1)} async-done(((bf16[128,512]{1,0:T(8,128)(2,1)}), bf16[2048,512]{1,0:T(8,128)(2,1)}) %all-gather.14.cloned.1.call-update) | async-done | bytes 2097168 | tf_op jit(solution)/shard_map/all_gather | solution.py:122
  215.6 4.0 copy.112
  219.6 99.6 %all-gather.12.cloned.1.call-done = bf16[2048,512]{1,0:T(8,128)(2,1)} async-done(((bf16[128,512]{1,0:T(8,128)(2,1)}), bf16[2048,512]{1,0:T(8,128)(2,1)}) %all-gather.12.cloned.1.call-update) | async-done | bytes 2097168 | tf_op jit(solution)/shard_map/all_gather | solution.py:123
  319.2 4.0 copy.111
  323.2 23.0 %while.53 = (s32[]{:T(128)}, f32[128,4,128]{0,2,1:T(8,128)S(1)}, bf16[2048,512]{0,1:T(8,128)(2,1)}, bf16[2048,512]{0,1:T(8,128)(2,1)}, bf16[128,512]{1,0:T(8,128...) while((s32[]{:T(128)}, f32[128,4,128]{0,2,1:T(8,128)S(1)}, ...), condition=%wide.region_3.4_spmd.clone, body=%wide.region_2.3_spmd.clone.sunk | while | flops 136514080 | bytes 4334300 | solution.py:75
  324.6 1.3 convert_divide_fusion.6
  326.9 1.3 constant_dynamic-slice_fusion.11
  330.4 1.3 convert_divide_fusion.6
  332.6 1.3 constant_dynamic-slice_fusion.11
  336.1 1.3 convert_divide_fusion.6
  338.4 1.3 constant_dynamic-slice_fusion.11
  341.9 1.3 convert_divide_fusion.6
  344.1 1.3 constant_dynamic-slice_fusion.11
  346.5 34.3 %all-gather.16.cloned.1.call-done = bf16[512,1024]{0,1:T(8,128)(2,1)} async-done(((bf16[512,32]{0,1:T(8,128)(2,1)}), bf16[512,1024]{0,1:T(8,128)(2,1)}) %all-gather.16.cloned.1.call-update) | async-done | bytes 1048592 | tf_op jit(solution)/shard_map/all_gather | solution.py:113
  380.8 1.6 fusion.71
  384.2 24.9 %while.55 = (s32[]{:T(128)}, f32[128,4,128]{0,2,1:T(8,128)S(1)}, bf16[2048,512]{0,1:T(8,128)(2,1)}, bf16[2048,512]{0,1:T(8,128)(2,1)}, bf16[128,4,128]{2,0,1:T(8...) while((s32[]{:T(128)}, f32[128,4,128]{0,2,1:T(8,128)S(1)}, ...), condition=%wide.region_11.12_spmd.clone, body=%wide.region_10.11_spmd.clone.sunk | while | flops 204737040 | bytes 7086820 | solution.py:75
  385.7 1.3 convert_divide_fusion.8
  388.0 1.3 constant_dynamic-slice_fusion.13
  391.9 1.3 convert_divide_fusion.8
  394.2 1.3 constant_dynamic-slice_fusion.13
  398.1 1.3 convert_divide_fusion.8
  400.4 1.3 constant_dynamic-slice_fusion.13
  404.3 1.3 convert_divide_fusion.8
  406.6 1.3 constant_dynamic-slice_fusion.13
  409.9 74.8 %all-gather.18.cloned.1.call-done = bf16[2048,512]{1,0:T(8,128)(2,1)} async-done(((bf16[128,512]{1,0:T(8,128)(2,1)}), bf16[2048,512]{1,0:T(8,128)(2,1)}) %all-gather.18.cloned.1.call-update) | async-done | bytes 2097168 | tf_op jit(solution)/shard_map/all_gather | solution.py:181
  484.7 102.9 %all-gather.20.cloned.1.call-done = bf16[2048,512]{1,0:T(8,128)(2,1)} async-done(((bf16[128,512]{1,0:T(8,128)(2,1)}), bf16[2048,512]{1,0:T(8,128)(2,1)}) %all-gather.20.cloned.1.call-update) | async-done | bytes 2097168 | tf_op jit(solution)/shard_map/all_gather | solution.py:182
  587.6 36.9 %while.54 = (s32[]{:T(128)}, f32[128,4,128]{0,2,1:T(8,128)}, f32[128,4,128]{0,2,1:T(8,128)}, bf16[2048,512]{1,0:T(8,128)(2,1)}, bf16[2048,512]{1,0:T(8,128)(2,1)...) while((s32[]{:T(128)}, f32[128,4,128]{0,2,1:T(8,128)}, ...), condition=%wide.region_9.10_spmd.clone, body=%wide.region_8.9_spmd.clone.sunk | while | flops 273551744 | bytes 14167873 | solution.py:75
  588.4 1.2 convert_divide_fusion.7
  591.3 1.3 constant_dynamic-slice_fusion.12
  593.4 1.2 fusion.160
  596.8 1.2 convert_divide_fusion.7
  599.8 1.3 constant_dynamic-slice_fusion.12
  601.9 2.2 fusion.160
  606.3 1.2 convert_divide_fusion.7
  609.3 1.3 constant_dynamic-slice_fusion.12
  611.4 2.2 fusion.160
  615.8 1.2 convert_divide_fusion.7
  618.8 1.3 constant_dynamic-slice_fusion.12
  620.9 2.2 fusion.160
  624.5 1.1 copy.140
  625.6 1.1 copy.142
  626.8 3.8 fusion.84
  630.9 1.0 copy.125
  631.9 2.9 copy.126
  634.8 2.5 fusion.90
  637.3 3.1 fusion.89
  640.5 2.8 copy.131
  643.3 1.3 fusion.76
  644.6 1.3 copy.128
  645.9 1.3 fusion.74
  647.2 1.3 dynamic-slice
  649.2 2.1 fusion.53
  651.3 277.8 %all-reduce.6.cloned.1.call-done = (f32[128,1024]{1,0:T(8,128)}, f32[128,1024]{1,0:T(8,128)}) async-done(((f32[128,1024]{1,0:T(8,128)}, f32[128,1024]{1,0:T(8,128)}), (f32[128,1024]{1,0:T(8,128)}, f32[128,1024]{1,0:T(8,128)})) %all-reduce.6.cloned.1.call-update) | async-done | bytes 1048592
  930.7 83.4 %all-reduce.3 = (f32[4,1024]{1,0:T(4,128)}, f32[4,1024]{1,0:T(4,128)}) all-reduce(f32[4,1024]{1,0:T(4,128)S(1)} %constant_dynamic-slice_fusion.7, f32[4,1024]{1,0:T(4,128)S(1)} %constant_dynamic-slice_fusion.6), channel_id=1, replica_groups=mesh['ctx'=16,'dp'=32] {'ctx'}, use_global_device_ids=true, to_apply=%region_14.15 | all-reduce | flops 8192 | bytes 65536 | tf_op jit(solution)/shard_map/psum | solution.py:240
  (248 shorter events, 54.6 us)
Async XLA Ops:
  7.2 51.6 %copy-start.20 = (bf16[4,1024]{1,0:T(4,128)(2,1)S(1)}, bf16[4,1024]{1,0:T(4,128)(2,1)}, u32[]{:S(2)}) copy-start(bf16[4,1024]{1,0:T(4,128)(2,1)} %param.19) | copy-start | bytes 24580
  7.2 90.4 %copy-start.24 = (s32[1,128]{1,0:T(1,128)S(1)}, s32[1,128]{1,0:T(1,128)}, u32[]{:S(2)}) copy-start(s32[1,128]{1,0:T(1,128)} %param.15) | copy-start | bytes 1540
  7.2 99.7 %all-gather.10.cloned.1.call-start = ((), (), s32[]{:S(2)}) async-start(), calls=%async_computation | async-start | bytes 4325376 | tf_op jit(solution)/shard_map/all_gather | solution.py:112
  7.9 207.7 %all-gather.14.cloned.1.call-start = ((), (), s32[]{:S(2)}) async-start(), calls=%async_computation.2 | async-start | bytes 2228224 | tf_op jit(solution)/shard_map/all_gather | solution.py:122
  58.8 44.6 %copy-start = (bf16[128,32,32]{2,1,0:T(8,128)(2,1)}, bf16[128,32,32]{2,1,0:T(8,128)(2,1)S(1)}, u32[]{:S(2)}) copy-start(bf16[128,32,32]{2,1,0:T(8,128)(2,1)S(1)} %copy.108) | copy-start | bytes 786436
  104.9 6.7 copy-start.6
  104.9 6.6 copy-start.26
  106.8 4.8 copy-start.28
  106.8 7.1 copy-start.30
  111.6 270.9 %copy-start.12 = (bf16[128,2048]{1,0:T(8,128)(2,1)}, bf16[128,2048]{1,0:T(8,128)(2,1)S(1)}, u32[]{:S(2)}) copy-start(bf16[128,2048]{1,0:T(8,128)(2,1)S(1)} %get-tuple-element.1250) | copy-start | bytes 1572868
  112.4 206.8 %all-gather.12.cloned.1.call-start = ((), (), s32[]{:S(2)}) async-start(), calls=%async_computation.1 | async-start | bytes 2228224 | tf_op jit(solution)/shard_map/all_gather | solution.py:123
  113.2 267.6 %all-gather.16.cloned.1.call-start = ((), (), s32[]{:S(2)}) async-start(), calls=%async_computation.3 | async-start | bytes 1081344 | tf_op jit(solution)/shard_map/all_gather | solution.py:113
  113.8 371.0 %all-gather.18.cloned.1.call-start = ((), (), s32[]{:S(2)}) async-start(), calls=%async_computation.4 | async-start | bytes 2228224 | tf_op jit(solution)/shard_map/all_gather | solution.py:181
  161.8 425.8 %all-gather.20.cloned.1.call-start = ((), (), s32[]{:S(2)}) async-start(), calls=%async_computation.5 | async-start | bytes 2228224 | tf_op jit(solution)/shard_map/all_gather | solution.py:182
  219.6 103.6 %copy-start.5 = (bf16[128,512]{1,0:T(8,128)(2,1)S(1)}, bf16[128,512]{1,0:T(8,128)(2,1)}, u32[]{:S(2)}) copy-start(bf16[128,512]{1,0:T(8,128)(2,1)} %get-tuple-element.1576) | copy-start | bytes 393220
  219.6 103.6 %copy-start.16 = (s32[1,2]{1,0:T(1,128)S(1)}, s32[1,2]{1,0:T(1,128)}, u32[]{:S(2)}) copy-start(s32[1,2]{1,0:T(1,128)} %param.17) | copy-start | bytes 28
  323.2 57.6 %copy-start.14 = (bf16[1,128,1024]{2,1,0:T(8,128)(2,1)S(1)}, bf16[1,128,1024]{2,1,0:T(8,128)(2,1)}, u32[]{:S(2)}) copy-start(bf16[1,128,1024]{2,1,0:T(8,128)(2,1)} %param.23) | copy-start | bytes 786436
  346.4 37.8 %copy-start.10 = (f32[128,512]{1,0:T(8,128)}, f32[128,512]{1,0:T(8,128)S(1)}, u32[]{:S(2)}) copy-start(f32[128,512]{1,0:T(8,128)S(1)} %copy.139) | copy-start | bytes 786436
  346.5 37.7 %copy-start.21 = (f32[128]{0:T(128)}, f32[128]{0:T(128)S(1)}, u32[]{:S(2)}) copy-start(f32[128]{0:T(128)S(1)} %add_rsqrt_fusion) | copy-start | bytes 1540
  383.3 0.7 copy-start.13
  383.9 545.2 %all-reduce.6.cloned.1.call-start = ((), (), s32[]{:S(2)}) async-start(), calls=%async_computation.6 | async-start | bytes 2097152
  384.2 203.4 %copy-start.4 = (bf16[128,512]{1,0:T(8,128)(2,1)S(1)}, bf16[128,512]{1,0:T(8,128)(2,1)}, u32[]{:S(2)}) copy-start(bf16[128,512]{1,0:T(8,128)(2,1)} %get-tuple-element.1520) | copy-start | bytes 393220
  587.6 39.1 %copy-start.7 = (f32[128,1024]{1,0:T(8,128)S(1)}, f32[128,1024]{1,0:T(8,128)}, u32[]{:S(2)}) copy-start(f32[128,1024]{1,0:T(8,128)} %copy-done.6) | copy-start | bytes 1572868
  593.4 1.2 copy-start.17
  593.4 1.2 copy-start.19
  595.4 0.7 copy-start.18
  601.9 2.2 copy-start.17
  601.9 2.2 copy-start.19
  604.9 0.7 copy-start.18
  611.4 2.2 copy-start.17
  611.4 2.2 copy-start.19
  614.4 0.7 copy-start.18
  620.9 2.2 copy-start.17
  620.9 2.2 copy-start.19
  623.8 0.7 copy-start.18
  626.7 3.9 copy-start.15
  626.7 3.9 copy-start.27
  626.7 3.9 copy-start.29
  630.9 3.9 copy-start.2
  634.8 2.5 copy-start.1
  640.5 2.8 copy-start.23
  640.5 4.1 copy-start.3
  643.3 2.6 copy-start.25
  644.6 4.6 copy-start.8
  644.6 4.6 copy-start.11
  644.6 4.6 copy-start.22
  645.9 3.3 copy-start.9
Sparse Core Ops, SparseCore 0:
  10.2 71.9 all-gather.9
  112.6 102.9 all-gather.13
  219.4 99.7 all-gather.11
  321.2 59.5 all-gather.15
  383.8 100.8 all-gather.17
  487.8 99.7 all-gather.19
  647.3 281.7 all-reduce.5
where the time goes:
time: 1030 us; the launch traced here: 1020 us
  waiting for transfers between devices  645 us (63%)
  blocking collectives  217 us (21%)
  local copies, waits for them, and re-layouts  58 us (6%)
  matrix products  44.1 us (4%)
  other arithmetic  39.1 us (4%)
  between operations  15.3 us (1%)
    unnamed x8, waiting for transfers between devices  280 us
    all_gather x1, waiting for transfers between devices, local(): remote_grads = lax.all_gather(mixed_grad, 'ctx', axis=0, tiled=True)  103 us
    all_gather x1, waiting for transfers between devices, local(): lax.all_gather(value_rows, 'ctx', axis=0, tiled=True)  99.6 us
    psum x1, blocking collectives, local(): group_first, group_second = lax.psum((partial_first, partial_second), 'ctx')  83.4 us
    all_gather x1, waiting for transfers between devices, local(): remote_queries = lax.all_gather(query_rows, 'ctx', axis=0, tiled=True)  74.8 us
    all_gather x1, waiting for transfers between devices, local(): lax.all_gather(key_rows, 'ctx', axis=0, tiled=True)  53.7 us
    all_gather x1, blocking collectives, local(): lax.all_gather(core_second, 'dp', axis=0, tiled=True)  48.2 us
    all_gather x1, blocking collectives, local(): lax.all_gather(block_mask[0], 'ctx', axis=0, tiled=True)  47.1 us
  transfers between devices with their start and end apart: 7, of which 6 were waited for; matrix products, arithmetic and copies ran while one was open for 7% of the time, Pallas kernels for 0%

commit v1 on v0

v1 whole, which is shorter than its diff:
```python
import jax
import jax.numpy as jnp
from jax import lax
from jax.experimental import pallas as pl
from jax.experimental.pallas import tpu as pltpu
from jax.sharding import PartitionSpec as P

DA = 32
DB = 32
D = 1024
R = 32
ROWS = 128
H = 4
HD = 128
E = 512
BLK = 128
SEQ = 2048
NBLK = 16
TILE = 256
NDP = 32
CHUNK = 512

EPSILON = 1e-05
SCALE = HD ** (-0.5)
F32 = jnp.float32
BF16 = jnp.bfloat16
NT_DIMS = (((1,), (1,)), ((), ()))

SMEM_SPEC = pl.BlockSpec(memory_space=pltpu.SMEM)
VMEM_SPEC = pl.BlockSpec(memory_space=pltpu.VMEM)


def mm(left, right):
    return jnp.dot(left, right, preferred_element_type=F32)


def mm_nt(left, right):
    return lax.dot_general(left, right, NT_DIMS, preferred_element_type=F32)


def sigmoid(values):
    return 0.5 * jnp.tanh(0.5 * values) + 0.5


def silu(values):
    return values * sigmoid(values)


def silu_slope(values):
    sig = sigmoid(values)
    return sig * (1.0 + values * (1.0 - sig))


def flip(values):
    return values.astype(F32).T


def normalize(values, axis):
    average = jnp.mean(values, axis=axis, keepdims=True)
    centred = values - average
    inv_scale = lax.rsqrt(jnp.mean(centred * centred, axis=axis, keepdims=True) + EPSILON)
    return (centred * inv_scale, inv_scale)


def norm_back(upstream, normed, inv_scale):
    return (
        upstream
        - jnp.mean(upstream, axis=-1, keepdims=True)
        - normed * jnp.mean(upstream * normed, axis=-1, keepdims=True)
    ) * inv_scale


def pair_onehot(firsts, seconds):
    row = lax.broadcasted_iota(jnp.int32, (2 * ROWS, BLK), 0)
    core_row = ((row >> 3) << 2) | (row & 3)
    of_first = (row & 4) == 0
    hot_first = jnp.where(of_first & (core_row == firsts), 1.0, 0.0)
    hot_second = jnp.where((~of_first) & (core_row == seconds), 1.0, 0.0)
    return jnp.concatenate([hot_first, hot_second], axis=1).astype(BF16)


def aligned(index, unit):
    return pl.multiple_of(index * unit, unit)


def user_end(last_pos, first_len):
    return jnp.where(last_pos < first_len, first_len, SEQ)


def user_start(first_pos, first_len):
    return jnp.where(first_pos < first_len, 0, first_len)


def up_tiles(pos):
    return (pos + (TILE - 1)) // TILE


def embed_kernel(
    info, indices, table, normed_t, own_terms, own_embedded, table_t, rows_first, rows_second, emb
):
    me = info[0]
    first_len = info[1]
    chunk = me // 4
    low = (user_start(chunk * CHUNK, first_len) // TILE) * 2
    high = up_tiles(user_end(chunk * CHUNK + CHUNK - 1, first_len)) * 2
    for part in range(8):
        table_t[part * 128 : (part + 1) * 128, :] = flip(
            table[:, part * 128 : (part + 1) * 128]
        ).astype(BF16)

    def block(position, carry):
        hot = pair_onehot(indices[position, 0:1, :], indices[position, 1:2, :])
        picked = mm(table_t[...], hot)
        rows_first[...] = picked[:, :BLK]
        rows_second[...] = picked[:, BLK:]

        def group(step, inner):
            base = aligned(step, 128)
            sums = [jnp.zeros((DB, BLK), F32) for _ in range(4)]
            for r in range(R):
                second = rows_second[r * DB : (r + 1) * DB, :]
                for k in range(4):
                    first = rows_first[pl.ds(base + (k * R + r), 1), :]
                    sums[k] = sums[k] + first * second
            for k in range(4):
                emb[pl.ds(pl.multiple_of(base + k * DB, DB), DB), :] = sums[k]
            return inner

        lax.fori_loop(0, 8, group, 0)
        rounded = emb[...].astype(BF16)
        normed, unused = normalize(rounded.astype(F32), 0)
        normed_t[:, pl.ds(aligned(position, BLK), BLK)] = normed.astype(BF16)

        @pl.when(position == me)
        def _():
            own_terms[0] = rows_first[...]
            own_terms[1] = rows_second[...]
            own_embedded[...] = rounded

        return carry

    lax.fori_loop(low, high, block, 0)


def weight_rows(weights, block, first=0, count=8):
    return weights[block * 8 + first : block * 8 + first + count, 0:64, :].reshape(count * 64, D)


def tile_scaling(row_first, column_first, shape, row_is_query, first_len, inverse, keep_low, keep_high):
    rows = row_first + lax.broadcasted_iota(jnp.int32, shape, 0)
    columns = column_first + lax.broadcasted_iota(jnp.int32, shape, 1)
    half = lax.broadcasted_iota(jnp.int32, shape, 1) < BLK
    query, key = (rows, columns) if row_is_query else (columns, rows)
    query_user = (query >= first_len).astype(jnp.int32)
    key_user = (key >= first_len).astype(jnp.int32)
    allowed = jnp.where(half, keep_low, keep_high)
    keep = (key >= query) & (query_user == key_user) & (allowed == 1)
    return jnp.where(keep, jnp.where(query_user == 1, inverse[1], inverse[0]), 0.0)


def forward_kernel(
    info,
    inverse,
    mask,
    normed_t,
    own_embedded,
    weights,
    cotangent,
    layer_out,
    grads_out,
    gate_out,
    keys_head,
    values_head,
    queries_head,
    slopes_out,
    keys_t,
    values_t,
    out_t,
    mixed,
    queries,
):
    me = info[0]
    first_len = info[1]
    chunk = me // 4
    head = me % 4
    kv_low = chunk * 2
    kv_high = up_tiles(user_end(chunk * CHUNK + CHUNK - 1, first_len))
    q_low = user_start(chunk * CHUNK, first_len) // TILE
    q_high = chunk * 2 + 2

    def kv_tile(position, carry):
        columns = pl.ds(aligned(position, TILE), TILE)
        piece = normed_t[:, columns]
        values_t[:, columns] = silu(mm(weight_rows(weights, 1), piece)).astype(BF16)
        keys_t[:, columns] = silu(mm(weight_rows(weights, 3), piece)).astype(BF16)
        return carry

    lax.fori_loop(kv_low, kv_high, kv_tile, 0)
    head_rows = pl.ds(aligned(head, HD), HD)
    keys_head[...] = keys_t[head_rows, :]
    values_head[...] = values_t[head_rows, :]

    def head_weights(block):
        return weights[pl.ds(block * 8 + head * 2, 2), 0:64, :].reshape(HD, D)

    def q_tile(position, carry):
        columns = pl.ds(aligned(position, TILE), TILE)
        queries_head[:, columns] = silu(mm(head_weights(2), normed_t[:, columns])).astype(BF16)
        return carry

    lax.fori_loop(q_low, q_high, q_tile, 0)

    chunk_piece = normed_t[:, pl.ds(aligned(chunk, CHUNK), CHUNK)]
    for place in range(3):
        slopes_out[:, place * HD : (place + 1) * HD] = silu_slope(
            mm(head_weights(place + 1), chunk_piece)
        ).T

    for owner in range(NDP):
        out_t[owner * 32 : owner * 32 + 16, :] = weights[owner, 64:80, :E]
        out_t[owner * 32 + 16 : owner * 32 + 32, :] = weights[owner, 64:80, E:]

    own_normed = flip(normed_t[:, pl.ds(aligned(me, BLK), BLK)]).astype(BF16)
    pre_gate = mm_nt(own_normed, weight_rows(weights, 0))
    gate = silu(pre_gate).astype(BF16).astype(F32)
    queries[...] = silu(mm_nt(own_normed, weight_rows(weights, 2))).astype(BF16)
    mixed[...] = jnp.zeros((BLK, E), F32)

    def attend(position, carry):
        columns = pl.ds(aligned(position, TILE), TILE)
        scaling = tile_scaling(
            me * BLK,
            position * TILE,
            (BLK, TILE),
            True,
            first_len,
            inverse,
            mask[me, position * 2],
            mask[me, position * 2 + 1],
        )
        for h in range(H):
            own = slice(h * HD, (h + 1) * HD)
            scores = mm(queries[:, own], keys_t[own, columns]) * SCALE
            attention = (silu(scores) * scaling).astype(BF16)
            mixed[:, own] += mm_nt(attention, values_t[own, columns])
        return carry

    lax.fori_loop(me // 2, up_tiles(user_end(me * BLK + BLK - 1, first_len)), attend, 0)

    mixed_normed, mixed_scale = normalize(mixed[...], -1)
    hidden = (mixed_normed * gate).astype(BF16)
    layer_out[...] = (flip(own_embedded[...]) + mm_nt(hidden, out_t[...])).astype(BF16)
    hidden_grad = mm(cotangent[...], out_t[...])
    gate_out[...] = (hidden_grad * mixed_normed * silu_slope(pre_gate)).astype(BF16)
    mixed_grad = norm_back(hidden_grad * gate, mixed_normed, mixed_scale).astype(BF16)
    for place in range(NBLK):
        h = place % 4
        grads_out[place] = mixed_grad[:, h * HD : (h + 1) * HD]


def backward_kernel(
    info,
    inverse,
    mask,
    keys_head,
    values_head,
    queries_head,
    grads,
    slopes,
    pre_grads,
    own_keys,
    own_values,
    own_queries,
    sums,
):
    me = info[0]
    first_len = info[1]
    chunk = me // 4
    columns = pl.ds(aligned(chunk, CHUNK), CHUNK)
    own_keys[...] = flip(keys_head[:, columns]).astype(BF16)
    own_values[...] = flip(values_head[:, columns]).astype(BF16)
    own_queries[...] = flip(queries_head[:, columns]).astype(BF16)
    for part in range(4):
        block = chunk * 4 + part
        rows = slice(part * BLK, (part + 1) * BLK)
        sums[...] = jnp.zeros((BLK, 3 * HD), F32)

        def query_side(position, carry):
            tile = pl.ds(aligned(position, TILE), TILE)
            scaling = tile_scaling(
                block * BLK,
                position * TILE,
                (BLK, TILE),
                True,
                first_len,
                inverse,
                mask[block, position * 2],
                mask[block, position * 2 + 1],
            )
            scores = mm(own_queries[rows, :], keys_head[:, tile]) * SCALE
            pressure = mm(grads[pl.ds(aligned(block, BLK), BLK), :], values_head[:, tile])
            score_grad = (pressure * silu_slope(scores) * scaling).astype(BF16)
            sums[:, HD : 2 * HD] += mm_nt(score_grad, keys_head[:, tile])
            return carry

        lax.fori_loop(
            block // 2, up_tiles(user_end(block * BLK + BLK - 1, first_len)), query_side, 0
        )

        def key_side(position, carry):
            tile = pl.ds(aligned(position, TILE), TILE)
            scaling = tile_scaling(
                block * BLK,
                position * TILE,
                (BLK, TILE),
                False,
                first_len,
                inverse,
                mask[position * 2, block],
                mask[position * 2 + 1, block],
            )
            scores = mm(own_keys[rows, :], queries_head[:, tile]) * SCALE
            sig = sigmoid(scores)
            grad_tile = grads[tile, :]
            attention = (scores * sig * scaling).astype(BF16)
            pressure = mm_nt(own_values[rows, :], grad_tile)
            slope = sig * (1.0 + scores * (1.0 - sig))
            score_grad = (pressure * slope * scaling).astype(BF16)
            sums[:, :HD] += mm(attention, grad_tile)
            sums[:, 2 * HD :] += mm_nt(score_grad, queries_head[:, tile])
            return carry

        lax.fori_loop(
            user_start(block * BLK, first_len) // TILE, block // 2 + 1, key_side, 0
        )
        pre_grads[part, :, :HD] = (sums[:, :HD] * slopes[rows, :HD]).astype(BF16)
        pre_grads[part, :, HD:] = (sums[:, HD:] * SCALE * slopes[rows, HD:]).astype(BF16)


def core_kernel(
    gate_grads,
    head_grads,
    weights,
    cotangent,
    own_embedded,
    own_terms,
    indices,
    partial_out,
    rows_second,
    grad_t,
    terms,
):
    normed_grad = mm(gate_grads[...], weight_rows(weights, 0))
    for place in range(3):
        joined = jnp.concatenate(
            [head_grads[h, :, place * HD : (place + 1) * HD] for h in range(H)], axis=1
        )
        normed_grad = normed_grad + mm(joined, weight_rows(weights, place + 1))
    x_normed, x_scale = normalize(flip(own_embedded[...]), -1)
    input_grad = cotangent[...].astype(F32) + norm_back(normed_grad, x_normed, x_scale)
    grad_t[...] = input_grad.T
    for b in range(DB):
        rows_second[b * R : (b + 1) * R, :] = own_terms.at[1][pl.ds(b, R, stride=DB), :]

    def group(step, carry):
        base = aligned(step, 128)
        sums = [jnp.zeros((R, BLK), F32) for _ in range(4)]
        for b in range(DB):
            second = rows_second[b * R : (b + 1) * R, :]
            for k in range(4):
                sums[k] = sums[k] + grad_t[pl.ds(base + (k * DB + b), 1), :] * second
        for k in range(4):
            terms[pl.ds(pl.multiple_of(base + k * R, R), R), :BLK] = sums[k]
        sums = [jnp.zeros((DB, BLK), F32) for _ in range(4)]
        for a in range(DA):
            grad = grad_t[a * DB : (a + 1) * DB, :]
            for k in range(4):
                sums[k] = sums[k] + own_terms[0, pl.ds(a * R + step * 4 + k, 1), :] * grad
        for k in range(4):
            terms[pl.ds(pl.multiple_of(base + k * DB, DB), DB), BLK:] = sums[k]
        return carry

    lax.fori_loop(0, 8, group, 0)
    hot = pair_onehot(indices[0:1, :], indices[1:2, :])
    whole = terms[...]
    upper = whole.astype(BF16)
    lower = (whole - upper.astype(F32)).astype(BF16)
    total = mm_nt(hot, upper) + mm_nt(hot, lower)
    partial_out[...] = total.astype(BF16)


def params(megabytes):
    return pltpu.CompilerParams(vmem_limit_bytes=megabytes * 1024 * 1024)


def shape(dims, kind):
    return jax.ShapeDtypeStruct(dims, kind)


def embed_stage(info, indices, table):
    return pl.pallas_call(
        embed_kernel,
        out_shape=(shape((D, SEQ), BF16), shape((2, D, BLK), F32), shape((D, BLK), BF16)),
        in_specs=[SMEM_SPEC, VMEM_SPEC, VMEM_SPEC],
        out_specs=(VMEM_SPEC,) * 3,
        scratch_shapes=[
            pltpu.VMEM((D, 2 * ROWS), BF16),
            pltpu.VMEM((D, BLK), F32),
            pltpu.VMEM((D, BLK), F32),
            pltpu.VMEM((D, BLK), F32),
        ],
        compiler_params=params(24),
        cost_estimate=pl.CostEstimate(flops=20_000_000_000, bytes_accessed=6_000_000, transcendentals=0),
        name="embed",
    )(info, indices, table)


def forward_stage(info, inverse, mask, normed_t, own_embedded, weights, cotangent):
    return pl.pallas_call(
        forward_kernel,
        out_shape=(
            shape((BLK, D), BF16),
            shape((NBLK, BLK, HD), BF16),
            shape((BLK, E), BF16),
            shape((HD, SEQ), BF16),
            shape((HD, SEQ), BF16),
            shape((HD, SEQ), BF16),
            shape((CHUNK, 3 * HD), F32),
        ),
        in_specs=[SMEM_SPEC] * 3 + [VMEM_SPEC] * 4,
        out_specs=(VMEM_SPEC,) * 7,
        scratch_shapes=[
            pltpu.VMEM((E, SEQ), BF16),
            pltpu.VMEM((E, SEQ), BF16),
            pltpu.VMEM((D, E), BF16),
            pltpu.VMEM((BLK, E), F32),
            pltpu.VMEM((BLK, E), BF16),
        ],
        compiler_params=params(40),
        cost_estimate=pl.CostEstimate(flops=8_000_000_000, bytes_accessed=12_000_000, transcendentals=0),
        name="forward",
    )(info, inverse, mask, normed_t, own_embedded, weights, cotangent)


def backward_stage(info, inverse, mask, keys_head, values_head, queries_head, grads, slopes):
    return pl.pallas_call(
        backward_kernel,
        out_shape=shape((4, BLK, 3 * HD), BF16),
        in_specs=[SMEM_SPEC] * 3 + [VMEM_SPEC] * 5,
        out_specs=VMEM_SPEC,
        scratch_shapes=[pltpu.VMEM((CHUNK, HD), BF16)] * 3 + [pltpu.VMEM((BLK, 3 * HD), F32)],
        compiler_params=params(24),
        name="backward",
    )(info, inverse, mask, keys_head, values_head, queries_head, grads, slopes)


def core_stage(gate_grads, head_grads, weights, cotangent, own_embedded, own_terms, indices):
    return pl.pallas_call(
        core_kernel,
        out_shape=shape((2 * ROWS, D), BF16),
        in_specs=[VMEM_SPEC] * 7,
        out_specs=VMEM_SPEC,
        scratch_shapes=[
            pltpu.VMEM((D, BLK), F32),
            pltpu.VMEM((D, BLK), F32),
            pltpu.VMEM((D, 2 * BLK), F32),
        ],
        compiler_params=params(32),
        name="cores",
    )(gate_grads, head_grads, weights, cotangent, own_embedded, own_terms, indices)


def pack_weights(w_proj, w_out):
    out_t = w_out.T
    return jnp.concatenate([w_proj.T, jnp.concatenate([out_t[:16], out_t[16:]], axis=1)], axis=0)


def pack_indices(item_first, item_second, block_mask):
    mask_row = jnp.pad(block_mask[0], ((0, 0), (0, BLK - NBLK)))
    return jnp.concatenate(
        [item_first, item_second, mask_row, jnp.zeros((5, BLK), jnp.int32)], axis=0
    )


def spread(values, axis, count):
    copies = jnp.broadcast_to(values[None], (count,) + values.shape)
    return lax.all_to_all(copies, axis, 0, 0)


def local(
    item_first, item_second, lengths, block_mask, core_first, core_second, w_proj, w_out, cotangent
):
    me = lax.axis_index("ctx").astype(jnp.int32)
    weights = lax.all_gather(pack_weights(w_proj, w_out), "dp", axis=0, tiled=True)
    weights = weights.reshape(NDP, 80, D)
    table = spread(jnp.concatenate([core_first, core_second], axis=0), "dp", NDP)
    table = table.reshape(2 * ROWS, D)
    own_indices = pack_indices(item_first, item_second, block_mask)
    indices = spread(own_indices, "ctx", NBLK)
    mask = indices[:, 2, :NBLK]
    info = jnp.stack([me, lengths[0, 0], lengths[0, 1], me])
    inverse = 1.0 / lengths[0].astype(F32)
    upstream = cotangent[0]

    normed_t, own_terms, own_embedded = embed_stage(info, indices, table)
    layer_out, grads, gate_grads, keys_head, values_head, queries_head, slopes = forward_stage(
        info, inverse, mask, normed_t, own_embedded, weights, upstream
    )
    grads = lax.all_to_all(grads, "ctx", 0, 0).reshape(SEQ, HD)
    pre_grads = backward_stage(
        info, inverse, mask, keys_head, values_head, queries_head, grads, slopes
    )
    groups = [[4 * c + h for h in range(4)] for c in range(4)]
    head_grads = lax.all_to_all(pre_grads, "ctx", 0, 0, axis_index_groups=groups)
    partial = core_stage(
        gate_grads, head_grads, weights, upstream, own_embedded, own_terms, own_indices
    )
    received = lax.all_to_all(partial.reshape(NDP, 8, D), "dp", 0, 0)
    pair_sum = jnp.sum(received.astype(F32), axis=0)
    total = jnp.sum(spread(pair_sum, "ctx", NBLK), axis=0)
    return (layer_out[None], total[:4], total[4:])


def solution(mesh):
    placed = (
        P("dp", "ctx"),
        P("dp", "ctx"),
        P("dp", None),
        P("dp", "ctx", None),
        P("dp", None),
        P("dp", None),
        P(None, "dp"),
        P(None, "dp"),
        P("dp", "ctx", None),
    )
    return jax.shard_map(
        local,
        mesh=mesh,
        in_specs=placed,
        out_specs=(P("dp", "ctx", None), P("dp", None), P("dp", None)),
        check_vma=False,
    )
```

time: 1030 us -> 226 us (0.22)
  waiting for transfers between devices: 645 us -> 39 us
  blocking collectives: 217 us -> 106 us
  local copies, waits for them, and re-layouts: 58 us -> 11.1 us
  matrix products: 44.1 us -> 0 us
  other arithmetic: 39.1 us -> 5.2 us
  starting transfers between devices: 0.46 us -> 25.5 us
  Pallas kernels: 0 us -> 24.5 us
    all_gather x6 -> x1, waiting for transfers between devices: 365 us -> 11.7 us  [local(): lax.all_gather(pack_weights(w_proj, w_out), 'dp', axis=0, tiled=True)]
    unnamed x8 -> x1, waiting for transfers between devices: 280 us -> 0.02 us
    all_gather x3 -> x0, blocking collectives: 134 us -> none  [the longest x1 48.2 us: local(): lax.all_gather(core_second, 'dp', axis=0, tiled=True)]
    all_to_all x0 -> x4, blocking collectives: none -> 106 us  [the longest x1 37.7 us: local(): received = lax.all_to_all(partial.reshape(NDP, 8, D), 'dp', 0, 0)]
    psum x1 -> x0, blocking collectives: 83.4 us -> none  [local(): group_first, group_second = lax.psum((partial_first, partial_second), 'ctx')]
    dot_general x35 -> x0, matrix products: 44.1 us -> none  [the longest x4 7.78 us: key_tile(): jnp.einsum('hqk,qhd->khd', attention.astype(jnp.bfloat16), grad_block, pr...]
    all_to_all x0 -> x2, waiting for transfers between devices: none -> 27.3 us  [spread(): return lax.all_to_all(copies, axis, 0, 0)]
    all_to_all x0 -> x2, starting transfers between devices: none -> 25.4 us  [spread(): return lax.all_to_all(copies, axis, 0, 0)]
  transfers between devices with their start and end apart: 7 -> 3, of which waited for: 6 -> 3; matrix products, arithmetic and copies ran while one was open for 7% -> 3% of each run, Pallas kernels for 0% -> 4%
where the time goes in v1:
time: 226 us; the launch traced here: 225 us
  blocking collectives  106 us (47%)
  waiting for transfers between devices  39 us (17%)
  starting transfers between devices  25.5 us (11%)
  Pallas kernels  24.5 us (11%)
  between operations  14.1 us (6%)
  local copies, waits for them, and re-layouts  11.1 us (5%)
  other arithmetic  5.2 us (2%)
    all_to_all x1, blocking collectives, local(): received = lax.all_to_all(partial.reshape(NDP, 8, D), 'dp', 0, 0)  37.7 us
    all_to_all x1, blocking collectives, spread(): return lax.all_to_all(copies, axis, 0, 0)  28.4 us
    all_to_all x1, blocking collectives, local(): grads = lax.all_to_all(grads, 'ctx', 0, 0).reshape(SEQ, HD)  28.4 us
    all_to_all x2, waiting for transfers between devices, spread(): return lax.all_to_all(copies, axis, 0, 0)  27.3 us
    all_to_all x2, starting transfers between devices, spread(): return lax.all_to_all(copies, axis, 0, 0)  25.4 us
    all_gather x1, waiting for transfers between devices, local(): lax.all_gather(pack_weights(w_proj, w_out), 'dp', axis=0, tiled=True)  11.7 us
    all_to_all x1, blocking collectives, local(): lax.all_to_all(pre_grads, 'ctx', 0, 0, axis_index_groups=groups)  11.4 us
    pallas_call x1, Pallas kernels, embed_stage(): pl.pallas_call(embed_kernel, out_shape=(shape((D, SEQ), BF16), shape((2,...  8.8 us
  transfers between devices with their start and end apart: 3, of which 3 were waited for; matrix products, arithmetic and copies ran while one was open for 3% of the time, Pallas kernels for 4%

profile of v1, /device:TPU:1, one launch (start us, length us, event | category | flops | bytes accessed | tf_op | source)
XLA Modules:
  0.0 225.3 jit_solution(14302152534038648257)
XLA Ops:
  7.2 0.0 all-gather.2.cloned.1.call-start
  7.2 0.7 fusion.2
  7.9 1.6 maximum_maximum_fusion
  9.5 0.0 all-gather.2.cloned.1.call-update
  9.6 0.1 pad.13.clone
  9.6 0.8 fusion.indices
  10.4 0.6 broadcast_in_dim.11
  11.0 16.2 %all-to-all-start = ((s32[16,8,128]{2,1,0:T(8,128)}), s32[16,8,128]{2,1,0:T(8,128)S(1)}, u32[]{:S(2)}, u32[]{:S(2)}) async-start(s32[16,8,128]{2,1,0:T(8,128)} %broadcast_in_dim.11), calls=%async_computation | async-start | bytes 131072 | tf_op jit(solution)/shard_map/all_to_all | solution.py:487
  27.2 0.7 pad_maximum_fusion
  28.0 10.6 %all-to-all-done.indices = s32[16,8,128]{2,1,0:T(8,128)S(1)} async-done(((s32[16,8,128]{2,1,0:T(8,128)}), s32[16,8,128]{2,1,0:T(8,128)S(1)}, u32[]{:S(2)}, u32[]{:S(2)}) %all-to-all-start) | async-done | bytes 65568 | tf_op jit(solution)/shard_map/all_to_all | solution.py:487
  38.6 0.9 broadcast_in_dim.12
  39.5 9.2 %all-to-all-start.1 = ((bf16[32,8,1024]{2,1,0:T(8,128)(2,1)}), bf16[32,8,1024]{2,1,0:T(8,128)(2,1)S(1)}, u32[]{:S(2)}, u32[]{:S(2)}) async-start(bf16[32,8,1024]{2,1,0:T(8,128)(2,1)} %broadcast_in_dim.12), calls=%async_computation.1 | async-start | bytes 1048576 | tf_op jit(solution)/shard_map/all_to_all | solution.py:487
  48.7 1.3 fusion.3
  50.1 1.4 pad_add_fusion.1.info
  51.4 0.7 divide_bitcast_fusion.inverse
  52.1 16.7 %all-to-all-done.1 = bf16[32,8,1024]{2,1,0:T(8,128)(2,1)S(1)} async-done(((bf16[32,8,1024]{2,1,0:T(8,128)(2,1)}), bf16[32,8,1024]{2,1,0:T(8,128)(2,1)S(1)}, u32[]{:S(2)}, u32[]{:S(2)}) %all-to-all-start.1) | async-done | bytes 524320 | tf_op jit(solution)/shard_map/all_to_all | solution.py:487
  68.8 0.0 copy-start.1
  68.8 8.8 %embed.1 = (bf16[1024,2048]{1,0:T(8,128)(2,1)S(1)}, f32[2,1024,128]{2,1,0:T(8,128)S(1)}, bf16[1024,128]{1,0:T(8,128)(2,1)S(1)}) custom-call(s32[4]{0:T(128)S(1)} %pad_add_fusion.1.info, s32[16,8,128]{2,1,0:T(8,128)S(1)} %all-to-all-done.indices, bf16[256,1024]{1,0:T(8,128)(2,1)S(1)} %bitcast.21), custom_call_target="tpu_custom_call" | custom-call | flops 20000000000 | bytes 6000000 | tf_op jit(solution)/shard_map/embed/pallas_call | solution.py:401
  77.6 0.0 copy-start.2
  77.6 2.0 copy-done.2
  79.6 11.7 %all-gather.2.cloned.1.call-done = bf16[2560,1024]{1,0:T(8,128)(2,1)} async-done(((bf16[80,1024]{1,0:T(8,128)(2,1)}), bf16[2560,1024]{1,0:T(8,128)(2,1)}) %all-gather.2.cloned.1.call-update) | async-done | bytes 5242896 | tf_op jit(solution)/shard_map/all_gather | solution.py:494
  91.3 0.0 copy-done.1
  91.3 0.0 copy-start
  91.3 2.5 %copy-done = bf16[2560,1024]{1,0:T(8,128)(2,1)S(1)} copy-done((bf16[2560,1024]{1,0:T(8,128)(2,1)S(1)}, bf16[2560,1024]{1,0:T(8,128)(2,1)}, u32[]{:S(2)}) %copy-start) | copy-done | bytes 5242904
  93.8 0.0 copy-start.3
  93.8 2.2 copy-done.3
  96.0 6.6 %forward.1 = (bf16[128,1024]{1,0:T(8,128)(2,1)}, bf16[16,128,128]{2,1,0:T(8,128)(2,1)S(1)}, bf16[128,512]{1,0:T(8,128)(2,1)S(1)}, bf16[128,2048]{1,0:T(8,128)(2,...) custom-call(s32[4]{0:T(128)S(1)} %pad_add_fusion.1.info, ...), custom_call_target="tpu_custom_call" | custom-call | flops 8000000000 | bytes 12000000 | tf_op jit(solution)/shard_map/forward/pallas_call | solution.py:419
  102.5 28.4 %all_to_all.30 = bf16[16,128,128]{2,1,0:T(8,128)(2,1)S(1)} all-to-all(bf16[16,128,128]{2,1,0:T(8,128)(2,1)S(1)} %get-tuple-element.20), channel_id=1, replica_groups=mesh['ctx'=16,'dp'=32] {'ctx'}, dimensions={0} | all-to-all | bytes 1048576 | tf_op jit(solution)/shard_map/all_to_all | solution.py:509
  130.9 4.9 %backward.1 = bf16[4,128,384]{2,1,0:T(8,128)(2,1)S(1)} custom-call(s32[4]{0:T(128)S(1)} %pad_add_fusion.1.info, f32[2]{0:T(128)S(1)} %divide_bitcast_fusion.inverse, s32[16,16]{1,0:T(8,128)S(1)} %bitcast.25, bf16[128,2048]{1,0:T(8,128)(2,1)S(1)} %get-tuple-element.17.keys_head, bf16[128,2048]{1,0:T(8,128)(2,1)S(1)} %get-tuple-element.18.values_head, ...), custom_call_target="tpu_custom_call" | custom-call | tf_op jit(solution)/shard_map/backward/pallas_call | solution.py:446
  135.9 11.4 %all_to_all.31.head_grads = bf16[4,128,384]{2,1,0:T(8,128)(2,1)S(1)} all-to-all(bf16[4,128,384]{2,1,0:T(8,128)(2,1)S(1)} %backward.1), channel_id=1, replica_groups={{0,32,64,96},{128,160,192,224},{256,288,320,352},{384,416,448,480},{1,3..., dimensions={0} | all-to-all | bytes 786432 | tf_op jit(solution)/shard_map/all_to_all | solution.py:514
  147.3 4.1 %cores.1 = bf16[256,1024]{1,0:T(8,128)(2,1)S(1)} custom-call(bf16[128,512]{1,0:T(8,128)(2,1)S(1)} %get-tuple-element.16.gate_grads, bf16[4,128,384]{2,1,0:T(8,128)(2,1)S(1)} %all_to_all.31.head_grads, bf16[32,80,1024]{2,1,0:T(8,128)(2,1)S(1)} %bitcast.18, bf16[128,1024]{1,0:T(8,128)(2,1)S(1)} %bitcast.23, ...), custom_call_target="tpu_custom_call" | custom-call | tf_op jit(solution)/shard_map/cores/pallas_call | solution.py:458
  151.5 37.7 %all_to_all.32 = bf16[32,8,1024]{2,1,0:T(8,128)(2,1)S(1)} all-to-all(bf16[32,8,1024]{2,1,0:T(8,128)(2,1)S(1)} %bitcast.19), channel_id=1, replica_groups=mesh['ctx'=16,'dp'=32] {'dp'}, dimensions={0} | all-to-all | bytes 1048576 | tf_op jit(solution)/shard_map/all_to_all | solution.py:518
  189.2 0.1 convert_reduce_fusion
  189.3 28.4 %all_to_all.33 = f32[16,8,1024]{2,1,0:T(8,128)S(1)} all-to-all(f32[16,8,1024]{2,1,0:T(8,128)S(1)} %broadcast_in_dim.28), channel_id=1, replica_groups=mesh['ctx'=16,'dp'=32] {'ctx'}, dimensions={0} | all-to-all | bytes 1048576 | tf_op jit(solution)/shard_map/all_to_all | solution.py:487
  217.8 0.6 fusion.1
  (4 shorter events, 0.1 us)
Async XLA Ops:
  7.2 84.1 %all-gather.2.cloned.1.call-start = ((), (), s32[]{:S(2)}) async-start(), calls=%async_computation.6 | async-start | bytes 5406720 | tf_op jit(solution)/shard_map/all_gather | solution.py:494
  11.0 27.5 %all-to-all-start = ((s32[16,8,128]{2,1,0:T(8,128)}), s32[16,8,128]{2,1,0:T(8,128)S(1)}, u32[]{:S(2)}, u32[]{:S(2)}) async-start(s32[16,8,128]{2,1,0:T(8,128)} %broadcast_in_dim.11), calls=%async_computation | async-start | bytes 131072 | tf_op jit(solution)/shard_map/all_to_all | solution.py:487
  39.5 29.3 %all-to-all-start.1 = ((bf16[32,8,1024]{2,1,0:T(8,128)(2,1)}), bf16[32,8,1024]{2,1,0:T(8,128)(2,1)S(1)}, u32[]{:S(2)}, u32[]{:S(2)}) async-start(bf16[32,8,1024]{2,1,0:T(8,128)(2,1)} %broadcast_in_dim.12), calls=%async_computation.1 | async-start | bytes 1048576 | tf_op jit(solution)/shard_map/all_to_all | solution.py:487
  68.8 22.5 %copy-start.1 = (bf16[1,128,1024]{2,1,0:T(8,128)(2,1)S(1)}, bf16[1,128,1024]{2,1,0:T(8,128)(2,1)}, u32[]{:S(2)}) copy-start(bf16[1,128,1024]{2,1,0:T(8,128)(2,1)} %param.17) | copy-start | bytes 786436
  77.6 2.0 copy-start.2
  91.3 2.5 %copy-start = (bf16[2560,1024]{1,0:T(8,128)(2,1)S(1)}, bf16[2560,1024]{1,0:T(8,128)(2,1)}, u32[]{:S(2)}) copy-start(bf16[2560,1024]{1,0:T(8,128)(2,1)} %all-gather.2.cloned.1.call-done) | copy-start | bytes 15728644
  93.8 2.2 copy-start.3
Sparse Core Ops, SparseCore 0:
  10.7 80.5 all-gather.1

commit v2 on v1

v2 whole, which is shorter than its diff:
```python
import jax
import jax.numpy as jnp
from jax import lax
from jax.experimental import pallas as pl
from jax.experimental.pallas import tpu as pltpu
from jax.sharding import PartitionSpec as P

DA = 32
DB = 32
D = 1024
R = 32
ROWS = 128
H = 4
HD = 128
E = 512
BLK = 128
SEQ = 2048
NBLK = 16
TILE = 256
NDP = 32
CHUNK = 512
WIDE = 8

EPSILON = 1e-05
SCALE = HD ** (-0.5)
F32 = jnp.float32
BF16 = jnp.bfloat16
NT_DIMS = (((1,), (1,)), ((), ()))

SMEM_SPEC = pl.BlockSpec(memory_space=pltpu.SMEM)
VMEM_SPEC = pl.BlockSpec(memory_space=pltpu.VMEM)
ANY_SPEC = pl.BlockSpec(memory_space=pl.ANY)


def mm(left, right):
    return jnp.dot(left, right, preferred_element_type=F32)


def mm_nt(left, right):
    return lax.dot_general(left, right, NT_DIMS, preferred_element_type=F32)


def sigmoid(values):
    return 0.5 * jnp.tanh(0.5 * values) + 0.5


def silu(values):
    return values * sigmoid(values)


def silu_slope(values):
    sig = sigmoid(values)
    return sig * (1.0 + values * (1.0 - sig))


def flip(values):
    return values.astype(F32).T


def normalize(values, axis):
    average = jnp.mean(values, axis=axis, keepdims=True)
    centred = values - average
    inv_scale = lax.rsqrt(jnp.mean(centred * centred, axis=axis, keepdims=True) + EPSILON)
    return (centred * inv_scale, inv_scale)


def norm_back(upstream, normed, inv_scale):
    return (
        upstream
        - jnp.mean(upstream, axis=-1, keepdims=True)
        - normed * jnp.mean(upstream * normed, axis=-1, keepdims=True)
    ) * inv_scale


def pair_onehot(firsts, seconds):
    row = lax.broadcasted_iota(jnp.int32, (2 * ROWS, BLK), 0)
    core_row = ((row >> 3) << 2) | (row & 3)
    of_first = (row & 4) == 0
    hot_first = jnp.where(of_first & (core_row == firsts), 1.0, 0.0)
    hot_second = jnp.where((~of_first) & (core_row == seconds), 1.0, 0.0)
    return jnp.concatenate([hot_first, hot_second], axis=1).astype(BF16)


def aligned(index, unit):
    return pl.multiple_of(index * unit, unit)


def user_end(last_pos, first_len):
    return jnp.where(last_pos < first_len, first_len, SEQ)


def user_start(first_pos, first_len):
    return jnp.where(first_pos < first_len, 0, first_len)


def up_tiles(pos):
    return (pos + (TILE - 1)) // TILE


def embed_kernel(
    info, indices, table, normed_t, chunk_terms, chunk_embedded, table_t, rows_first, rows_second, emb
):
    me = info[0]
    first_len = info[1]
    chunk = me // 4
    low = (user_start(chunk * CHUNK, first_len) // TILE) * 2
    high = up_tiles(user_end(chunk * CHUNK + CHUNK - 1, first_len)) * 2
    for part in range(8):
        table_t[part * 128 : (part + 1) * 128, :] = flip(
            table[:, part * 128 : (part + 1) * 128]
        ).astype(BF16)

    def block(position, carry):
        hot = pair_onehot(indices[position, 0:1, :], indices[position, 1:2, :])
        picked = mm(table_t[...], hot)
        rows_first[...] = picked[:, :BLK]
        rows_second[...] = picked[:, BLK:]

        def group(step, inner):
            base = aligned(step, WIDE * 32)
            sums = [jnp.zeros((DB, BLK), F32) for _ in range(WIDE)]
            for r in range(R):
                second = rows_second[r * DB : (r + 1) * DB, :]
                for k in range(WIDE):
                    first = rows_first[pl.ds(base + (k * R + r), 1), :]
                    sums[k] = sums[k] + first * second
            for k in range(WIDE):
                emb[pl.ds(pl.multiple_of(base + k * DB, DB), DB), :] = sums[k]
            return inner

        lax.fori_loop(0, DA // WIDE, group, 0)
        rounded = emb[...].astype(BF16)
        normed, unused = normalize(rounded.astype(F32), 0)
        normed_t[:, pl.ds(aligned(position, BLK), BLK)] = normed.astype(BF16)

        @pl.when(position // 4 == chunk)
        def _():
            place = position % 4
            chunk_terms[place, 0] = rows_first[...]
            chunk_terms[place, 1] = rows_second[...]
            chunk_embedded[place] = rounded

        return carry

    lax.fori_loop(low, high, block, 0)


def weight_rows(weights, block, first=0, count=8):
    return weights[block * 8 + first : block * 8 + first + count, 0:64, :].reshape(count * 64, D)


def tile_scaling(row_first, column_first, shape, row_is_query, first_len, inverse, keep_low, keep_high):
    rows = row_first + lax.broadcasted_iota(jnp.int32, shape, 0)
    columns = column_first + lax.broadcasted_iota(jnp.int32, shape, 1)
    half = lax.broadcasted_iota(jnp.int32, shape, 1) < BLK
    query, key = (rows, columns) if row_is_query else (columns, rows)
    query_user = (query >= first_len).astype(jnp.int32)
    key_user = (key >= first_len).astype(jnp.int32)
    allowed = jnp.where(half, keep_low, keep_high)
    keep = (key >= query) & (query_user == key_user) & (allowed == 1)
    return jnp.where(keep, jnp.where(query_user == 1, inverse[1], inverse[0]), 0.0)


def fetch(source, target, semaphore):
    copy = pltpu.make_async_copy(source, target, semaphore)
    copy.start()
    return copy


def forward_kernel(
    info,
    inverse,
    mask,
    normed_t,
    weights_far,
    cotangent,
    grads_out,
    gate_out,
    hidden_out,
    keys_head,
    values_head,
    out_t,
    weights,
    keys_t,
    values_t,
    mixed,
    queries,
    semaphores,
):
    me = info[0]
    first_len = info[1]
    chunk = me // 4
    head = me % 4
    copies = [
        fetch(
            weights_far.at[pl.ds(block * 8, 8)],
            weights.at[pl.ds(block * 8, 8)],
            semaphores.at[block],
        )
        for block in (1, 3, 0, 2)
    ]
    copies[0].wait()
    copies[1].wait()

    def kv_tile(position, carry):
        columns = pl.ds(aligned(position, TILE), TILE)
        piece = normed_t[:, columns]
        values_t[:, columns] = silu(mm(weight_rows(weights, 1), piece)).astype(BF16)
        keys_t[:, columns] = silu(mm(weight_rows(weights, 3), piece)).astype(BF16)
        return carry

    kv_high = up_tiles(user_end(chunk * CHUNK + CHUNK - 1, first_len))
    lax.fori_loop(chunk * 2, kv_high, kv_tile, 0)
    head_rows = pl.ds(aligned(head, HD), HD)
    keys_head[...] = keys_t[head_rows, :]
    values_head[...] = values_t[head_rows, :]
    copies[2].wait()
    copies[3].wait()

    for owner in range(NDP):
        out_t[owner * 32 : owner * 32 + 16, :] = weights[owner, 64:80, :E]
        out_t[owner * 32 + 16 : owner * 32 + 32, :] = weights[owner, 64:80, E:]

    own_normed = flip(normed_t[:, pl.ds(aligned(me, BLK), BLK)]).astype(BF16)
    pre_gate = mm_nt(own_normed, weight_rows(weights, 0))
    gate = silu(pre_gate).astype(BF16).astype(F32)
    queries[...] = silu(mm_nt(own_normed, weight_rows(weights, 2))).astype(BF16)
    mixed[...] = jnp.zeros((BLK, E), F32)

    def attend(position, carry):
        columns = pl.ds(aligned(position, TILE), TILE)
        scaling = tile_scaling(
            me * BLK,
            position * TILE,
            (BLK, TILE),
            True,
            first_len,
            inverse,
            mask[me, position * 2],
            mask[me, position * 2 + 1],
        )
        for h in range(H):
            own = slice(h * HD, (h + 1) * HD)
            scores = mm(queries[:, own], keys_t[own, columns]) * SCALE
            attention = (silu(scores) * scaling).astype(BF16)
            mixed[:, own] += mm_nt(attention, values_t[own, columns])
        return carry

    lax.fori_loop(me // 2, up_tiles(user_end(me * BLK + BLK - 1, first_len)), attend, 0)

    hidden_grad = mm(cotangent[...], out_t[...])
    mixed_normed, mixed_scale = normalize(mixed[...], -1)
    mixed_grad = norm_back(hidden_grad * gate, mixed_normed, mixed_scale).astype(BF16)
    for place in range(NBLK):
        h = place % 4
        grads_out[place] = mixed_grad[:, h * HD : (h + 1) * HD]
    hidden_out[...] = (mixed_normed * gate).astype(BF16)
    gate_out[...] = (hidden_grad * mixed_normed * silu_slope(pre_gate)).astype(BF16)


def prepare_kernel(
    info,
    normed_t,
    chunk_embedded,
    weights_far,
    hidden,
    out_t,
    keys_head,
    values_head,
    layer_out,
    queries_head,
    slopes_out,
    own_keys,
    own_values,
    own_queries,
    head_weights,
    semaphores,
):
    me = info[0]
    first_len = info[1]
    chunk = me // 4
    head = me % 4
    copies = [
        fetch(
            weights_far.at[pl.ds(block * 8 + head * 2, 2)],
            head_weights.at[block - 1],
            semaphores.at[block - 1],
        )
        for block in (1, 2, 3)
    ]
    layer_out[...] = (flip(chunk_embedded[head]) + mm_nt(hidden[...], out_t[...])).astype(BF16)
    columns = pl.ds(aligned(chunk, CHUNK), CHUNK)
    own_keys[...] = flip(keys_head[:, columns]).astype(BF16)
    own_values[...] = flip(values_head[:, columns]).astype(BF16)
    for copy in copies:
        copy.wait()

    def rows_of(place):
        return head_weights[place, :, 0:64, :].reshape(HD, D)

    def q_tile(position, carry):
        tile = pl.ds(aligned(position, TILE), TILE)
        queries_head[:, tile] = silu(mm(rows_of(1), normed_t[:, tile])).astype(BF16)
        return carry

    lax.fori_loop(user_start(chunk * CHUNK, first_len) // TILE, chunk * 2 + 2, q_tile, 0)
    own_queries[...] = flip(queries_head[:, columns]).astype(BF16)
    chunk_piece = normed_t[:, columns]
    for place in range(3):
        slopes_out[:, place * HD : (place + 1) * HD] = silu_slope(
            mm(rows_of(place), chunk_piece)
        ).T


def backward_kernel(
    info,
    inverse,
    mask,
    indices,
    keys_head,
    values_head,
    queries_head,
    own_keys,
    own_values,
    own_queries,
    grads,
    slopes,
    gate_grads,
    cotangent,
    chunk_embedded,
    chunk_terms,
    weights_far,
    partial_out,
    sums,
    head_weights,
    gate_weights,
    normed_grad,
    grad_t,
    rows_second,
    terms,
    total,
    semaphores,
):
    me = info[0]
    first_len = info[1]
    chunk = me // 4
    head = me % 4
    copies = [
        fetch(
            weights_far.at[pl.ds(block * 8 + head * 2, 2)],
            head_weights.at[block - 1],
            semaphores.at[block],
        )
        for block in (1, 2, 3)
    ] + [fetch(weights_far.at[pl.ds(0, 8)], gate_weights, semaphores.at[0])]
    for copy in copies:
        copy.wait()
    for part in range(4):
        block = chunk * 4 + part
        rows = slice(part * BLK, (part + 1) * BLK)
        sums[...] = jnp.zeros((BLK, 3 * HD), F32)

        def query_side(position, carry):
            tile = pl.ds(aligned(position, TILE), TILE)
            scaling = tile_scaling(
                block * BLK,
                position * TILE,
                (BLK, TILE),
                True,
                first_len,
                inverse,
                mask[block, position * 2],
                mask[block, position * 2 + 1],
            )
            scores = mm(own_queries[rows, :], keys_head[:, tile]) * SCALE
            pressure = mm(grads[pl.ds(aligned(block, BLK), BLK), :], values_head[:, tile])
            score_grad = (pressure * silu_slope(scores) * scaling).astype(BF16)
            sums[:, HD : 2 * HD] += mm_nt(score_grad, keys_head[:, tile])
            return carry

        lax.fori_loop(
            block // 2, up_tiles(user_end(block * BLK + BLK - 1, first_len)), query_side, 0
        )

        def key_side(position, carry):
            tile = pl.ds(aligned(position, TILE), TILE)
            scaling = tile_scaling(
                block * BLK,
                position * TILE,
                (BLK, TILE),
                False,
                first_len,
                inverse,
                mask[position * 2, block],
                mask[position * 2 + 1, block],
            )
            scores = mm(own_keys[rows, :], queries_head[:, tile]) * SCALE
            sig = sigmoid(scores)
            grad_tile = grads[tile, :]
            attention = (scores * sig * scaling).astype(BF16)
            pressure = mm_nt(own_values[rows, :], grad_tile)
            slope = sig * (1.0 + scores * (1.0 - sig))
            score_grad = (pressure * slope * scaling).astype(BF16)
            sums[:, :HD] += mm(attention, grad_tile)
            sums[:, 2 * HD :] += mm_nt(score_grad, queries_head[:, tile])
            return carry

        lax.fori_loop(
            user_start(block * BLK, first_len) // TILE, block // 2 + 1, key_side, 0
        )
        value_pre = (sums[:, :HD] * slopes[rows, :HD]).astype(BF16)
        other_pre = (sums[:, HD:] * SCALE * slopes[rows, HD:]).astype(BF16)
        pre_grad = jnp.concatenate([value_pre, other_pre], axis=1)
        normed_grad[...] = mm(pre_grad, head_weights[:, :, 0:64, :].reshape(3 * HD, D))

        @pl.when(head == part)
        def _():
            normed_grad[...] += mm(gate_grads[...], gate_weights[:, 0:64, :].reshape(E, D))

        x_normed, x_scale = normalize(chunk_embedded[part].astype(F32), 0)
        upstream = normed_grad[...].T
        grad_t[...] = (
            upstream
            - jnp.mean(upstream, axis=0, keepdims=True)
            - x_normed * jnp.mean(upstream * x_normed, axis=0, keepdims=True)
        ) * x_scale

        @pl.when(head == part)
        def _():
            grad_t[...] += flip(cotangent[...])

        for b in range(DB):
            rows_second[b * R : (b + 1) * R, :] = chunk_terms.at[part, 1][pl.ds(b, R, stride=DB), :]

        def group(step, carry):
            base = aligned(step, WIDE * 32)
            sums = [jnp.zeros((R, BLK), F32) for _ in range(WIDE)]
            for b in range(DB):
                second = rows_second[b * R : (b + 1) * R, :]
                for k in range(WIDE):
                    sums[k] = sums[k] + grad_t[pl.ds(base + (k * DB + b), 1), :] * second
            for k in range(WIDE):
                terms[pl.ds(pl.multiple_of(base + k * R, R), R), :BLK] = sums[k]
            sums = [jnp.zeros((DB, BLK), F32) for _ in range(WIDE)]
            for a in range(DA):
                grad = grad_t[a * DB : (a + 1) * DB, :]
                for k in range(WIDE):
                    first = chunk_terms[part, 0, pl.ds(a * R + step * WIDE + k, 1), :]
                    sums[k] = sums[k] + first * grad
            for k in range(WIDE):
                terms[pl.ds(pl.multiple_of(base + k * DB, DB), DB), BLK:] = sums[k]
            return carry

        lax.fori_loop(0, DA // WIDE, group, 0)
        hot = pair_onehot(indices[block, 0:1, :], indices[block, 1:2, :])
        whole = terms[...]
        upper = whole.astype(BF16)
        lower = (whole - upper.astype(F32)).astype(BF16)
        added = mm_nt(hot, upper) + mm_nt(hot, lower)
        if part == 0:
            total[...] = added
        elif part < 3:
            total[...] += added
        else:
            partial_out[...] = (total[...] + added).astype(BF16)


def params(megabytes):
    return pltpu.CompilerParams(vmem_limit_bytes=megabytes * 1024 * 1024)


def shape(dims, kind):
    return jax.ShapeDtypeStruct(dims, kind)


def cost(flops, moved):
    return pl.CostEstimate(flops=flops, bytes_accessed=moved, transcendentals=0)


def embed_stage(info, indices, table):
    return pl.pallas_call(
        embed_kernel,
        out_shape=(
            shape((D, SEQ), BF16),
            shape((4, 2, D, BLK), F32),
            shape((4, D, BLK), BF16),
        ),
        in_specs=[SMEM_SPEC, VMEM_SPEC, VMEM_SPEC],
        out_specs=(VMEM_SPEC,) * 3,
        scratch_shapes=[
            pltpu.VMEM((D, 2 * ROWS), BF16),
            pltpu.VMEM((D, BLK), F32),
            pltpu.VMEM((D, BLK), F32),
            pltpu.VMEM((D, BLK), F32),
        ],
        compiler_params=params(20),
        cost_estimate=cost(20_000_000_000, 6_000_000),
        name="embed",
    )(info, indices, table)


def forward_stage(info, inverse, mask, normed_t, weights, cotangent):
    return pl.pallas_call(
        forward_kernel,
        out_shape=(
            shape((NBLK, BLK, HD), BF16),
            shape((BLK, E), BF16),
            shape((BLK, E), BF16),
            shape((HD, SEQ), BF16),
            shape((HD, SEQ), BF16),
            shape((D, E), BF16),
        ),
        in_specs=[SMEM_SPEC] * 3 + [VMEM_SPEC, ANY_SPEC, VMEM_SPEC],
        out_specs=(VMEM_SPEC,) * 6,
        scratch_shapes=[
            pltpu.VMEM((NDP, 80, D), BF16),
            pltpu.VMEM((E, SEQ), BF16),
            pltpu.VMEM((E, SEQ), BF16),
            pltpu.VMEM((BLK, E), F32),
            pltpu.VMEM((BLK, E), BF16),
            pltpu.SemaphoreType.DMA((4,)),
        ],
        compiler_params=params(24),
        cost_estimate=cost(8_000_000_000, 12_000_000),
        name="forward",
    )(info, inverse, mask, normed_t, weights, cotangent)


def prepare_stage(info, normed_t, chunk_embedded, weights, hidden, out_t, keys_head, values_head):
    return pl.pallas_call(
        prepare_kernel,
        out_shape=(
            shape((BLK, D), BF16),
            shape((HD, SEQ), BF16),
            shape((CHUNK, 3 * HD), F32),
            shape((CHUNK, HD), BF16),
            shape((CHUNK, HD), BF16),
            shape((CHUNK, HD), BF16),
        ),
        in_specs=[SMEM_SPEC, VMEM_SPEC, VMEM_SPEC, ANY_SPEC] + [VMEM_SPEC] * 4,
        out_specs=(VMEM_SPEC,) * 6,
        scratch_shapes=[
            pltpu.VMEM((3, 2, 80, D), BF16),
            pltpu.SemaphoreType.DMA((3,)),
        ],
        compiler_params=params(20),
        cost_estimate=cost(3_000_000_000, 6_000_000),
        name="prepare",
    )(info, normed_t, chunk_embedded, weights, hidden, out_t, keys_head, values_head)


def backward_stage(info, inverse, mask, *arrays):
    return pl.pallas_call(
        backward_kernel,
        out_shape=shape((2 * ROWS, D), BF16),
        in_specs=[SMEM_SPEC] * 3 + [VMEM_SPEC] * 13 + [ANY_SPEC],
        out_specs=VMEM_SPEC,
        scratch_shapes=[
            pltpu.VMEM((BLK, 3 * HD), F32),
            pltpu.VMEM((3, 2, 80, D), BF16),
            pltpu.VMEM((8, 80, D), BF16),
            pltpu.VMEM((BLK, D), F32),
            pltpu.VMEM((D, BLK), F32),
            pltpu.VMEM((D, BLK), F32),
            pltpu.VMEM((D, 2 * BLK), F32),
            pltpu.VMEM((2 * ROWS, D), F32),
            pltpu.SemaphoreType.DMA((4,)),
        ],
        compiler_params=params(28),
        cost_estimate=cost(10_000_000_000, 12_000_000),
        name="backward",
    )(info, inverse, mask, *arrays)


def pack_weights(w_proj, w_out):
    out_t = w_out.T
    return jnp.concatenate([w_proj.T, jnp.concatenate([out_t[:16], out_t[16:]], axis=1)], axis=0)


def pack_indices(item_first, item_second, block_mask):
    mask_row = jnp.pad(block_mask[0], ((0, 0), (0, BLK - NBLK)))
    return jnp.concatenate(
        [item_first, item_second, mask_row, jnp.zeros((5, BLK), jnp.int32)], axis=0
    )


def exchange(values, axis, groups=None):
    return lax.all_to_all(values, axis, 0, 0, axis_index_groups=groups)


def spread(values, axis, count, groups=None):
    return exchange(jnp.broadcast_to(values[None], (count,) + values.shape), axis, groups)


NEAR = [[4 * c + h for h in range(4)] for c in range(4)]
FAR = [[4 * c + h for c in range(4)] for h in range(4)]


def local(
    item_first, item_second, lengths, block_mask, core_first, core_second, w_proj, w_out, cotangent
):
    me = lax.axis_index("ctx").astype(jnp.int32)
    weights = lax.all_gather(pack_weights(w_proj, w_out), "dp", axis=0, tiled=True)
    weights = weights.reshape(NDP, 80, D)
    table = spread(jnp.concatenate([core_first, core_second], axis=0), "dp", NDP)
    table = table.reshape(2 * ROWS, D)
    own_indices = pack_indices(item_first, item_second, block_mask)
    near_indices = spread(own_indices, "ctx", 4, NEAR)
    indices = spread(near_indices, "ctx", 4, FAR).reshape(NBLK, 8, BLK)
    mask = indices[:, 2, :NBLK]
    info = jnp.stack([me, lengths[0, 0], lengths[0, 1], me])
    inverse = 1.0 / lengths[0].astype(F32)
    upstream = cotangent[0]

    normed_t, chunk_terms, chunk_embedded = embed_stage(info, indices, table)
    grads, gate_grads, hidden, keys_head, values_head, out_t = forward_stage(
        info, inverse, mask, normed_t, weights, upstream
    )
    grads = exchange(grads, "ctx").reshape(SEQ, HD)
    layer_out, queries_head, slopes, own_keys, own_values, own_queries = prepare_stage(
        info, normed_t, chunk_embedded, weights, hidden, out_t, keys_head, values_head
    )
    partial = backward_stage(
        info,
        inverse,
        mask,
        indices,
        keys_head,
        values_head,
        queries_head,
        own_keys,
        own_values,
        own_queries,
        grads,
        slopes,
        gate_grads,
        upstream,
        chunk_embedded,
        chunk_terms,
        weights,
    )
    received = exchange(partial.reshape(NDP, 8, D), "dp")
    pair_sum = jnp.sum(received.astype(F32), axis=0).astype(BF16)
    total = jnp.sum(spread(pair_sum, "ctx", NBLK).astype(F32), axis=0)
    return (layer_out[None], total[:4], total[4:])


def solution(mesh):
    placed = (
        P("dp", "ctx"),
        P("dp", "ctx"),
        P("dp", None),
        P("dp", "ctx", None),
        P("dp", None),
        P("dp", None),
        P(None, "dp"),
        P(None, "dp"),
        P("dp", "ctx", None),
    )
    return jax.shard_map(
        local,
        mesh=mesh,
        in_specs=placed,
        out_specs=(P("dp", "ctx", None), P("dp", None), P("dp", None)),
        check_vma=False,
    )
```

time: 226 us -> 235 us (1.040)
  blocking collectives: 106 us -> 63.8 us
  local copies, waits for them, and re-layouts: 11.1 us -> 33 us
  starting transfers between devices: 25.5 us -> 43.7 us
  Pallas kernels: 24.5 us -> 38.9 us
  waiting for transfers between devices: 39 us -> 35.3 us
    all_to_all x4 -> x3, blocking collectives: 106 us -> 63.8 us  [exchange(): return lax.all_to_all(values, axis, 0, 0, axis_index_groups=groups)]
    unnamed x8 -> x42, local copies, waits for them, and re-layouts: 6.7 us -> 28.7 us
    all_to_all x2 -> x3, starting transfers between devices: 25.4 us -> 43.7 us  [exchange(): return lax.all_to_all(values, axis, 0, 0, axis_index_groups=groups)]
    pallas_call x4, Pallas kernels: 24.5 us -> 38.9 us  [the longest x1 22.3 us: backward_stage(): pl.pallas_call(backward_kernel, out_shape=shape((2 * ROWS, D), BF16), in_...]
    all_gather x1, waiting for transfers between devices: 11.7 us -> 2.31 us  [local(): lax.all_gather(pack_weights(w_proj, w_out), 'dp', axis=0, tiled=True)]
    all_to_all x2 -> x3, waiting for transfers between devices: 27.3 us -> 32.9 us  [exchange(): return lax.all_to_all(values, axis, 0, 0, axis_index_groups=groups)]
  transfers between devices with their start and end apart: 3 -> 4, of which waited for: 3 -> 4; matrix products, arithmetic and copies ran while one was open for 3% -> 3% of each run, Pallas kernels for 4% -> 5%
where the time goes in v2:
time: 235 us; the launch traced here: 234 us
  blocking collectives  63.8 us (27%)
  starting transfers between devices  43.7 us (19%)
  Pallas kernels  38.9 us (17%)
  waiting for transfers between devices  35.3 us (15%)
  local copies, waits for them, and re-layouts  33 us (14%)
  between operations  14.2 us (6%)
  other arithmetic  5.2 us (2%)
    all_to_all x3, blocking collectives, exchange(): return lax.all_to_all(values, axis, 0, 0, axis_index_groups=groups)  63.8 us
    all_to_all x3, starting transfers between devices, exchange(): return lax.all_to_all(values, axis, 0, 0, axis_index_groups=groups)  43.7 us
    all_to_all x3, waiting for transfers between devices, exchange(): return lax.all_to_all(values, axis, 0, 0, axis_index_groups=groups)  32.9 us
    unnamed x42, local copies, waits for them, and re-layouts  28.7 us
    pallas_call x1, Pallas kernels, backward_stage(): pl.pallas_call(backward_kernel, out_shape=shape((2 * ROWS, D), BF16), in_...  22.3 us
    pallas_call x1, Pallas kernels, embed_stage(): pl.pallas_call(embed_kernel, out_shape=(shape((D, SEQ), BF16), shape((4,...  8.59 us
    pallas_call x1, Pallas kernels, forward_stage(): pl.pallas_call(forward_kernel, out_shape=(shape((NBLK, BLK, HD), BF16), s...  4.93 us
  transfers between devices with their start and end apart: 4, of which 4 were waited for; matrix products, arithmetic and copies ran while one was open for 3% of the time, Pallas kernels for 5%

profile of v2, /device:TPU:1, one launch (start us, length us, event | category | flops | bytes accessed | tf_op | source)
XLA Modules:
  0.0 234.0 jit_solution(3061281158856989677)
XLA Ops:
  7.2 0.0 all-gather.2.cloned.1.call-start
  7.2 0.7 fusion.2
  7.9 1.6 maximum_maximum_fusion
  9.5 0.0 all-gather.2.cloned.1.call-update
  9.6 0.1 pad.13.clone
  9.6 0.8 fusion
  10.4 9.7 %all_to_all.30 = s32[4,8,128]{2,1,0:T(8,128)S(1)} all-to-all(s32[4,8,128]{2,1,0:T(8,128)S(1)} %broadcast_in_dim.13), channel_id=1, replica_groups={{0,32,64,96},{128,160,192,224},{256,288,320,352},{384,416,448,480},{1,3..., dimensions={0} | all-to-all | bytes 32768 | tf_op jit(solution)/shard_map/all_to_all | solution.py:588
  20.1 0.6 broadcast_in_dim.14
  20.7 13.2 %all-to-all-start.1 = ((s32[4,4,8,128]{3,2,1,0:T(8,128)}), s32[4,4,8,128]{3,2,1,0:T(8,128)S(1)}, u32[]{:S(2)}, u32[]{:S(2)}) async-start(s32[4,4,8,128]{3,2,1,0:T(8,128)} %broadcast_in_dim.14), calls=%async_computation.1 | async-start | bytes 131072 | tf_op jit(solution)/shard_map/all_to_all | solution.py:588
  33.9 0.7 pad_maximum_fusion
  34.7 11.0 %all-to-all-done.1 = s32[4,4,8,128]{3,2,1,0:T(8,128)S(1)} async-done(((s32[4,4,8,128]{3,2,1,0:T(8,128)}), s32[4,4,8,128]{3,2,1,0:T(8,128)S(1)}, u32[]{:S(2)}, u32[]{:S(2)}) %all-to-all-start.1) | async-done | bytes 65568 | tf_op jit(solution)/shard_map/all_to_all | solution.py:588
  45.7 0.9 broadcast_in_dim.15
  46.5 10.2 %all-to-all-start.2 = ((bf16[32,8,1024]{2,1,0:T(8,128)(2,1)}), bf16[32,8,1024]{2,1,0:T(8,128)(2,1)S(1)}, u32[]{:S(2)}, u32[]{:S(2)}) async-start(bf16[32,8,1024]{2,1,0:T(8,128)(2,1)} %broadcast_in_dim.15), calls=%async_computation.2 | async-start | bytes 1048576 | tf_op jit(solution)/shard_map/all_to_all | solution.py:588
  56.7 1.4 fusion.3
  58.1 1.3 pad_add_fusion.1.info
  59.5 0.7 divide_bitcast_fusion.inverse
  60.1 16.0 %all-to-all-done.2 = bf16[32,8,1024]{2,1,0:T(8,128)(2,1)S(1)} async-done(((bf16[32,8,1024]{2,1,0:T(8,128)(2,1)}), bf16[32,8,1024]{2,1,0:T(8,128)(2,1)S(1)}, u32[]{:S(2)}, u32[]{:S(2)}) %all-to-all-start.2) | async-done | bytes 524320 | tf_op jit(solution)/shard_map/all_to_all | solution.py:588
  76.1 8.6 %embed.1 = (bf16[1024,2048]{1,0:T(8,128)(2,1)S(1)}, f32[4,2,1024,128]{3,2,1,0:T(8,128)S(1)}, bf16[4,1024,128]{2,1,0:T(8,128)(2,1)S(1)}) custom-call(s32[4]{0:T(128)S(1)} %pad_add_fusion.1.info, s32[16,8,128]{2,1,0:T(8,128)S(1)} %bitcast.22, bf16[256,1024]{1,0:T(8,128)(2,1)S(1)} %bitcast.19), custom_call_target="tpu_custom_call" | custom-call | flops 20000000000 | bytes 6000000 | tf_op jit(solution)/shard_map/embed/pallas_call | solution.py:481
  84.7 0.0 copy-start.3
  84.7 2.1 copy-done.3
  86.8 0.0 copy-start.17
  86.8 2.0 copy-done.17
  88.8 2.3 all-gather.2.cloned.1.call-done
  91.1 0.0 copy-start
  91.1 2.5 %copy-done = bf16[2560,1024]{1,0:T(8,128)(2,1)S(1)} copy-done((bf16[2560,1024]{1,0:T(8,128)(2,1)S(1)}, bf16[2560,1024]{1,0:T(8,128)(2,1)}, u32[]{:S(2)}) %copy-start) | copy-done | bytes 5242904
  93.6 0.0 copy-start.4
  93.6 2.2 copy-done.4
  95.8 0.0 copy-start.11
  95.8 0.9 copy-done.11
  96.8 4.9 %forward.1 = (bf16[16,128,128]{2,1,0:T(8,128)(2,1)S(1)}, bf16[128,512]{1,0:T(8,128)(2,1)S(1)}, bf16[128,512]{1,0:T(8,128)(2,1)S(1)}, bf16[128,2048]{1,0:T(8,128)...) custom-call(s32[4]{0:T(128)S(1)} %pad_add_fusion.1.info, f32[2]{0:T(128)S(1)} %divide_bitcast_fusion.inverse, ...), custom_call_target="tpu_custom_call" | custom-call | flops 8000000000 | bytes 12000000 | tf_op jit(solution)/shard_map/forward/pallas_call | solution.py:503
  101.7 0.0 copy-start.6
  101.7 0.8 copy-done.6
  102.5 0.0 copy-start.19
  102.5 20.2 %all-to-all-start.3 = ((bf16[16,128,128]{2,1,0:T(8,128)(2,1)}), bf16[16,128,128]{2,1,0:T(8,128)(2,1)}, u32[]{:S(2)}, u32[]{:S(2)}) async-start(bf16[16,128,128]{2,1,0:T(8,128)(2,1)} %copy-done.6), calls=%async_computation.3 | async-start | bytes 1048576 | tf_op jit(solution)/shard_map/all_to_all | solution.py:588
  122.8 0.0 copy-done.19
  122.8 0.0 copy-start.1
  122.8 2.5 %copy-done.1 = bf16[2560,1024]{1,0:T(8,128)(2,1)S(1)} copy-done((bf16[2560,1024]{1,0:T(8,128)(2,1)S(1)}, bf16[2560,1024]{1,0:T(8,128)(2,1)}, u32[]{:S(2)}) %copy-start.1) | copy-done | bytes 5242904
  125.3 0.0 copy-start.5
  125.3 2.2 copy-done.5
  127.5 3.0 %prepare.1 = (bf16[128,1024]{1,0:T(8,128)(2,1)}, bf16[128,2048]{1,0:T(8,128)(2,1)S(1)}, f32[512,384]{1,0:T(8,128)S(1)}, bf16[512,128]{1,0:T(8,128)(2,1)S(1)}, bf...) custom-call(s32[4]{0:T(128)S(1)} %pad_add_fusion.1.info, bf16[1024,2048]{1,0:T(8,128)(2,1)S(1)} %copy-done.5, ...), custom_call_target="tpu_custom_call" | custom-call | flops 3000000000 | bytes 6000000 | tf_op jit(solution)/shard_map/prepare/pallas_call | solution.py:530
  130.5 0.0 copy-start.7
  130.5 0.9 copy-done.7
  131.3 0.0 copy-start.9
  131.3 0.8 copy-done.9
  132.1 0.0 copy-start.13
  132.1 0.7 copy-done.13
  132.8 0.0 copy-start.15
  132.8 0.6 copy-done.15
  133.4 5.9 %all-to-all-done.3 = bf16[16,128,128]{2,1,0:T(8,128)(2,1)} async-done(((bf16[16,128,128]{2,1,0:T(8,128)(2,1)}), bf16[16,128,128]{2,1,0:T(8,128)(2,1)}, u32[]{:S(2)}, u32[]{:S(2)}) %all-to-all-start.3) | async-done | bytes 524320 | tf_op jit(solution)/shard_map/all_to_all | solution.py:588
  139.4 2.5 %copy-done.2 = bf16[2560,1024]{1,0:T(8,128)(2,1)S(1)} copy-done((bf16[2560,1024]{1,0:T(8,128)(2,1)S(1)}, bf16[2560,1024]{1,0:T(8,128)(2,1)}, u32[]{:S(2)}) %copy-start.2) | copy-done | bytes 5242904
  141.9 0.0 copy-start.8
  141.9 1.1 copy-done.8
  143.0 0.0 copy-start.10
  143.0 1.0 copy-done.10
  144.0 0.9 copy-done.12
  145.0 0.9 copy-done.14
  145.9 0.9 copy-done.16
  146.8 2.2 copy-done.18
  149.0 0.9 copy-done.20
  149.9 22.3 %backward.1 = bf16[256,1024]{1,0:T(8,128)(2,1)S(1)} custom-call(s32[4]{0:T(128)S(1)} %pad_add_fusion.1.info, f32[2]{0:T(128)S(1)} %divide_bitcast_fusion.inverse, s32[16,16]{1,0:T(8,128)S(1)} %bitcast.25, s32[16,8,128]{2,1,0:T(8,128)S(1)} %bitcast.23, bf16[128,2048]{1,0:T(8,128)(2,1)S(1)} %get-tuple-element.22.keys_head, ...), custom_call_target="tpu_custom_call" | custom-call | flops 10000000000 | bytes 12000000 | tf_op jit(solution)/shard_map/backward/pallas_call | solution.py:553
  172.2 34.2 %all_to_all.31 = bf16[32,8,1024]{2,1,0:T(8,128)(2,1)S(1)} all-to-all(bf16[32,8,1024]{2,1,0:T(8,128)(2,1)S(1)} %bitcast.20), channel_id=1, replica_groups=mesh['ctx'=16,'dp'=32] {'dp'}, dimensions={0} | all-to-all | bytes 1048576 | tf_op jit(solution)/shard_map/all_to_all | solution.py:588
  206.4 0.1 reduce_sum.21
  206.5 19.9 %all_to_all.32 = bf16[16,8,1024]{2,1,0:T(8,128)(2,1)S(1)} all-to-all(bf16[16,8,1024]{2,1,0:T(8,128)(2,1)S(1)} %broadcast_in_dim.17), channel_id=1, replica_groups=mesh['ctx'=16,'dp'=32] {'ctx'}, dimensions={0} | all-to-all | bytes 524288 | tf_op jit(solution)/shard_map/all_to_all | solution.py:588
  226.5 0.6 fusion.1
  (11 shorter events, 0.1 us)
Async XLA Ops:
  7.2 84.0 %all-gather.2.cloned.1.call-start = ((), (), s32[]{:S(2)}) async-start(), calls=%async_computation.6 | async-start | bytes 5406720 | tf_op jit(solution)/shard_map/all_gather | solution.py:603
  20.7 25.0 %all-to-all-start.1 = ((s32[4,4,8,128]{3,2,1,0:T(8,128)}), s32[4,4,8,128]{3,2,1,0:T(8,128)S(1)}, u32[]{:S(2)}, u32[]{:S(2)}) async-start(s32[4,4,8,128]{3,2,1,0:T(8,128)} %broadcast_in_dim.14), calls=%async_computation.1 | async-start | bytes 131072 | tf_op jit(solution)/shard_map/all_to_all | solution.py:588
  46.5 29.6 %all-to-all-start.2 = ((bf16[32,8,1024]{2,1,0:T(8,128)(2,1)}), bf16[32,8,1024]{2,1,0:T(8,128)(2,1)S(1)}, u32[]{:S(2)}, u32[]{:S(2)}) async-start(bf16[32,8,1024]{2,1,0:T(8,128)(2,1)} %broadcast_in_dim.15), calls=%async_computation.2 | async-start | bytes 1048576 | tf_op jit(solution)/shard_map/all_to_all | solution.py:588
  84.7 2.1 copy-start.3
  86.8 2.0 copy-start.17
  91.1 2.5 %copy-start = (bf16[2560,1024]{1,0:T(8,128)(2,1)S(1)}, bf16[2560,1024]{1,0:T(8,128)(2,1)}, u32[]{:S(2)}) copy-start(bf16[2560,1024]{1,0:T(8,128)(2,1)} %all-gather.2.cloned.1.call-done) | copy-start | bytes 15728644
  93.6 2.2 copy-start.4
  95.8 0.9 copy-start.11
  101.7 0.8 copy-start.6
  102.5 20.3 %copy-start.19 = (bf16[128,512]{1,0:T(8,128)(2,1)}, bf16[128,512]{1,0:T(8,128)(2,1)S(1)}, u32[]{:S(2)}) copy-start(bf16[128,512]{1,0:T(8,128)(2,1)S(1)} %get-tuple-element.31.gate_grads) | copy-start | bytes 393220
  102.5 36.8 %all-to-all-start.3 = ((bf16[16,128,128]{2,1,0:T(8,128)(2,1)}), bf16[16,128,128]{2,1,0:T(8,128)(2,1)}, u32[]{:S(2)}, u32[]{:S(2)}) async-start(bf16[16,128,128]{2,1,0:T(8,128)(2,1)} %copy-done.6), calls=%async_computation.3 | async-start | bytes 1048576 | tf_op jit(solution)/shard_map/all_to_all | solution.py:588
  122.8 2.5 %copy-start.1 = (bf16[2560,1024]{1,0:T(8,128)(2,1)S(1)}, bf16[2560,1024]{1,0:T(8,128)(2,1)}, u32[]{:S(2)}) copy-start(bf16[2560,1024]{1,0:T(8,128)(2,1)} %all-gather.2.cloned.1.call-done) | copy-start | bytes 15728644
  125.3 2.2 copy-start.5
  130.5 0.9 copy-start.7
  131.3 0.8 copy-start.9
  132.1 0.7 copy-start.13
  132.8 0.6 copy-start.15
  139.4 2.5 %copy-start.2 = (bf16[2560,1024]{1,0:T(8,128)(2,1)S(1)}, bf16[2560,1024]{1,0:T(8,128)(2,1)}, u32[]{:S(2)}) copy-start(bf16[2560,1024]{1,0:T(8,128)(2,1)} %all-gather.2.cloned.1.call-done) | copy-start | bytes 15728644
  141.9 1.1 copy-start.8
  143.0 1.0 copy-start.10
  144.0 0.9 copy-start.12
  145.0 0.9 copy-start.14
  145.9 0.9 copy-start.16
  146.8 2.2 copy-start.18
  149.0 0.9 copy-start.20
Sparse Core Ops, SparseCore 0:
  10.7 80.3 all-gather.1

commit v3 on v1

--- a/solution.py
+++ b/solution.py
@@ -19,6 +19,7 @@
 TILE = 256
 NDP = 32
 CHUNK = 512
+WIDE = 8
 
 EPSILON = 1e-05
 SCALE = HD ** (-0.5)
@@ -28,6 +29,7 @@
 
 SMEM_SPEC = pl.BlockSpec(memory_space=pltpu.SMEM)
 VMEM_SPEC = pl.BlockSpec(memory_space=pltpu.VMEM)
+HBM_SPEC = pl.BlockSpec(memory_space=pltpu.HBM)
 
 
 def mm(left, right):
@@ -96,7 +98,18 @@
 
 
 def embed_kernel(
-    info, indices, table, normed_t, own_terms, own_embedded, table_t, rows_first, rows_second, emb
+    info,
+    indices,
+    table,
+    normed_far,
+    own_terms,
+    own_embedded,
+    table_t,
+    rows_first,
+    rows_second,
+    emb,
+    normed_t,
+    semaphores,
 ):
     me = info[0]
     first_len = info[1]
@@ -108,6 +121,12 @@
             table[:, part * 128 : (part + 1) * 128]
         ).astype(BF16)
 
+    def send(position):
+        columns = pl.ds(aligned(position, BLK), BLK)
+        return pltpu.make_async_copy(
+            normed_t.at[:, columns], normed_far.at[:, columns], semaphores.at[position]
+        )
+
     def block(position, carry):
         hot = pair_onehot(indices[position, 0:1, :], indices[position, 1:2, :])
         picked = mm(table_t[...], hot)
@@ -115,21 +134,22 @@
         rows_second[...] = picked[:, BLK:]
 
         def group(step, inner):
-            base = aligned(step, 128)
-            sums = [jnp.zeros((DB, BLK), F32) for _ in range(4)]
+            base = aligned(step, WIDE * 32)
+            sums = [jnp.zeros((DB, BLK), F32) for _ in range(WIDE)]
             for r in range(R):
                 second = rows_second[r * DB : (r + 1) * DB, :]
-                for k in range(4):
+                for k in range(WIDE):
                     first = rows_first[pl.ds(base + (k * R + r), 1), :]
                     sums[k] = sums[k] + first * second
-            for k in range(4):
+            for k in range(WIDE):
                 emb[pl.ds(pl.multiple_of(base + k * DB, DB), DB), :] = sums[k]
             return inner
 
-        lax.fori_loop(0, 8, group, 0)
+        lax.fori_loop(0, DA // WIDE, group, 0)
         rounded = emb[...].astype(BF16)
         normed, unused = normalize(rounded.astype(F32), 0)
         normed_t[:, pl.ds(aligned(position, BLK), BLK)] = normed.astype(BF16)
+        send(position).start()
 
         @pl.when(position == me)
         def _():
@@ -139,7 +159,12 @@
 
         return carry
 
+    def finish(position, carry):
+        send(position).wait()
+        return carry
+
     lax.fori_loop(low, high, block, 0)
+    lax.fori_loop(low, high, finish, 0)
 
 
 def weight_rows(weights, block, first=0, count=8):
@@ -158,13 +183,27 @@
     return jnp.where(keep, jnp.where(query_user == 1, inverse[1], inverse[0]), 0.0)
 
 
+def fetch(source, target, semaphore):
+    copy = pltpu.make_async_copy(source, target, semaphore)
+    copy.start()
+    return copy
+
+
+def fetch_weights(far, near, semaphores, order):
+    parts = [pl.ds(block * 8, 8) for block in order]
+    return [
+        fetch(far.at[part], near.at[part], semaphores.at[place])
+        for place, part in enumerate(parts)
+    ]
+
+
 def forward_kernel(
     info,
     inverse,
     mask,
-    normed_t,
+    normed_far,
     own_embedded,
-    weights,
+    weights_far,
     cotangent,
     layer_out,
     grads_out,
@@ -178,7 +217,12 @@
     out_t,
     mixed,
     queries,
+    weights,
+    normed_t,
+    semaphores,
+    tile_semaphores,
 ):
+    copies = fetch_weights(weights_far, weights, semaphores, (1, 3, 2, 0))
     me = info[0]
     first_len = info[1]
     chunk = me // 4
@@ -188,8 +232,29 @@
     q_low = user_start(chunk * CHUNK, first_len) // TILE
     q_high = chunk * 2 + 2
 
+
+    def receive(position):
+        columns = pl.ds(aligned(position, TILE), TILE)
+        return pltpu.make_async_copy(
+            normed_far.at[:, columns], normed_t.at[:, columns], tile_semaphores.at[position]
+        )
+
+    def begin(position, carry):
+        receive(position).start()
+        return carry
+
+    def finish(position, carry):
+        receive(position).wait()
+        return carry
+
+    lax.fori_loop(kv_low, kv_high, begin, 0)
+    lax.fori_loop(q_low, kv_low, begin, 0)
+    copies[0].wait()
+    copies[1].wait()
+
     def kv_tile(position, carry):
         columns = pl.ds(aligned(position, TILE), TILE)
+        receive(position).wait()
         piece = normed_t[:, columns]
         values_t[:, columns] = silu(mm(weight_rows(weights, 1), piece)).astype(BF16)
         keys_t[:, columns] = silu(mm(weight_rows(weights, 3), piece)).astype(BF16)
@@ -199,6 +264,10 @@
     head_rows = pl.ds(aligned(head, HD), HD)
     keys_head[...] = keys_t[head_rows, :]
     values_head[...] = values_t[head_rows, :]
+
+    lax.fori_loop(q_low, kv_low, finish, 0)
+    copies[2].wait()
+    copies[3].wait()
 
     def head_weights(block):
         return weights[pl.ds(block * 8 + head * 2, 2), 0:64, :].reshape(HD, D)
@@ -340,7 +409,7 @@
 def core_kernel(
     gate_grads,
     head_grads,
-    weights,
+    weights_far,
     cotangent,
     own_embedded,
     own_terms,
@@ -349,38 +418,44 @@
     rows_second,
     grad_t,
     terms,
+    weights,
+    semaphores,
 ):
+    copies = fetch_weights(weights_far, weights, semaphores, (0, 1, 2, 3))
+    x_normed, x_scale = normalize(flip(own_embedded[...]), -1)
+    copies[0].wait()
     normed_grad = mm(gate_grads[...], weight_rows(weights, 0))
     for place in range(3):
+        copies[place + 1].wait()
         joined = jnp.concatenate(
             [head_grads[h, :, place * HD : (place + 1) * HD] for h in range(H)], axis=1
         )
         normed_grad = normed_grad + mm(joined, weight_rows(weights, place + 1))
-    x_normed, x_scale = normalize(flip(own_embedded[...]), -1)
     input_grad = cotangent[...].astype(F32) + norm_back(normed_grad, x_normed, x_scale)
     grad_t[...] = input_grad.T
     for b in range(DB):
         rows_second[b * R : (b + 1) * R, :] = own_terms.at[1][pl.ds(b, R, stride=DB), :]
 
     def group(step, carry):
-        base = aligned(step, 128)
-        sums = [jnp.zeros((R, BLK), F32) for _ in range(4)]
+        base = aligned(step, WIDE * 32)
+        sums = [jnp.zeros((R, BLK), F32) for _ in range(WIDE)]
         for b in range(DB):
             second = rows_second[b * R : (b + 1) * R, :]
-            for k in range(4):
+            for k in range(WIDE):
                 sums[k] = sums[k] + grad_t[pl.ds(base + (k * DB + b), 1), :] * second
-        for k in range(4):
+        for k in range(WIDE):
             terms[pl.ds(pl.multiple_of(base + k * R, R), R), :BLK] = sums[k]
-        sums = [jnp.zeros((DB, BLK), F32) for _ in range(4)]
+        sums = [jnp.zeros((DB, BLK), F32) for _ in range(WIDE)]
         for a in range(DA):
             grad = grad_t[a * DB : (a + 1) * DB, :]
-            for k in range(4):
-                sums[k] = sums[k] + own_terms[0, pl.ds(a * R + step * 4 + k, 1), :] * grad
-        for k in range(4):
+            for k in range(WIDE):
+                first = own_terms[0, pl.ds(a * R + step * WIDE + k, 1), :]
+                sums[k] = sums[k] + first * grad
+        for k in range(WIDE):
             terms[pl.ds(pl.multiple_of(base + k * DB, DB), DB), BLK:] = sums[k]
         return carry
 
-    lax.fori_loop(0, 8, group, 0)
+    lax.fori_loop(0, DA // WIDE, group, 0)
     hot = pair_onehot(indices[0:1, :], indices[1:2, :])
     whole = terms[...]
     upper = whole.astype(BF16)
@@ -402,14 +477,16 @@
         embed_kernel,
         out_shape=(shape((D, SEQ), BF16), shape((2, D, BLK), F32), shape((D, BLK), BF16)),
         in_specs=[SMEM_SPEC, VMEM_SPEC, VMEM_SPEC],
-        out_specs=(VMEM_SPEC,) * 3,
+        out_specs=(HBM_SPEC, VMEM_SPEC, VMEM_SPEC),
         scratch_shapes=[
             pltpu.VMEM((D, 2 * ROWS), BF16),
             pltpu.VMEM((D, BLK), F32),
             pltpu.VMEM((D, BLK), F32),
             pltpu.VMEM((D, BLK), F32),
+            pltpu.VMEM((D, SEQ), BF16),
+            pltpu.SemaphoreType.DMA((NBLK,)),
         ],
-        compiler_params=params(24),
+        compiler_params=params(57),
         cost_estimate=pl.CostEstimate(flops=20_000_000_000, bytes_accessed=6_000_000, transcendentals=0),
         name="embed",
     )(info, indices, table)
@@ -427,7 +504,7 @@
             shape((HD, SEQ), BF16),
             shape((CHUNK, 3 * HD), F32),
         ),
-        in_specs=[SMEM_SPEC] * 3 + [VMEM_SPEC] * 4,
+        in_specs=[SMEM_SPEC] * 3 + [HBM_SPEC, VMEM_SPEC, HBM_SPEC, VMEM_SPEC],
         out_specs=(VMEM_SPEC,) * 7,
         scratch_shapes=[
             pltpu.VMEM((E, SEQ), BF16),
@@ -435,8 +512,12 @@
             pltpu.VMEM((D, E), BF16),
             pltpu.VMEM((BLK, E), F32),
             pltpu.VMEM((BLK, E), BF16),
+            pltpu.VMEM((NDP, 80, D), BF16),
+            pltpu.VMEM((D, SEQ), BF16),
+            pltpu.SemaphoreType.DMA((4,)),
+            pltpu.SemaphoreType.DMA((8,)),
         ],
-        compiler_params=params(40),
+        compiler_params=params(50),
         cost_estimate=pl.CostEstimate(flops=8_000_000_000, bytes_accessed=12_000_000, transcendentals=0),
         name="forward",
     )(info, inverse, mask, normed_t, own_embedded, weights, cotangent)
@@ -449,7 +530,7 @@
         in_specs=[SMEM_SPEC] * 3 + [VMEM_SPEC] * 5,
         out_specs=VMEM_SPEC,
         scratch_shapes=[pltpu.VMEM((CHUNK, HD), BF16)] * 3 + [pltpu.VMEM((BLK, 3 * HD), F32)],
-        compiler_params=params(24),
+        compiler_params=params(16),
         name="backward",
     )(info, inverse, mask, keys_head, values_head, queries_head, grads, slopes)
 
@@ -458,14 +539,16 @@
     return pl.pallas_call(
         core_kernel,
         out_shape=shape((2 * ROWS, D), BF16),
-        in_specs=[VMEM_SPEC] * 7,
+        in_specs=[VMEM_SPEC, VMEM_SPEC, HBM_SPEC] + [VMEM_SPEC] * 4,
         out_specs=VMEM_SPEC,
         scratch_shapes=[
             pltpu.VMEM((D, BLK), F32),
             pltpu.VMEM((D, BLK), F32),
             pltpu.VMEM((D, 2 * BLK), F32),
+            pltpu.VMEM((NDP, 80, D), BF16),
+            pltpu.SemaphoreType.DMA((4,)),
         ],
-        compiler_params=params(32),
+        compiler_params=params(50),
         name="cores",
     )(gate_grads, head_grads, weights, cotangent, own_embedded, own_terms, indices)
 
@@ -516,8 +599,8 @@
         gate_grads, head_grads, weights, upstream, own_embedded, own_terms, own_indices
     )
     received = lax.all_to_all(partial.reshape(NDP, 8, D), "dp", 0, 0)
-    pair_sum = jnp.sum(received.astype(F32), axis=0)
-    total = jnp.sum(spread(pair_sum, "ctx", NBLK), axis=0)
+    pair_sum = jnp.sum(received.astype(F32), axis=0).astype(BF16)
+    total = jnp.sum(spread(pair_sum, "ctx", NBLK).astype(F32), axis=0)
     return (layer_out[None], total[:4], total[4:])
 
 

time: 226 us -> 218 us (0.965)
  blocking collectives: 106 us -> 96.3 us
  Pallas kernels: 24.5 us -> 31.5 us
  local copies, waits for them, and re-layouts: 11.1 us -> 6.09 us
    all_to_all x1, blocking collectives: 28.4 us -> 18.6 us  [spread(): return lax.all_to_all(copies, axis, 0, 0)]
    unnamed x8 -> x14, local copies, waits for them, and re-layouts: 6.7 us -> 1.77 us
    pallas_call x1, Pallas kernels: 6.58 us -> 9.28 us  [forward_stage(): pl.pallas_call(forward_kernel, out_shape=(shape((BLK, D), BF16), shape((N...]
  transfers between devices with their start and end apart: 3 -> 3, of which waited for: 3 -> 3; matrix products, arithmetic and copies ran while one was open for 3% -> 3% of each run, Pallas kernels for 4% -> 5%
where the time goes in v3:
time: 218 us; the launch traced here: 217 us
  blocking collectives  96.3 us (44%)
  waiting for transfers between devices  37.5 us (17%)
  Pallas kernels  31.5 us (14%)
  starting transfers between devices  25.5 us (12%)
  between operations  14.1 us (6%)
  local copies, waits for them, and re-layouts  6.09 us (3%)
  other arithmetic  5.74 us (3%)
    all_to_all x1, blocking collectives, local(): received = lax.all_to_all(partial.reshape(NDP, 8, D), 'dp', 0, 0)  37.7 us
    all_to_all x1, blocking collectives, local(): grads = lax.all_to_all(grads, 'ctx', 0, 0).reshape(SEQ, HD)  29.4 us
    all_to_all x2, waiting for transfers between devices, spread(): return lax.all_to_all(copies, axis, 0, 0)  26.8 us
    all_to_all x2, starting transfers between devices, spread(): return lax.all_to_all(copies, axis, 0, 0)  25.4 us
    all_to_all x1, blocking collectives, spread(): return lax.all_to_all(copies, axis, 0, 0)  18.6 us
    pallas_call x1, Pallas kernels, embed_stage(): pl.pallas_call(embed_kernel, out_shape=(shape((D, SEQ), BF16), shape((2,...  10.9 us
    all_gather x1, waiting for transfers between devices, local(): lax.all_gather(pack_weights(w_proj, w_out), 'dp', axis=0, tiled=True)  10.8 us
    all_to_all x1, blocking collectives, local(): lax.all_to_all(pre_grads, 'ctx', 0, 0, axis_index_groups=groups)  10.6 us
  transfers between devices with their start and end apart: 3, of which 3 were waited for; matrix products, arithmetic and copies ran while one was open for 3% of the time, Pallas kernels for 5%

profile of v3, /device:TPU:1, one launch (start us, length us, event | category | flops | bytes accessed | tf_op | source)
XLA Modules:
  0.0 216.8 jit_solution(16085705558521854974)
XLA Ops:
  7.2 0.0 all-gather.2.cloned.1.call-start
  7.2 0.7 fusion.2
  7.9 1.6 maximum_maximum_fusion
  9.5 0.0 all-gather.2.cloned.1.call-update
  9.6 0.1 pad.13.clone
  9.6 0.8 fusion.indices
  10.4 0.6 broadcast_in_dim.11
  11.0 16.2 %all-to-all-start = ((s32[16,8,128]{2,1,0:T(8,128)}), s32[16,8,128]{2,1,0:T(8,128)S(1)}, u32[]{:S(2)}, u32[]{:S(2)}) async-start(s32[16,8,128]{2,1,0:T(8,128)} %broadcast_in_dim.11), calls=%async_computation | async-start | bytes 131072 | tf_op jit(solution)/shard_map/all_to_all | solution.py:570
  27.2 0.7 pad_maximum_fusion
  28.0 10.6 %all-to-all-done.indices = s32[16,8,128]{2,1,0:T(8,128)S(1)} async-done(((s32[16,8,128]{2,1,0:T(8,128)}), s32[16,8,128]{2,1,0:T(8,128)S(1)}, u32[]{:S(2)}, u32[]{:S(2)}) %all-to-all-start) | async-done | bytes 65568 | tf_op jit(solution)/shard_map/all_to_all | solution.py:570
  38.6 0.0 copy-start.6
  38.6 0.9 broadcast_in_dim.12
  39.5 9.2 %all-to-all-start.1 = ((bf16[32,8,1024]{2,1,0:T(8,128)(2,1)}), bf16[32,8,1024]{2,1,0:T(8,128)(2,1)S(1)}, u32[]{:S(2)}, u32[]{:S(2)}) async-start(bf16[32,8,1024]{2,1,0:T(8,128)(2,1)} %broadcast_in_dim.12), calls=%async_computation.1 | async-start | bytes 1048576 | tf_op jit(solution)/shard_map/all_to_all | solution.py:570
  48.7 1.3 fusion.3
  50.0 1.9 pad_add_fusion.1.info
  51.9 0.7 divide_bitcast_fusion.inverse
  52.6 16.2 %all-to-all-done.1 = bf16[32,8,1024]{2,1,0:T(8,128)(2,1)S(1)} async-done(((bf16[32,8,1024]{2,1,0:T(8,128)(2,1)}), bf16[32,8,1024]{2,1,0:T(8,128)(2,1)S(1)}, u32[]{:S(2)}, u32[]{:S(2)}) %all-to-all-start.1) | async-done | bytes 524320 | tf_op jit(solution)/shard_map/all_to_all | solution.py:570
  68.8 0.0 copy-start.5
  68.8 0.0 copy-done.6
  68.8 0.8 copy-done.5
  69.6 0.0 copy-start.1
  69.6 0.0 copy-start.4
  69.6 10.9 %embed.1 = (bf16[1024,2048]{1,0:T(8,128)(2,1)}, f32[2,1024,128]{2,1,0:T(8,128)}, bf16[1024,128]{1,0:T(8,128)(2,1)}) custom-call(s32[4]{0:T(128)} %pad_add_fusion.1.info, s32[16,8,128]{2,1,0:T(8,128)} %copy-done.6, bf16[256,1024]{1,0:T(8,128)(2,1)} %bitcast.25), custom_call_target="tpu_custom_call" | custom-call | flops 20000000000 | bytes 6000000 | tf_op jit(solution)/shard_map/embed/pallas_call | solution.py:476
  80.5 10.8 %all-gather.2.cloned.1.call-done = bf16[2560,1024]{1,0:T(8,128)(2,1)} async-done(((bf16[80,1024]{1,0:T(8,128)(2,1)}), bf16[2560,1024]{1,0:T(8,128)(2,1)}) %all-gather.2.cloned.1.call-update) | async-done | bytes 5242896 | tf_op jit(solution)/shard_map/all_gather | solution.py:577
  91.3 0.0 copy-done.1
  91.3 0.0 copy-done.4
  91.3 0.0 copy-start.2
  91.3 0.9 copy-done.2
  92.2 9.3 %forward.1 = (bf16[128,1024]{1,0:T(8,128)(2,1)}, bf16[16,128,128]{2,1,0:T(8,128)(2,1)S(1)}, bf16[128,512]{1,0:T(8,128)(2,1)S(1)}, bf16[128,2048]{1,0:T(8,128)(2,...) custom-call(s32[4]{0:T(128)S(1)} %copy-done.4, ...), custom_call_target="tpu_custom_call" | custom-call | flops 8000000000 | bytes 12000000 | tf_op jit(solution)/shard_map/forward/pallas_call | solution.py:496
  101.5 0.0 copy-start
  101.5 0.0 copy-start.3
  101.5 29.4 %all_to_all.30 = bf16[16,128,128]{2,1,0:T(8,128)(2,1)S(1)} all-to-all(bf16[16,128,128]{2,1,0:T(8,128)(2,1)S(1)} %get-tuple-element.20), channel_id=1, replica_groups=mesh['ctx'=16,'dp'=32] {'ctx'}, dimensions={0} | all-to-all | bytes 1048576 | tf_op jit(solution)/shard_map/all_to_all | solution.py:592
  130.9 4.9 %backward.1 = bf16[4,128,384]{2,1,0:T(8,128)(2,1)S(1)} custom-call(s32[4]{0:T(128)S(1)} %copy-done.4, f32[2]{0:T(128)S(1)} %divide_bitcast_fusion.inverse, s32[16,16]{1,0:T(8,128)S(1)} %bitcast.22, bf16[128,2048]{1,0:T(8,128)(2,1)S(1)} %get-tuple-element.17.keys_head, bf16[128,2048]{1,0:T(8,128)(2,1)S(1)} %get-tuple-element.18.values_head, ...), custom_call_target="tpu_custom_call" | custom-call | tf_op jit(solution)/shard_map/backward/pallas_call | solution.py:527
  135.9 10.6 %all_to_all.31.head_grads = bf16[4,128,384]{2,1,0:T(8,128)(2,1)S(1)} all-to-all(bf16[4,128,384]{2,1,0:T(8,128)(2,1)S(1)} %backward.1), channel_id=1, replica_groups={{0,32,64,96},{128,160,192,224},{256,288,320,352},{384,416,448,480},{1,3..., dimensions={0} | all-to-all | bytes 786432 | tf_op jit(solution)/shard_map/all_to_all | solution.py:597
  146.5 0.0 copy-done
  146.5 0.0 copy-done.3
  146.5 6.3 %cores.1 = bf16[256,1024]{1,0:T(8,128)(2,1)S(1)} custom-call(bf16[128,512]{1,0:T(8,128)(2,1)S(1)} %get-tuple-element.16.gate_grads, bf16[4,128,384]{2,1,0:T(8,128)(2,1)S(1)} %all_to_all.31.head_grads, bf16[32,80,1024]{2,1,0:T(8,128)(2,1)} %bitcast.24, bf16[128,1024]{1,0:T(8,128)(2,1)S(1)} %bitcast.20, bf16[1024,128]{1,0:T(8,128)(2,1)S(1)} %copy-done.3, ...), custom_call_target="tpu_custom_call" | custom-call | tf_op jit(solution)/shard_map/cores/pallas_call | solution.py:539
  152.8 37.7 %all_to_all.32 = bf16[32,8,1024]{2,1,0:T(8,128)(2,1)S(1)} all-to-all(bf16[32,8,1024]{2,1,0:T(8,128)(2,1)S(1)} %bitcast.17), channel_id=1, replica_groups=mesh['ctx'=16,'dp'=32] {'dp'}, dimensions={0} | all-to-all | bytes 1048576 | tf_op jit(solution)/shard_map/all_to_all | solution.py:601
  190.5 0.1 reduce_sum.21
  190.6 18.6 %all_to_all.33 = bf16[16,8,1024]{2,1,0:T(8,128)(2,1)S(1)} all-to-all(bf16[16,8,1024]{2,1,0:T(8,128)(2,1)S(1)} %broadcast_in_dim.28), channel_id=1, replica_groups=mesh['ctx'=16,'dp'=32] {'ctx'}, dimensions={0} | all-to-all | bytes 524288 | tf_op jit(solution)/shard_map/all_to_all | solution.py:570
  209.3 0.6 fusion.1
  (4 shorter events, 0.1 us)
Async XLA Ops:
  7.2 84.1 %all-gather.2.cloned.1.call-start = ((), (), s32[]{:S(2)}) async-start(), calls=%async_computation.6 | async-start | bytes 5406720 | tf_op jit(solution)/shard_map/all_gather | solution.py:577
  11.0 27.5 %all-to-all-start = ((s32[16,8,128]{2,1,0:T(8,128)}), s32[16,8,128]{2,1,0:T(8,128)S(1)}, u32[]{:S(2)}, u32[]{:S(2)}) async-start(s32[16,8,128]{2,1,0:T(8,128)} %broadcast_in_dim.11), calls=%async_computation | async-start | bytes 131072 | tf_op jit(solution)/shard_map/all_to_all | solution.py:570
  38.6 30.2 %copy-start.6 = (s32[16,8,128]{2,1,0:T(8,128)}, s32[16,8,128]{2,1,0:T(8,128)S(1)}, u32[]{:S(2)}) copy-start(s32[16,8,128]{2,1,0:T(8,128)S(1)} %all-to-all-done.indices) | copy-start | bytes 196612
  39.5 29.3 %all-to-all-start.1 = ((bf16[32,8,1024]{2,1,0:T(8,128)(2,1)}), bf16[32,8,1024]{2,1,0:T(8,128)(2,1)S(1)}, u32[]{:S(2)}, u32[]{:S(2)}) async-start(bf16[32,8,1024]{2,1,0:T(8,128)(2,1)} %broadcast_in_dim.12), calls=%async_computation.1 | async-start | bytes 1048576 | tf_op jit(solution)/shard_map/all_to_all | solution.py:570
  68.8 0.8 copy-start.5
  69.6 21.7 %copy-start.1 = (bf16[1,128,1024]{2,1,0:T(8,128)(2,1)S(1)}, bf16[1,128,1024]{2,1,0:T(8,128)(2,1)}, u32[]{:S(2)}) copy-start(bf16[1,128,1024]{2,1,0:T(8,128)(2,1)} %param.17) | copy-start | bytes 786436
  69.6 21.7 %copy-start.4 = (s32[4]{0:T(128)S(1)}, s32[4]{0:T(128)}, u32[]{:S(2)}) copy-start(s32[4]{0:T(128)} %pad_add_fusion.1.info) | copy-start | bytes 52
  91.3 1.0 copy-start.2
  101.5 45.0 %copy-start = (f32[2,1024,128]{2,1,0:T(8,128)S(1)}, f32[2,1024,128]{2,1,0:T(8,128)}, u32[]{:S(2)}) copy-start(f32[2,1024,128]{2,1,0:T(8,128)} %get-tuple-element.22.own_terms) | copy-start | bytes 3145732
  101.5 44.9 %copy-start.3 = (bf16[1024,128]{1,0:T(8,128)(2,1)S(1)}, bf16[1024,128]{1,0:T(8,128)(2,1)}, u32[]{:S(2)}) copy-start(bf16[1024,128]{1,0:T(8,128)(2,1)} %get-tuple-element.14.own_embedded) | copy-start | bytes 786436
Sparse Core Ops, SparseCore 0:
  10.7 80.5 all-gather.1

commit v4 on v3

--- a/solution.py
+++ b/solution.py
@@ -20,6 +20,9 @@
 NDP = 32
 CHUNK = 512
 WIDE = 8
+FORWARD_MB = 56
+PREPARE_MB = 60
+CORES_MB = 20
 
 EPSILON = 1e-05
 SCALE = HD ** (-0.5)
@@ -95,6 +98,43 @@
 
 def up_tiles(pos):
     return (pos + (TILE - 1)) // TILE
+
+
+def block_range(chunk, first_len):
+    low = (user_start(chunk * CHUNK, first_len) // TILE) * 2
+    high = up_tiles(user_end(chunk * CHUNK + CHUNK - 1, first_len)) * 2
+    return low, jnp.maximum(low, high - 12), high
+
+
+def turn_table(table, table_t):
+    for part in range(8):
+        table_t[part * 128 : (part + 1) * 128, :] = flip(
+            table[:, part * 128 : (part + 1) * 128]
+        ).astype(BF16)
+
+
+def embed_block(indices, position, table_t, rows_first, rows_second, emb):
+    hot = pair_onehot(indices[position, 0:1, :], indices[position, 1:2, :])
+    picked = mm(table_t[...], hot)
+    rows_first[...] = picked[:, :BLK]
+    rows_second[...] = picked[:, BLK:]
+
+    def group(step, inner):
+        base = aligned(step, WIDE * 32)
+        sums = [jnp.zeros((DB, BLK), F32) for _ in range(WIDE)]
+        for r in range(R):
+            second = rows_second[r * DB : (r + 1) * DB, :]
+            for k in range(WIDE):
+                first = rows_first[pl.ds(base + (k * R + r), 1), :]
+                sums[k] = sums[k] + first * second
+        for k in range(WIDE):
+            emb[pl.ds(pl.multiple_of(base + k * DB, DB), DB), :] = sums[k]
+        return inner
+
+    lax.fori_loop(0, DA // WIDE, group, 0)
+    rounded = emb[...].astype(BF16)
+    normed, unused = normalize(rounded.astype(F32), 0)
+    return rounded, normed.astype(BF16)
 
 
 def embed_kernel(
@@ -112,14 +152,8 @@
     semaphores,
 ):
     me = info[0]
-    first_len = info[1]
-    chunk = me // 4
-    low = (user_start(chunk * CHUNK, first_len) // TILE) * 2
-    high = up_tiles(user_end(chunk * CHUNK + CHUNK - 1, first_len)) * 2
-    for part in range(8):
-        table_t[part * 128 : (part + 1) * 128, :] = flip(
-            table[:, part * 128 : (part + 1) * 128]
-        ).astype(BF16)
+    unused, middle, high = block_range(me // 4, info[1])
+    turn_table(table, table_t)
 
     def send(position):
         columns = pl.ds(aligned(position, BLK), BLK)
@@ -128,27 +162,8 @@
         )
 
     def block(position, carry):
-        hot = pair_onehot(indices[position, 0:1, :], indices[position, 1:2, :])
-        picked = mm(table_t[...], hot)
-        rows_first[...] = picked[:, :BLK]
-        rows_second[...] = picked[:, BLK:]
-
-        def group(step, inner):
-            base = aligned(step, WIDE * 32)
-            sums = [jnp.zeros((DB, BLK), F32) for _ in range(WIDE)]
-            for r in range(R):
-                second = rows_second[r * DB : (r + 1) * DB, :]
-                for k in range(WIDE):
-                    first = rows_first[pl.ds(base + (k * R + r), 1), :]
-                    sums[k] = sums[k] + first * second
-            for k in range(WIDE):
-                emb[pl.ds(pl.multiple_of(base + k * DB, DB), DB), :] = sums[k]
-            return inner
-
-        lax.fori_loop(0, DA // WIDE, group, 0)
-        rounded = emb[...].astype(BF16)
-        normed, unused = normalize(rounded.astype(F32), 0)
-        normed_t[:, pl.ds(aligned(position, BLK), BLK)] = normed.astype(BF16)
+        rounded, normed = embed_block(indices, position, table_t, rows_first, rows_second, emb)
+        normed_t[:, pl.ds(aligned(position, BLK), BLK)] = normed
         send(position).start()
 
         @pl.when(position == me)
@@ -163,8 +178,8 @@
         send(position).wait()
         return carry
 
-    lax.fori_loop(low, high, block, 0)
-    lax.fori_loop(low, high, finish, 0)
+    lax.fori_loop(middle, high, block, 0)
+    lax.fori_loop(middle, high, finish, 0)
 
 
 def weight_rows(weights, block, first=0, count=8):
@@ -197,24 +212,26 @@
     ]
 
 
+def tile_copy(far, near, semaphores, position):
+    columns = pl.ds(aligned(position, TILE), TILE)
+    return pltpu.make_async_copy(far.at[:, columns], near.at[:, columns], semaphores.at[position])
+
+
 def forward_kernel(
     info,
     inverse,
     mask,
     normed_far,
-    own_embedded,
     weights_far,
     cotangent,
-    layer_out,
     grads_out,
     gate_out,
+    hidden_out,
     keys_head,
     values_head,
-    queries_head,
-    slopes_out,
+    out_t,
     keys_t,
     values_t,
-    out_t,
     mixed,
     queries,
     weights,
@@ -229,32 +246,18 @@
     head = me % 4
     kv_low = chunk * 2
     kv_high = up_tiles(user_end(chunk * CHUNK + CHUNK - 1, first_len))
-    q_low = user_start(chunk * CHUNK, first_len) // TILE
-    q_high = chunk * 2 + 2
-
-
-    def receive(position):
-        columns = pl.ds(aligned(position, TILE), TILE)
-        return pltpu.make_async_copy(
-            normed_far.at[:, columns], normed_t.at[:, columns], tile_semaphores.at[position]
-        )
 
     def begin(position, carry):
-        receive(position).start()
-        return carry
-
-    def finish(position, carry):
-        receive(position).wait()
+        tile_copy(normed_far, normed_t, tile_semaphores, position).start()
         return carry
 
     lax.fori_loop(kv_low, kv_high, begin, 0)
-    lax.fori_loop(q_low, kv_low, begin, 0)
     copies[0].wait()
     copies[1].wait()
 
     def kv_tile(position, carry):
         columns = pl.ds(aligned(position, TILE), TILE)
-        receive(position).wait()
+        tile_copy(normed_far, normed_t, tile_semaphores, position).wait()
         piece = normed_t[:, columns]
         values_t[:, columns] = silu(mm(weight_rows(weights, 1), piece)).astype(BF16)
         keys_t[:, columns] = silu(mm(weight_rows(weights, 3), piece)).astype(BF16)
@@ -264,26 +267,8 @@
     head_rows = pl.ds(aligned(head, HD), HD)
     keys_head[...] = keys_t[head_rows, :]
     values_head[...] = values_t[head_rows, :]
-
-    lax.fori_loop(q_low, kv_low, finish, 0)
     copies[2].wait()
     copies[3].wait()
-
-    def head_weights(block):
-        return weights[pl.ds(block * 8 + head * 2, 2), 0:64, :].reshape(HD, D)
-
-    def q_tile(position, carry):
-        columns = pl.ds(aligned(position, TILE), TILE)
-        queries_head[:, columns] = silu(mm(head_weights(2), normed_t[:, columns])).astype(BF16)
-        return carry
-
-    lax.fori_loop(q_low, q_high, q_tile, 0)
-
-    chunk_piece = normed_t[:, pl.ds(aligned(chunk, CHUNK), CHUNK)]
-    for place in range(3):
-        slopes_out[:, place * HD : (place + 1) * HD] = silu_slope(
-            mm(head_weights(place + 1), chunk_piece)
-        ).T
 
     for owner in range(NDP):
         out_t[owner * 32 : owner * 32 + 16, :] = weights[owner, 64:80, :E]
@@ -316,15 +301,90 @@
 
     lax.fori_loop(me // 2, up_tiles(user_end(me * BLK + BLK - 1, first_len)), attend, 0)
 
+    hidden_grad = mm(cotangent[...], out_t[...])
     mixed_normed, mixed_scale = normalize(mixed[...], -1)
-    hidden = (mixed_normed * gate).astype(BF16)
-    layer_out[...] = (flip(own_embedded[...]) + mm_nt(hidden, out_t[...])).astype(BF16)
-    hidden_grad = mm(cotangent[...], out_t[...])
-    gate_out[...] = (hidden_grad * mixed_normed * silu_slope(pre_gate)).astype(BF16)
     mixed_grad = norm_back(hidden_grad * gate, mixed_normed, mixed_scale).astype(BF16)
     for place in range(NBLK):
         h = place % 4
         grads_out[place] = mixed_grad[:, h * HD : (h + 1) * HD]
+    hidden_out[...] = (mixed_normed * gate).astype(BF16)
+    gate_out[...] = (hidden_grad * mixed_normed * silu_slope(pre_gate)).astype(BF16)
+
+
+def prepare_kernel(
+    info,
+    indices,
+    table,
+    normed_far,
+    own_embedded,
+    weights_far,
+    hidden,
+    out_t,
+    layer_out,
+    queries_head,
+    slopes_out,
+    table_t,
+    rows_first,
+    rows_second,
+    emb,
+    normed_t,
+    head_weights,
+    semaphores,
+    tile_semaphores,
+):
+    me = info[0]
+    first_len = info[1]
+    chunk = me // 4
+    head = me % 4
+    copies = [
+        fetch(
+            weights_far.at[pl.ds(block * 8 + head * 2, 2)],
+            head_weights.at[block - 1],
+            semaphores.at[block - 1],
+        )
+        for block in (1, 2, 3)
+    ]
+    low, middle, unused = block_range(chunk, first_len)
+    q_low = low // 2
+    q_middle = jnp.minimum(middle, chunk * 4) // 2
+    q_high = chunk * 2 + 2
+
+    def begin(position, carry):
+        tile_copy(normed_far, normed_t, tile_semaphores, position).start()
+        return carry
+
+    def finish(position, carry):
+        tile_copy(normed_far, normed_t, tile_semaphores, position).wait()
+        return carry
+
+    lax.fori_loop(q_middle, q_high, begin, 0)
+    turn_table(table, table_t)
+
+    def late_block(position, carry):
+        unused, normed = embed_block(indices, position, table_t, rows_first, rows_second, emb)
+        normed_t[:, pl.ds(aligned(position, BLK), BLK)] = normed
+        return carry
+
+    lax.fori_loop(low, q_middle * 2, late_block, 0)
+    layer_out[...] = (flip(own_embedded[...]) + mm_nt(hidden[...], out_t[...])).astype(BF16)
+    for copy in copies:
+        copy.wait()
+    lax.fori_loop(q_middle, q_high, finish, 0)
+
+    def rows_of(place):
+        return head_weights[place, :, 0:64, :].reshape(HD, D)
+
+    def q_tile(position, carry):
+        tile = pl.ds(aligned(position, TILE), TILE)
+        queries_head[:, tile] = silu(mm(rows_of(1), normed_t[:, tile])).astype(BF16)
+        return carry
+
+    lax.fori_loop(q_low, q_high, q_tile, 0)
+    chunk_piece = normed_t[:, pl.ds(aligned(chunk, CHUNK), CHUNK)]
+    for place in range(3):
+        slopes_out[:, place * HD : (place + 1) * HD] = silu_slope(
+            mm(rows_of(place), chunk_piece)
+        ).T
 
 
 def backward_kernel(
@@ -336,12 +396,16 @@
     queries_head,
     grads,
     slopes,
+    weights_far,
     pre_grads,
+    weights,
     own_keys,
     own_values,
     own_queries,
     sums,
+    semaphores,
 ):
+    copies = fetch_weights(weights_far, weights, semaphores, (0, 1, 2, 3))
     me = info[0]
     first_len = info[1]
     chunk = me // 4
@@ -404,12 +468,14 @@
         )
         pre_grads[part, :, :HD] = (sums[:, :HD] * slopes[rows, :HD]).astype(BF16)
         pre_grads[part, :, HD:] = (sums[:, HD:] * SCALE * slopes[rows, HD:]).astype(BF16)
+    for copy in copies:
+        copy.wait()
 
 
 def core_kernel(
     gate_grads,
     head_grads,
-    weights_far,
+    weights,
     cotangent,
     own_embedded,
     own_terms,
@@ -418,15 +484,10 @@
     rows_second,
     grad_t,
     terms,
-    weights,
-    semaphores,
 ):
-    copies = fetch_weights(weights_far, weights, semaphores, (0, 1, 2, 3))
     x_normed, x_scale = normalize(flip(own_embedded[...]), -1)
-    copies[0].wait()
     normed_grad = mm(gate_grads[...], weight_rows(weights, 0))
     for place in range(3):
-        copies[place + 1].wait()
         joined = jnp.concatenate(
             [head_grads[h, :, place * HD : (place + 1) * HD] for h in range(H)], axis=1
         )
@@ -492,24 +553,26 @@
     )(info, indices, table)
 
 
-def forward_stage(info, inverse, mask, normed_t, own_embedded, weights, cotangent):
+def cost(flops, moved):
+    return pl.CostEstimate(flops=flops, bytes_accessed=moved, transcendentals=0)
+
+
+def forward_stage(info, inverse, mask, normed_t, weights, cotangent):
     return pl.pallas_call(
         forward_kernel,
         out_shape=(
-            shape((BLK, D), BF16),
             shape((NBLK, BLK, HD), BF16),
+            shape((BLK, E), BF16),
             shape((BLK, E), BF16),
             shape((HD, SEQ), BF16),
             shape((HD, SEQ), BF16),
-            shape((HD, SEQ), BF16),
-            shape((CHUNK, 3 * HD), F32),
+            shape((D, E), BF16),
         ),
-        in_specs=[SMEM_SPEC] * 3 + [HBM_SPEC, VMEM_SPEC, HBM_SPEC, VMEM_SPEC],
-        out_specs=(VMEM_SPEC,) * 7,
+        in_specs=[SMEM_SPEC] * 3 + [HBM_SPEC, HBM_SPEC, VMEM_SPEC],
+        out_specs=(VMEM_SPEC,) * 6,
         scratch_shapes=[
             pltpu.VMEM((E, SEQ), BF16),
             pltpu.VMEM((E, SEQ), BF16),
-            pltpu.VMEM((D, E), BF16),
             pltpu.VMEM((BLK, E), F32),
             pltpu.VMEM((BLK, E), BF16),
             pltpu.VMEM((NDP, 80, D), BF16),
@@ -517,38 +580,74 @@
             pltpu.SemaphoreType.DMA((4,)),
             pltpu.SemaphoreType.DMA((8,)),
         ],
-        compiler_params=params(50),
-        cost_estimate=pl.CostEstimate(flops=8_000_000_000, bytes_accessed=12_000_000, transcendentals=0),
+        compiler_params=params(FORWARD_MB),
+        cost_estimate=cost(8_000_000_000, 12_000_000),
         name="forward",
-    )(info, inverse, mask, normed_t, own_embedded, weights, cotangent)
-
-
-def backward_stage(info, inverse, mask, keys_head, values_head, queries_head, grads, slopes):
+    )(info, inverse, mask, normed_t, weights, cotangent)
+
+
+def prepare_stage(info, indices, table, normed_t, own_embedded, weights, hidden, out_t):
+    return pl.pallas_call(
+        prepare_kernel,
+        out_shape=(
+            shape((BLK, D), BF16),
+            shape((HD, SEQ), BF16),
+            shape((CHUNK, 3 * HD), F32),
+        ),
+        in_specs=[
+            SMEM_SPEC,
+            VMEM_SPEC,
+            VMEM_SPEC,
+            HBM_SPEC,
+            VMEM_SPEC,
+            HBM_SPEC,
+            VMEM_SPEC,
+            VMEM_SPEC,
+        ],
+        out_specs=(VMEM_SPEC,) * 3,
+        scratch_shapes=[
+            pltpu.VMEM((D, 2 * ROWS), BF16),
+            pltpu.VMEM((D, BLK), F32),
+            pltpu.VMEM((D, BLK), F32),
+            pltpu.VMEM((D, BLK), F32),
+            pltpu.VMEM((D, SEQ), BF16),
+            pltpu.VMEM((3, 2, 80, D), BF16),
+            pltpu.SemaphoreType.DMA((3,)),
+            pltpu.SemaphoreType.DMA((8,)),
+        ],
+        compiler_params=params(PREPARE_MB),
+        cost_estimate=cost(5_000_000_000, 6_000_000),
+        name="prepare",
+    )(info, indices, table, normed_t, own_embedded, weights, hidden, out_t)
+
+
+def backward_stage(
+    info, inverse, mask, keys_head, values_head, queries_head, grads, slopes, weights
+):
     return pl.pallas_call(
         backward_kernel,
-        out_shape=shape((4, BLK, 3 * HD), BF16),
-        in_specs=[SMEM_SPEC] * 3 + [VMEM_SPEC] * 5,
-        out_specs=VMEM_SPEC,
-        scratch_shapes=[pltpu.VMEM((CHUNK, HD), BF16)] * 3 + [pltpu.VMEM((BLK, 3 * HD), F32)],
-        compiler_params=params(16),
+        out_shape=(shape((4, BLK, 3 * HD), BF16), shape((NDP, 80, D), BF16)),
+        in_specs=[SMEM_SPEC] * 3 + [VMEM_SPEC] * 5 + [HBM_SPEC],
+        out_specs=(VMEM_SPEC, VMEM_SPEC),
+        scratch_shapes=[pltpu.VMEM((CHUNK, HD), BF16)] * 3
+        + [pltpu.VMEM((BLK, 3 * HD), F32), pltpu.SemaphoreType.DMA((4,))],
+        compiler_params=params(43),
         name="backward",
-    )(info, inverse, mask, keys_head, values_head, queries_head, grads, slopes)
+    )(info, inverse, mask, keys_head, values_head, queries_head, grads, slopes, weights)
 
 
 def core_stage(gate_grads, head_grads, weights, cotangent, own_embedded, own_terms, indices):
     return pl.pallas_call(
         core_kernel,
         out_shape=shape((2 * ROWS, D), BF16),
-        in_specs=[VMEM_SPEC, VMEM_SPEC, HBM_SPEC] + [VMEM_SPEC] * 4,
+        in_specs=[VMEM_SPEC] * 7,
         out_specs=VMEM_SPEC,
         scratch_shapes=[
             pltpu.VMEM((D, BLK), F32),
             pltpu.VMEM((D, BLK), F32),
             pltpu.VMEM((D, 2 * BLK), F32),
-            pltpu.VMEM((NDP, 80, D), BF16),
-            pltpu.SemaphoreType.DMA((4,)),
         ],
-        compiler_params=params(50),
+        compiler_params=params(CORES_MB),
         name="cores",
     )(gate_grads, head_grads, weights, cotangent, own_embedded, own_terms, indices)
 
@@ -586,17 +685,20 @@
     upstream = cotangent[0]
 
     normed_t, own_terms, own_embedded = embed_stage(info, indices, table)
-    layer_out, grads, gate_grads, keys_head, values_head, queries_head, slopes = forward_stage(
-        info, inverse, mask, normed_t, own_embedded, weights, upstream
+    grads, gate_grads, hidden, keys_head, values_head, out_t = forward_stage(
+        info, inverse, mask, normed_t, weights, upstream
     )
     grads = lax.all_to_all(grads, "ctx", 0, 0).reshape(SEQ, HD)
-    pre_grads = backward_stage(
-        info, inverse, mask, keys_head, values_head, queries_head, grads, slopes
+    layer_out, queries_head, slopes = prepare_stage(
+        info, indices, table, normed_t, own_embedded, weights, hidden, out_t
+    )
+    pre_grads, weights_near = backward_stage(
+        info, inverse, mask, keys_head, values_head, queries_head, grads, slopes, weights
     )
     groups = [[4 * c + h for h in range(4)] for c in range(4)]
     head_grads = lax.all_to_all(pre_grads, "ctx", 0, 0, axis_index_groups=groups)
     partial = core_stage(
-        gate_grads, head_grads, weights, upstream, own_embedded, own_terms, own_indices
+        gate_grads, head_grads, weights_near, upstream, own_embedded, own_terms, own_indices
     )
     received = lax.all_to_all(partial.reshape(NDP, 8, D), "dp", 0, 0)
     pair_sum = jnp.sum(received.astype(F32), axis=0).astype(BF16)

time: 218 us -> 211 us (0.968)
  blocking collectives: 96.3 us -> 62.5 us
  starting transfers between devices: 25.5 us -> 36.9 us
  waiting for transfers between devices: 37.5 us -> 48.2 us
  Pallas kernels: 31.5 us -> 34.2 us
    all_to_all x1 -> x0, blocking collectives: 29.4 us -> none  [local(): grads = lax.all_to_all(grads, 'ctx', 0, 0).reshape(SEQ, HD)]
    all_to_all x0 -> x1, starting transfers between devices: none -> 11.5 us  [local(): grads = lax.all_to_all(grads, 'ctx', 0, 0).reshape(SEQ, HD)]
    all_to_all x0 -> x1, waiting for transfers between devices: none -> 11.4 us  [local(): grads = lax.all_to_all(grads, 'ctx', 0, 0).reshape(SEQ, HD)]
    all_to_all x1, blocking collectives: 37.7 us -> 32.3 us  [local(): received = lax.all_to_all(partial.reshape(NDP, 8, D), 'dp', 0, 0)]
    pallas_call x2 -> x3, Pallas kernels: 14.2 us -> 19.1 us  [the longest x1 8.67 us: forward_stage(): pl.pallas_call(forward_kernel, out_shape=(shape((NBLK, BLK, HD), BF16), s...]
  transfers between devices with their start and end apart: 3 -> 4, of which waited for: 3 -> 4; matrix products, arithmetic and copies ran while one was open for 3% -> 4% of each run, Pallas kernels for 5% -> 8%
where the time goes in v4:
time: 211 us; the launch traced here: 210 us
  blocking collectives  62.5 us (30%)
  waiting for transfers between devices  48.2 us (23%)
  starting transfers between devices  36.9 us (17%)
  Pallas kernels  34.2 us (16%)
  between operations  14.2 us (7%)
  local copies, waits for them, and re-layouts  7.88 us (4%)
  other arithmetic  6.17 us (3%)
    all_to_all x1, blocking collectives, local(): received = lax.all_to_all(partial.reshape(NDP, 8, D), 'dp', 0, 0)  32.3 us
    all_to_all x2, waiting for transfers between devices, spread(): return lax.all_to_all(copies, axis, 0, 0)  25.8 us
    all_to_all x2, starting transfers between devices, spread(): return lax.all_to_all(copies, axis, 0, 0)  25.4 us
    all_to_all x1, blocking collectives, spread(): return lax.all_to_all(copies, axis, 0, 0)  19.4 us
    all_to_all x1, starting transfers between devices, local(): grads = lax.all_to_all(grads, 'ctx', 0, 0).reshape(SEQ, HD)  11.5 us
    all_to_all x1, waiting for transfers between devices, local(): grads = lax.all_to_all(grads, 'ctx', 0, 0).reshape(SEQ, HD)  11.4 us
    all_gather x1, waiting for transfers between devices, local(): lax.all_gather(pack_weights(w_proj, w_out), 'dp', axis=0, tiled=True)  11 us
    pallas_call x1, Pallas kernels, embed_stage(): pl.pallas_call(embed_kernel, out_shape=(shape((D, SEQ), BF16), shape((2,...  10.9 us
  transfers between devices with their start and end apart: 4, of which 4 were waited for; matrix products, arithmetic and copies ran while one was open for 4% of the time, Pallas kernels for 8%

profile of v4, /device:TPU:1, one launch (start us, length us, event | category | flops | bytes accessed | tf_op | source)
XLA Modules:
  0.0 210.2 jit_solution(6351329839335188819)
XLA Ops:
  7.2 0.0 all-gather.2.cloned.1.call-start
  7.2 0.7 fusion.2
  7.9 1.6 maximum_maximum_fusion
  9.5 0.0 all-gather.2.cloned.1.call-update
  9.6 0.1 pad.13.clone
  9.6 0.8 fusion.indices
  10.4 0.6 broadcast_in_dim.11
  11.0 16.2 %all-to-all-start = ((s32[16,8,128]{2,1,0:T(8,128)}), s32[16,8,128]{2,1,0:T(8,128)S(1)}, u32[]{:S(2)}, u32[]{:S(2)}) async-start(s32[16,8,128]{2,1,0:T(8,128)} %broadcast_in_dim.11), calls=%async_computation | async-start | bytes 131072 | tf_op jit(solution)/shard_map/all_to_all | solution.py:669
  27.2 0.7 pad_maximum_fusion
  28.0 10.6 %all-to-all-done.indices = s32[16,8,128]{2,1,0:T(8,128)S(1)} async-done(((s32[16,8,128]{2,1,0:T(8,128)}), s32[16,8,128]{2,1,0:T(8,128)S(1)}, u32[]{:S(2)}, u32[]{:S(2)}) %all-to-all-start) | async-done | bytes 65568 | tf_op jit(solution)/shard_map/all_to_all | solution.py:669
  38.6 0.0 copy-start.12
  38.6 0.9 broadcast_in_dim.12
  39.4 9.2 %all-to-all-start.1 = ((bf16[32,8,1024]{2,1,0:T(8,128)(2,1)}), bf16[32,8,1024]{2,1,0:T(8,128)(2,1)S(1)}, u32[]{:S(2)}, u32[]{:S(2)}) async-start(bf16[32,8,1024]{2,1,0:T(8,128)(2,1)} %broadcast_in_dim.12), calls=%async_computation.1 | async-start | bytes 1048576 | tf_op jit(solution)/shard_map/all_to_all | solution.py:669
  48.7 1.3 fusion.3
  50.0 1.8 pad_add_fusion.1.info
  51.8 1.2 divide_bitcast_fusion.inverse
  52.9 0.6 slice.30
  53.6 15.2 %all-to-all-done.1 = bf16[32,8,1024]{2,1,0:T(8,128)(2,1)S(1)} async-done(((bf16[32,8,1024]{2,1,0:T(8,128)(2,1)}), bf16[32,8,1024]{2,1,0:T(8,128)(2,1)S(1)}, u32[]{:S(2)}, u32[]{:S(2)}) %all-to-all-start.1) | async-done | bytes 524320 | tf_op jit(solution)/shard_map/all_to_all | solution.py:669
  68.8 0.0 copy-start.11
  68.8 0.0 copy-done.12
  68.8 0.8 copy-done.11
  69.6 10.9 %embed.1 = (bf16[1024,2048]{1,0:T(8,128)(2,1)}, f32[2,1024,128]{2,1,0:T(8,128)}, bf16[1024,128]{1,0:T(8,128)(2,1)}) custom-call(s32[4]{0:T(128)} %pad_add_fusion.1.info, s32[16,8,128]{2,1,0:T(8,128)} %copy-done.12, bf16[256,1024]{1,0:T(8,128)(2,1)} %bitcast.26), custom_call_target="tpu_custom_call" | custom-call | flops 20000000000 | bytes 6000000 | tf_op jit(solution)/shard_map/embed/pallas_call | solution.py:537
  80.5 11.0 %all-gather.2.cloned.1.call-done = bf16[2560,1024]{1,0:T(8,128)(2,1)} async-done(((bf16[80,1024]{1,0:T(8,128)(2,1)}), bf16[2560,1024]{1,0:T(8,128)(2,1)}) %all-gather.2.cloned.1.call-update) | async-done | bytes 5242896 | tf_op jit(solution)/shard_map/all_gather | solution.py:676
  91.5 8.7 %forward.1 = (bf16[16,128,128]{2,1,0:T(8,128)(2,1)}, bf16[128,512]{1,0:T(8,128)(2,1)}, bf16[128,512]{1,0:T(8,128)(2,1)}, bf16[128,2048]{1,0:T(8,128)(2,1)}, bf16...) custom-call(s32[4]{0:T(128)} %pad_add_fusion.1.info, f32[2]{0:T(128)} %divide_bitcast_fusion.inverse, s32[16,16]{1,0:T(8,128)} %bitcast.21, ...), custom_call_target="tpu_custom_call" | custom-call | flops 8000000000 | bytes 12000000 | tf_op jit(solution)/shard_map/forward/pallas_call | solution.py:561
  100.2 11.5 %all-to-all-start.2 = ((bf16[16,128,128]{2,1,0:T(8,128)(2,1)}), bf16[16,128,128]{2,1,0:T(8,128)(2,1)S(1)}, u32[]{:S(2)}, u32[]{:S(2)}) async-start(bf16[16,128,128]{2,1,0:T(8,128)(2,1)} %get-tuple-element.26), calls=%async_computation.2 | async-start | bytes 1048576 | tf_op jit(solution)/shard_map/all_to_all | solution.py:691
  111.6 0.0 copy-start.2
  111.6 0.0 copy-start.3
  111.6 0.0 copy-start.8
  111.7 0.0 copy-start.9
  111.7 0.0 copy-start.10
  111.7 0.0 copy-start.5
  111.7 0.0 copy-start.6
  111.7 0.0 copy-start.7
  111.7 5.4 %prepare.1 = (bf16[128,1024]{1,0:T(8,128)(2,1)}, bf16[128,2048]{1,0:T(8,128)(2,1)}, f32[512,384]{1,0:T(8,128)}) custom-call(s32[4]{0:T(128)} %pad_add_fusion.1.info, s32[16,8,128]{2,1,0:T(8,128)} %copy-done.12, bf16[256,1024]{1,0:T(8,128)(2,1)} %bitcast.27, bf16[1024,2048]{1,0:T(8,128)(2,1)} %get-tuple-element.17.normed_far, ...), custom_call_target="tpu_custom_call" | custom-call | flops 5000000000 | bytes 6000000 | tf_op jit(solution)/shard_map/prepare/pallas_call | solution.py:590
  117.1 0.0 copy-start
  117.2 11.4 %all-to-all-done.2 = bf16[16,128,128]{2,1,0:T(8,128)(2,1)S(1)} async-done(((bf16[16,128,128]{2,1,0:T(8,128)(2,1)}), bf16[16,128,128]{2,1,0:T(8,128)(2,1)S(1)}, u32[]{:S(2)}, u32[]{:S(2)}) %all-to-all-start.2) | async-done | bytes 524320 | tf_op jit(solution)/shard_map/all_to_all | solution.py:691
  128.6 0.0 copy-done.2
  128.6 0.0 copy-done.3
  128.6 0.0 copy-done.8
  128.6 0.0 copy-done.9
  128.6 0.0 copy-done.10
  128.6 0.0 copy-start.1
  128.6 1.1 copy-done.1
  129.8 0.0 copy-start.4
  129.8 1.0 copy-done.4
  130.8 5.0 %backward.1 = (bf16[4,128,384]{2,1,0:T(8,128)(2,1)S(1)}, bf16[32,80,1024]{2,1,0:T(8,128)(2,1)S(1)}) custom-call(s32[4]{0:T(128)S(1)} %copy-done.9, f32[2]{0:T(128)S(1)} %copy-done.10, s32[16,16]{1,0:T(8,128)S(1)} %bitcast.22, bf16[128,2048]{1,0:T(8,128)(2,1)S(1)} %copy-done.2, bf16[128,2048]{1,0:T(8,128)(2,1)S(1)} %copy-done.3, ...), custom_call_target="tpu_custom_call" | custom-call | tf_op jit(solution)/shard_map/backward/pallas_call | solution.py:627
  135.8 10.9 %all_to_all.30.head_grads = bf16[4,128,384]{2,1,0:T(8,128)(2,1)S(1)} all-to-all(bf16[4,128,384]{2,1,0:T(8,128)(2,1)S(1)} %get-tuple-element.28), channel_id=1, replica_groups={{0,32,64,96},{128,160,192,224},{256,288,320,352},{384,416,448,480},{1,3..., dimensions={0} | all-to-all | bytes 786432 | tf_op jit(solution)/shard_map/all_to_all | solution.py:699
  146.7 0.0 copy-done.5
  146.7 0.0 copy-done.6
  146.7 0.0 copy-done.7
  146.7 0.0 copy-done
  146.7 4.2 %cores.1 = bf16[256,1024]{1,0:T(8,128)(2,1)S(1)} custom-call(bf16[128,512]{1,0:T(8,128)(2,1)S(1)} %copy-done.7, bf16[4,128,384]{2,1,0:T(8,128)(2,1)S(1)} %all_to_all.30.head_grads, bf16[32,80,1024]{2,1,0:T(8,128)(2,1)S(1)} %get-tuple-element.29.weights, bf16[128,1024]{1,0:T(8,128)(2,1)S(1)} %bitcast.20, bf16[1024,128]{1,0:T(8,128)(2,1)S(1)} %copy-done.6, ...), custom_call_target="tpu_custom_call" | custom-call | tf_op jit(solution)/shard_map/cores/pallas_call | solution.py:640
  150.9 32.3 %all_to_all.31 = bf16[32,8,1024]{2,1,0:T(8,128)(2,1)S(1)} all-to-all(bf16[32,8,1024]{2,1,0:T(8,128)(2,1)S(1)} %bitcast.18), channel_id=1, replica_groups=mesh['ctx'=16,'dp'=32] {'dp'}, dimensions={0} | all-to-all | bytes 1048576 | tf_op jit(solution)/shard_map/all_to_all | solution.py:703
  183.2 0.1 reduce_sum.21
  183.3 19.4 %all_to_all.32 = bf16[16,8,1024]{2,1,0:T(8,128)(2,1)S(1)} all-to-all(bf16[16,8,1024]{2,1,0:T(8,128)(2,1)S(1)} %broadcast_in_dim.28), channel_id=1, replica_groups=mesh['ctx'=16,'dp'=32] {'ctx'}, dimensions={0} | all-to-all | bytes 524288 | tf_op jit(solution)/shard_map/all_to_all | solution.py:669
  202.7 0.6 fusion.1
  (3 shorter events, 0.1 us)
Async XLA Ops:
  7.2 84.3 %all-gather.2.cloned.1.call-start = ((), (), s32[]{:S(2)}) async-start(), calls=%async_computation.6 | async-start | bytes 5406720 | tf_op jit(solution)/shard_map/all_gather | solution.py:676
  11.0 27.5 %all-to-all-start = ((s32[16,8,128]{2,1,0:T(8,128)}), s32[16,8,128]{2,1,0:T(8,128)S(1)}, u32[]{:S(2)}, u32[]{:S(2)}) async-start(s32[16,8,128]{2,1,0:T(8,128)} %broadcast_in_dim.11), calls=%async_computation | async-start | bytes 131072 | tf_op jit(solution)/shard_map/all_to_all | solution.py:669
  38.6 30.2 %copy-start.12 = (s32[16,8,128]{2,1,0:T(8,128)}, s32[16,8,128]{2,1,0:T(8,128)S(1)}, u32[]{:S(2)}) copy-start(s32[16,8,128]{2,1,0:T(8,128)S(1)} %all-to-all-done.indices) | copy-start | bytes 196612
  39.4 29.3 %all-to-all-start.1 = ((bf16[32,8,1024]{2,1,0:T(8,128)(2,1)}), bf16[32,8,1024]{2,1,0:T(8,128)(2,1)S(1)}, u32[]{:S(2)}, u32[]{:S(2)}) async-start(bf16[32,8,1024]{2,1,0:T(8,128)(2,1)} %broadcast_in_dim.12), calls=%async_computation.1 | async-start | bytes 1048576 | tf_op jit(solution)/shard_map/all_to_all | solution.py:669
  68.8 0.8 copy-start.11
  100.2 28.4 %all-to-all-start.2 = ((bf16[16,128,128]{2,1,0:T(8,128)(2,1)}), bf16[16,128,128]{2,1,0:T(8,128)(2,1)S(1)}, u32[]{:S(2)}, u32[]{:S(2)}) async-start(bf16[16,128,128]{2,1,0:T(8,128)(2,1)} %get-tuple-element.26), calls=%async_computation.2 | async-start | bytes 1048576 | tf_op jit(solution)/shard_map/all_to_all | solution.py:691
  111.6 17.0 %copy-start.2 = (bf16[128,2048]{1,0:T(8,128)(2,1)S(1)}, bf16[128,2048]{1,0:T(8,128)(2,1)}, u32[]{:S(2)}) copy-start(bf16[128,2048]{1,0:T(8,128)(2,1)} %get-tuple-element.23.keys_head) | copy-start | bytes 1572868
  111.6 17.0 %copy-start.3 = (bf16[128,2048]{1,0:T(8,128)(2,1)S(1)}, bf16[128,2048]{1,0:T(8,128)(2,1)}, u32[]{:S(2)}) copy-start(bf16[128,2048]{1,0:T(8,128)(2,1)} %get-tuple-element.24.values_head) | copy-start | bytes 1572868
  111.6 17.0 %copy-start.8 = (s32[16,1,16]{2,1,0:T(1,128)S(1)}, s32[16,1,16]{2,1,0:T(1,128)}, u32[]{:S(2)}) copy-start(s32[16,1,16]{2,1,0:T(1,128)} %slice.30) | copy-start | bytes 3076
  111.7 17.0 %copy-start.9 = (s32[4]{0:T(128)S(1)}, s32[4]{0:T(128)}, u32[]{:S(2)}) copy-start(s32[4]{0:T(128)} %pad_add_fusion.1.info) | copy-start | bytes 52
  111.7 17.0 %copy-start.10 = (f32[2]{0:T(128)S(1)}, f32[2]{0:T(128)}, u32[]{:S(2)}) copy-start(f32[2]{0:T(128)} %divide_bitcast_fusion.inverse) | copy-start | bytes 28
  111.7 35.0 %copy-start.5 = (bf16[1,128,1024]{2,1,0:T(8,128)(2,1)S(1)}, bf16[1,128,1024]{2,1,0:T(8,128)(2,1)}, u32[]{:S(2)}) copy-start(bf16[1,128,1024]{2,1,0:T(8,128)(2,1)} %param.17) | copy-start | bytes 786436
  111.7 35.0 %copy-start.6 = (bf16[1024,128]{1,0:T(8,128)(2,1)S(1)}, bf16[1024,128]{1,0:T(8,128)(2,1)}, u32[]{:S(2)}) copy-start(bf16[1024,128]{1,0:T(8,128)(2,1)} %get-tuple-element.18.own_embedded) | copy-start | bytes 786436
  111.7 35.0 %copy-start.7 = (bf16[128,512]{1,0:T(8,128)(2,1)S(1)}, bf16[128,512]{1,0:T(8,128)(2,1)}, u32[]{:S(2)}) copy-start(bf16[128,512]{1,0:T(8,128)(2,1)} %get-tuple-element.22.gate_grads) | copy-start | bytes 393220
  117.1 29.6 %copy-start = (f32[2,1024,128]{2,1,0:T(8,128)S(1)}, f32[2,1024,128]{2,1,0:T(8,128)}, u32[]{:S(2)}) copy-start(f32[2,1024,128]{2,1,0:T(8,128)} %get-tuple-element.30.own_terms) | copy-start | bytes 3145732
  128.6 1.1 copy-start.1
  129.8 1.0 copy-start.4
Sparse Core Ops, SparseCore 0:
  10.7 80.7 all-gather.1

commit v5 on v4

--- a/solution.py
+++ b/solution.py
@@ -21,7 +21,7 @@
 CHUNK = 512
 WIDE = 8
 FORWARD_MB = 56
-PREPARE_MB = 60
+PREPARE_MB = 50
 CORES_MB = 20
 
 EPSILON = 1e-05
@@ -194,6 +194,29 @@
     query_user = (query >= first_len).astype(jnp.int32)
     key_user = (key >= first_len).astype(jnp.int32)
     allowed = jnp.where(half, keep_low, keep_high)
+    keep = (key >= query) & (query_user == key_user) & (allowed == 1)
+    return jnp.where(keep, jnp.where(query_user == 1, inverse[1], inverse[0]), 0.0)
+
+
+def square_scaling(mask, row_tile, column_tile, first_len, inverse, row_is_query):
+    dims = (TILE, TILE)
+    rows = row_tile * TILE + lax.broadcasted_iota(jnp.int32, dims, 0)
+    columns = column_tile * TILE + lax.broadcasted_iota(jnp.int32, dims, 1)
+    row_half = lax.broadcasted_iota(jnp.int32, dims, 0) < BLK
+    column_half = lax.broadcasted_iota(jnp.int32, dims, 1) < BLK
+
+    def flag(row, column):
+        row, column = row_tile * 2 + row, column_tile * 2 + column
+        return mask[row, column] if row_is_query else mask[column, row]
+
+    allowed = jnp.where(
+        row_half,
+        jnp.where(column_half, flag(0, 0), flag(0, 1)),
+        jnp.where(column_half, flag(1, 0), flag(1, 1)),
+    )
+    query, key = (rows, columns) if row_is_query else (columns, rows)
+    query_user = (query >= first_len).astype(jnp.int32)
+    key_user = (key >= first_len).astype(jnp.int32)
     keep = (key >= query) & (query_user == key_user) & (allowed == 1)
     return jnp.where(keep, jnp.where(query_user == 1, inverse[1], inverse[0]), 0.0)
 
@@ -413,45 +436,27 @@
     own_keys[...] = flip(keys_head[:, columns]).astype(BF16)
     own_values[...] = flip(values_head[:, columns]).astype(BF16)
     own_queries[...] = flip(queries_head[:, columns]).astype(BF16)
-    for part in range(4):
-        block = chunk * 4 + part
-        rows = slice(part * BLK, (part + 1) * BLK)
-        sums[...] = jnp.zeros((BLK, 3 * HD), F32)
+    for part in range(2):
+        place = chunk * 2 + part
+        rows = slice(part * TILE, (part + 1) * TILE)
+        sums[...] = jnp.zeros((TILE, 3 * HD), F32)
 
         def query_side(position, carry):
             tile = pl.ds(aligned(position, TILE), TILE)
-            scaling = tile_scaling(
-                block * BLK,
-                position * TILE,
-                (BLK, TILE),
-                True,
-                first_len,
-                inverse,
-                mask[block, position * 2],
-                mask[block, position * 2 + 1],
-            )
+            scaling = square_scaling(mask, place, position, first_len, inverse, True)
             scores = mm(own_queries[rows, :], keys_head[:, tile]) * SCALE
-            pressure = mm(grads[pl.ds(aligned(block, BLK), BLK), :], values_head[:, tile])
+            pressure = mm(grads[pl.ds(aligned(place, TILE), TILE), :], values_head[:, tile])
             score_grad = (pressure * silu_slope(scores) * scaling).astype(BF16)
             sums[:, HD : 2 * HD] += mm_nt(score_grad, keys_head[:, tile])
             return carry
 
         lax.fori_loop(
-            block // 2, up_tiles(user_end(block * BLK + BLK - 1, first_len)), query_side, 0
+            place, up_tiles(user_end(place * TILE + TILE - 1, first_len)), query_side, 0
         )
 
         def key_side(position, carry):
             tile = pl.ds(aligned(position, TILE), TILE)
-            scaling = tile_scaling(
-                block * BLK,
-                position * TILE,
-                (BLK, TILE),
-                False,
-                first_len,
-                inverse,
-                mask[position * 2, block],
-                mask[position * 2 + 1, block],
-            )
+            scaling = square_scaling(mask, place, position, first_len, inverse, False)
             scores = mm(own_keys[rows, :], queries_head[:, tile]) * SCALE
             sig = sigmoid(scores)
             grad_tile = grads[tile, :]
@@ -463,11 +468,13 @@
             sums[:, 2 * HD :] += mm_nt(score_grad, queries_head[:, tile])
             return carry
 
-        lax.fori_loop(
-            user_start(block * BLK, first_len) // TILE, block // 2 + 1, key_side, 0
-        )
-        pre_grads[part, :, :HD] = (sums[:, :HD] * slopes[rows, :HD]).astype(BF16)
-        pre_grads[part, :, HD:] = (sums[:, HD:] * SCALE * slopes[rows, HD:]).astype(BF16)
+        lax.fori_loop(user_start(place * TILE, first_len) // TILE, place + 1, key_side, 0)
+        for half in range(2):
+            near = slice(half * BLK, (half + 1) * BLK)
+            far = slice(part * TILE + half * BLK, part * TILE + (half + 1) * BLK)
+            block = part * 2 + half
+            pre_grads[block, :, :HD] = (sums[near, :HD] * slopes[far, :HD]).astype(BF16)
+            pre_grads[block, :, HD:] = (sums[near, HD:] * SCALE * slopes[far, HD:]).astype(BF16)
     for copy in copies:
         copy.wait()
 
@@ -630,7 +637,7 @@
         in_specs=[SMEM_SPEC] * 3 + [VMEM_SPEC] * 5 + [HBM_SPEC],
         out_specs=(VMEM_SPEC, VMEM_SPEC),
         scratch_shapes=[pltpu.VMEM((CHUNK, HD), BF16)] * 3
-        + [pltpu.VMEM((BLK, 3 * HD), F32), pltpu.SemaphoreType.DMA((4,))],
+        + [pltpu.VMEM((TILE, 3 * HD), F32), pltpu.SemaphoreType.DMA((4,))],
         compiler_params=params(43),
         name="backward",
     )(info, inverse, mask, keys_head, values_head, queries_head, grads, slopes, weights)
@@ -652,9 +659,21 @@
     )(gate_grads, head_grads, weights, cotangent, own_embedded, own_terms, indices)
 
 
+def pack_kernel(proj_t, out_t, packed):
+    packed[:64, :] = proj_t[...]
+    packed[64:, :E] = out_t[:16, :]
+    packed[64:, E:] = out_t[16:, :]
+
+
 def pack_weights(w_proj, w_out):
-    out_t = w_out.T
-    return jnp.concatenate([w_proj.T, jnp.concatenate([out_t[:16], out_t[16:]], axis=1)], axis=0)
+    return pl.pallas_call(
+        pack_kernel,
+        out_shape=shape((80, D), BF16),
+        in_specs=[VMEM_SPEC] * 2,
+        out_specs=VMEM_SPEC,
+        compiler_params=params(60),
+        name="pack",
+    )(w_proj.T, w_out.T)
 
 
 def pack_indices(item_first, item_second, block_mask):

time: 211 us -> 207 us (0.981)
  local copies, waits for them, and re-layouts: 7.88 us -> 11.4 us
  waiting for transfers between devices: 48.2 us -> 45.9 us
    unnamed x26 -> x36, local copies, waits for them, and re-layouts: 3.04 us -> 7.24 us
    all_to_all x1, waiting for transfers between devices: 11.4 us -> 8.39 us  [local(): grads = lax.all_to_all(grads, 'ctx', 0, 0).reshape(SEQ, HD)]
    all_to_all x1, blocking collectives: 32.3 us -> 30.1 us  [local(): received = lax.all_to_all(partial.reshape(NDP, 8, D), 'dp', 0, 0)]
  transfers between devices with their start and end apart: 4 -> 4, of which waited for: 4 -> 4; matrix products, arithmetic and copies ran while one was open for 4% -> 4% of each run, Pallas kernels for 8% -> 7%
where the time goes in v5:
time: 207 us; the launch traced here: 206 us
  blocking collectives  61.2 us (30%)
  waiting for transfers between devices  45.9 us (22%)
  starting transfers between devices  36.5 us (18%)
  Pallas kernels  32.5 us (16%)
  between operations  14.2 us (7%)
  local copies, waits for them, and re-layouts  11.4 us (6%)
  other arithmetic  4.68 us (2%)
    all_to_all x1, blocking collectives, local(): received = lax.all_to_all(partial.reshape(NDP, 8, D), 'dp', 0, 0)  30.1 us
    all_to_all x2, starting transfers between devices, spread(): return lax.all_to_all(copies, axis, 0, 0)  25.4 us
    all_to_all x2, waiting for transfers between devices, spread(): return lax.all_to_all(copies, axis, 0, 0)  24.7 us
    all_to_all x1, blocking collectives, spread(): return lax.all_to_all(copies, axis, 0, 0)  19.9 us
    all_gather x1, waiting for transfers between devices, local(): lax.all_gather(pack_weights(w_proj, w_out), 'dp', axis=0, tiled=True)  12.7 us
    all_to_all x1, blocking collectives, local(): lax.all_to_all(pre_grads, 'ctx', 0, 0, axis_index_groups=groups)  11.2 us
    all_to_all x1, starting transfers between devices, local(): grads = lax.all_to_all(grads, 'ctx', 0, 0).reshape(SEQ, HD)  11.1 us
    pallas_call x1, Pallas kernels, embed_stage(): pl.pallas_call(embed_kernel, out_shape=(shape((D, SEQ), BF16), shape((2,...  10.9 us
  transfers between devices with their start and end apart: 4, of which 4 were waited for; matrix products, arithmetic and copies ran while one was open for 4% of the time, Pallas kernels for 7%

profile of v5, /device:TPU:1, one launch (start us, length us, event | category | flops | bytes accessed | tf_op | source)
XLA Modules:
  0.0 206.4 jit_solution(2364265676524001621)
XLA Ops:
  7.2 0.0 all-gather.2.cloned.1.call-start
  7.2 1.6 pack.1
  8.8 0.0 all-gather.2.cloned.1.call-update
  8.8 0.1 pad.10.clone
  8.9 0.8 fusion.indices
  9.7 0.6 broadcast_in_dim.11
  10.3 16.2 %all-to-all-start = ((s32[16,8,128]{2,1,0:T(8,128)}), s32[16,8,128]{2,1,0:T(8,128)S(1)}, u32[]{:S(2)}, u32[]{:S(2)}) async-start(s32[16,8,128]{2,1,0:T(8,128)} %broadcast_in_dim.11), calls=%async_computation | async-start | bytes 131072 | tf_op jit(solution)/shard_map/all_to_all | solution.py:688
  26.5 0.7 pad_maximum_fusion
  27.2 10.6 %all-to-all-done.indices = s32[16,8,128]{2,1,0:T(8,128)S(1)} async-done(((s32[16,8,128]{2,1,0:T(8,128)}), s32[16,8,128]{2,1,0:T(8,128)S(1)}, u32[]{:S(2)}, u32[]{:S(2)}) %all-to-all-start) | async-done | bytes 65568 | tf_op jit(solution)/shard_map/all_to_all | solution.py:688
  37.9 0.0 copy-start.11
  37.9 0.9 broadcast_in_dim.12
  38.7 9.2 %all-to-all-start.1 = ((bf16[32,8,1024]{2,1,0:T(8,128)(2,1)}), bf16[32,8,1024]{2,1,0:T(8,128)(2,1)S(1)}, u32[]{:S(2)}, u32[]{:S(2)}) async-start(bf16[32,8,1024]{2,1,0:T(8,128)(2,1)} %broadcast_in_dim.12), calls=%async_computation.1 | async-start | bytes 1048576 | tf_op jit(solution)/shard_map/all_to_all | solution.py:688
  47.9 1.3 fusion.2
  49.3 1.9 pad_add_fusion.1.info
  51.2 1.2 divide_bitcast_fusion.inverse
  52.3 0.6 slice.20
  52.9 14.1 %all-to-all-done.1 = bf16[32,8,1024]{2,1,0:T(8,128)(2,1)S(1)} async-done(((bf16[32,8,1024]{2,1,0:T(8,128)(2,1)}), bf16[32,8,1024]{2,1,0:T(8,128)(2,1)S(1)}, u32[]{:S(2)}, u32[]{:S(2)}) %all-to-all-start.1) | async-done | bytes 524320 | tf_op jit(solution)/shard_map/all_to_all | solution.py:688
  67.1 0.0 copy-start.5
  67.1 0.0 copy-done.11
  67.1 0.8 copy-done.5
  67.9 10.9 %embed.1 = (bf16[1024,2048]{1,0:T(8,128)(2,1)}, f32[2,1024,128]{2,1,0:T(8,128)}, bf16[1024,128]{1,0:T(8,128)(2,1)}) custom-call(s32[4]{0:T(128)} %pad_add_fusion.1.info, s32[16,8,128]{2,1,0:T(8,128)} %copy-done.11, bf16[256,1024]{1,0:T(8,128)(2,1)} %bitcast.19), custom_call_target="tpu_custom_call" | custom-call | flops 20000000000 | bytes 6000000 | tf_op jit(solution)/shard_map/embed/pallas_call | solution.py:544
  78.7 12.7 %all-gather.2.cloned.1.call-done = bf16[2560,1024]{1,0:T(8,128)(2,1)} async-done(((bf16[80,1024]{1,0:T(8,128)(2,1)}), bf16[2560,1024]{1,0:T(8,128)(2,1)}) %all-gather.2.cloned.1.call-update) | async-done | bytes 5242896 | tf_op jit(solution)/shard_map/all_gather | solution.py:695
  91.5 0.0 copy-start.6
  91.5 0.0 copy-start.14
  91.5 8.7 %forward.1 = (bf16[16,128,128]{2,1,0:T(8,128)(2,1)}, bf16[128,512]{1,0:T(8,128)(2,1)}, bf16[128,512]{1,0:T(8,128)(2,1)}, bf16[128,2048]{1,0:T(8,128)(2,1)}, bf16...) custom-call(s32[4]{0:T(128)} %pad_add_fusion.1.info, f32[2]{0:T(128)} %divide_bitcast_fusion.inverse, s32[16,16]{1,0:T(8,128)} %bitcast.23, ...), custom_call_target="tpu_custom_call" | custom-call | flops 8000000000 | bytes 12000000 | tf_op jit(solution)/shard_map/forward/pallas_call | solution.py:568
  100.2 11.1 %all-to-all-start.2 = ((bf16[16,128,128]{2,1,0:T(8,128)(2,1)}), bf16[16,128,128]{2,1,0:T(8,128)(2,1)S(1)}, u32[]{:S(2)}, u32[]{:S(2)}) async-start(bf16[16,128,128]{2,1,0:T(8,128)(2,1)} %get-tuple-element.26), calls=%async_computation.2 | async-start | bytes 1048576 | tf_op jit(solution)/shard_map/all_to_all | solution.py:710
  111.3 0.0 copy-done.6
  111.3 0.0 copy-done.14
  111.3 0.0 copy-start.8
  111.3 0.9 copy-done.8
  112.3 0.0 copy-start.12
  112.3 0.8 copy-done.12
  113.1 0.0 copy-start.16
  113.1 1.2 copy-done.16
  114.3 0.0 copy-start.17
  114.3 0.9 copy-done.17
  115.2 0.0 copy-start.1
  115.2 0.0 copy-start.2
  115.2 0.0 copy-start.13
  115.2 0.0 copy-start.10
  115.2 3.6 %prepare.1 = (bf16[128,1024]{1,0:T(8,128)(2,1)}, bf16[128,2048]{1,0:T(8,128)(2,1)S(1)}, f32[512,384]{1,0:T(8,128)S(1)}) custom-call(s32[4]{0:T(128)S(1)} %copy-done.14, s32[16,8,128]{2,1,0:T(8,128)S(1)} %copy-done.12, bf16[256,1024]{1,0:T(8,128)(2,1)S(1)} %bitcast.20, bf16[1024,2048]{1,0:T(8,128)(2,1)} %get-tuple-element.17.normed_far, ...), custom_call_target="tpu_custom_call" | custom-call | flops 5000000000 | bytes 6000000 | tf_op jit(solution)/shard_map/prepare/pallas_call | solution.py:597
  118.8 0.0 copy-start.3
  118.8 0.8 copy-done.3
  119.6 0.0 copy-start
  119.6 8.4 %all-to-all-done.2 = bf16[16,128,128]{2,1,0:T(8,128)(2,1)S(1)} async-done(((bf16[16,128,128]{2,1,0:T(8,128)(2,1)}), bf16[16,128,128]{2,1,0:T(8,128)(2,1)S(1)}, u32[]{:S(2)}, u32[]{:S(2)}) %all-to-all-start.2) | async-done | bytes 524320 | tf_op jit(solution)/shard_map/all_to_all | solution.py:710
  128.0 0.0 copy-done.1
  128.0 0.0 copy-done.2
  128.0 0.0 copy-done.13
  128.0 0.0 copy-start.4
  128.0 1.0 copy-done.4
  129.1 0.0 copy-start.15
  129.1 0.7 copy-done.15
  129.7 0.0 copy-start.7
  129.7 3.7 %backward.1 = (bf16[4,128,384]{2,1,0:T(8,128)(2,1)S(1)}, bf16[32,80,1024]{2,1,0:T(8,128)(2,1)S(1)}) custom-call(s32[4]{0:T(128)S(1)} %copy-done.14, f32[2]{0:T(128)S(1)} %copy-done.15, s32[16,16]{1,0:T(8,128)S(1)} %bitcast.24, bf16[128,2048]{1,0:T(8,128)(2,1)S(1)} %copy-done.1, bf16[128,2048]{1,0:T(8,128)(2,1)S(1)} %copy-done.2, ...), custom_call_target="tpu_custom_call" | custom-call | tf_op jit(solution)/shard_map/backward/pallas_call | solution.py:634
  133.4 11.2 %all_to_all.30.head_grads = bf16[4,128,384]{2,1,0:T(8,128)(2,1)S(1)} all-to-all(bf16[4,128,384]{2,1,0:T(8,128)(2,1)S(1)} %get-tuple-element.28), channel_id=1, replica_groups={{0,32,64,96},{128,160,192,224},{256,288,320,352},{384,416,448,480},{1,3..., dimensions={0} | all-to-all | bytes 786432 | tf_op jit(solution)/shard_map/all_to_all | solution.py:718
  144.6 0.0 copy-done.10
  144.6 0.0 copy-done
  144.6 0.0 copy-done.7
  144.6 0.0 copy-done.9
  144.6 4.1 %cores.1 = bf16[256,1024]{1,0:T(8,128)(2,1)S(1)} custom-call(bf16[128,512]{1,0:T(8,128)(2,1)S(1)} %copy-done.10, bf16[4,128,384]{2,1,0:T(8,128)(2,1)S(1)} %all_to_all.30.head_grads, bf16[32,80,1024]{2,1,0:T(8,128)(2,1)S(1)} %get-tuple-element.29.weights, bf16[128,1024]{1,0:T(8,128)(2,1)S(1)} %bitcast.22, bf16[1024,128]{1,0:T(8,128)(2,1)S(1)} %copy-done.9, ...), custom_call_target="tpu_custom_call" | custom-call | tf_op jit(solution)/shard_map/cores/pallas_call | solution.py:647
  148.8 30.1 %all_to_all.31 = bf16[32,8,1024]{2,1,0:T(8,128)(2,1)S(1)} all-to-all(bf16[32,8,1024]{2,1,0:T(8,128)(2,1)S(1)} %bitcast.18), channel_id=1, replica_groups=mesh['ctx'=16,'dp'=32] {'dp'}, dimensions={0} | all-to-all | bytes 1048576 | tf_op jit(solution)/shard_map/all_to_all | solution.py:722
  178.9 0.1 reduce_sum.21
  179.0 19.9 %all_to_all.32 = bf16[16,8,1024]{2,1,0:T(8,128)(2,1)S(1)} all-to-all(bf16[16,8,1024]{2,1,0:T(8,128)(2,1)S(1)} %broadcast_in_dim.28), channel_id=1, replica_groups=mesh['ctx'=16,'dp'=32] {'ctx'}, dimensions={0} | all-to-all | bytes 524288 | tf_op jit(solution)/shard_map/all_to_all | solution.py:688
  198.9 0.6 fusion.1
  (4 shorter events, 0.1 us)
Async XLA Ops:
  7.2 84.3 %all-gather.2.cloned.1.call-start = ((), (), s32[]{:S(2)}) async-start(), calls=%async_computation.6 | async-start | bytes 5406720 | tf_op jit(solution)/shard_map/all_gather | solution.py:695
  10.3 27.6 %all-to-all-start = ((s32[16,8,128]{2,1,0:T(8,128)}), s32[16,8,128]{2,1,0:T(8,128)S(1)}, u32[]{:S(2)}, u32[]{:S(2)}) async-start(s32[16,8,128]{2,1,0:T(8,128)} %broadcast_in_dim.11), calls=%async_computation | async-start | bytes 131072 | tf_op jit(solution)/shard_map/all_to_all | solution.py:688
  37.9 29.2 %copy-start.11 = (s32[16,8,128]{2,1,0:T(8,128)}, s32[16,8,128]{2,1,0:T(8,128)S(1)}, u32[]{:S(2)}) copy-start(s32[16,8,128]{2,1,0:T(8,128)S(1)} %all-to-all-done.indices) | copy-start | bytes 196612
  38.7 28.3 %all-to-all-start.1 = ((bf16[32,8,1024]{2,1,0:T(8,128)(2,1)}), bf16[32,8,1024]{2,1,0:T(8,128)(2,1)S(1)}, u32[]{:S(2)}, u32[]{:S(2)}) async-start(bf16[32,8,1024]{2,1,0:T(8,128)(2,1)} %broadcast_in_dim.12), calls=%async_computation.1 | async-start | bytes 1048576 | tf_op jit(solution)/shard_map/all_to_all | solution.py:688
  67.1 0.8 copy-start.5
  91.5 19.8 %copy-start.6 = (bf16[32,8,1024]{2,1,0:T(8,128)(2,1)S(1)}, bf16[32,8,1024]{2,1,0:T(8,128)(2,1)}, u32[]{:S(2)}) copy-start(bf16[32,8,1024]{2,1,0:T(8,128)(2,1)} %copy-done.5) | copy-start | bytes 1572868
  91.5 19.8 %copy-start.14 = (s32[4]{0:T(128)S(1)}, s32[4]{0:T(128)}, u32[]{:S(2)}) copy-start(s32[4]{0:T(128)} %pad_add_fusion.1.info) | copy-start | bytes 52
  100.2 27.8 %all-to-all-start.2 = ((bf16[16,128,128]{2,1,0:T(8,128)(2,1)}), bf16[16,128,128]{2,1,0:T(8,128)(2,1)S(1)}, u32[]{:S(2)}, u32[]{:S(2)}) async-start(bf16[16,128,128]{2,1,0:T(8,128)(2,1)} %get-tuple-element.26), calls=%async_computation.2 | async-start | bytes 1048576 | tf_op jit(solution)/shard_map/all_to_all | solution.py:710
  111.3 1.0 copy-start.8
  112.3 0.8 copy-start.12
  113.1 1.2 copy-start.16
  114.3 0.9 copy-start.17
  115.2 12.8 %copy-start.1 = (bf16[128,2048]{1,0:T(8,128)(2,1)S(1)}, bf16[128,2048]{1,0:T(8,128)(2,1)}, u32[]{:S(2)}) copy-start(bf16[128,2048]{1,0:T(8,128)(2,1)} %get-tuple-element.23.keys_head) | copy-start | bytes 1572868
  115.2 12.8 %copy-start.2 = (bf16[128,2048]{1,0:T(8,128)(2,1)S(1)}, bf16[128,2048]{1,0:T(8,128)(2,1)}, u32[]{:S(2)}) copy-start(bf16[128,2048]{1,0:T(8,128)(2,1)} %get-tuple-element.24.values_head) | copy-start | bytes 1572868
  115.2 12.8 %copy-start.13 = (s32[16,1,16]{2,1,0:T(1,128)S(1)}, s32[16,1,16]{2,1,0:T(1,128)}, u32[]{:S(2)}) copy-start(s32[16,1,16]{2,1,0:T(1,128)} %slice.20) | copy-start | bytes 3076
  115.2 29.4 %copy-start.10 = (bf16[128,512]{1,0:T(8,128)(2,1)S(1)}, bf16[128,512]{1,0:T(8,128)(2,1)}, u32[]{:S(2)}) copy-start(bf16[128,512]{1,0:T(8,128)(2,1)} %get-tuple-element.22.gate_grads) | copy-start | bytes 393220
  118.8 0.8 copy-start.3
  119.6 25.0 %copy-start = (f32[2,1024,128]{2,1,0:T(8,128)S(1)}, f32[2,1024,128]{2,1,0:T(8,128)}, u32[]{:S(2)}) copy-start(f32[2,1024,128]{2,1,0:T(8,128)} %get-tuple-element.30.own_terms) | copy-start | bytes 3145732
  128.0 1.0 copy-start.4
  129.1 0.7 copy-start.15
  129.7 14.9 %copy-start.7 = (bf16[1,128,1024]{2,1,0:T(8,128)(2,1)S(1)}, bf16[1,128,1024]{2,1,0:T(8,128)(2,1)}, u32[]{:S(2)}) copy-start(bf16[1,128,1024]{2,1,0:T(8,128)(2,1)} %param.17) | copy-start | bytes 786436
  129.7 14.9 %copy-start.9 = (bf16[1024,128]{1,0:T(8,128)(2,1)S(1)}, bf16[1024,128]{1,0:T(8,128)(2,1)}, u32[]{:S(2)}) copy-start(bf16[1024,128]{1,0:T(8,128)(2,1)} %get-tuple-element.18.own_embedded) | copy-start | bytes 786436
Sparse Core Ops, SparseCore 0:
  10.7 80.7 all-gather.1

commit v6 on v5

--- a/solution.py
+++ b/solution.py
@@ -250,17 +250,19 @@
     grads_out,
     gate_out,
     hidden_out,
-    keys_head,
-    values_head,
-    out_t,
+    keys_far,
+    values_far,
+    out_far,
     keys_t,
     values_t,
     mixed,
     queries,
     weights,
     normed_t,
+    out_t,
     semaphores,
     tile_semaphores,
+    away,
 ):
     copies = fetch_weights(weights_far, weights, semaphores, (1, 3, 2, 0))
     me = info[0]
@@ -288,14 +290,17 @@
 
     lax.fori_loop(kv_low, kv_high, kv_tile, 0)
     head_rows = pl.ds(aligned(head, HD), HD)
-    keys_head[...] = keys_t[head_rows, :]
-    values_head[...] = values_t[head_rows, :]
+    leaving = [
+        fetch(keys_t.at[head_rows, :], keys_far, away.at[0]),
+        fetch(values_t.at[head_rows, :], values_far, away.at[1]),
+    ]
     copies[2].wait()
     copies[3].wait()
 
     for owner in range(NDP):
         out_t[owner * 32 : owner * 32 + 16, :] = weights[owner, 64:80, :E]
         out_t[owner * 32 + 16 : owner * 32 + 32, :] = weights[owner, 64:80, E:]
+    leaving.append(fetch(out_t, out_far, away.at[2]))
 
     own_normed = flip(normed_t[:, pl.ds(aligned(me, BLK), BLK)]).astype(BF16)
     pre_gate = mm_nt(own_normed, weight_rows(weights, 0))
@@ -332,6 +337,8 @@
         grads_out[place] = mixed_grad[:, h * HD : (h + 1) * HD]
     hidden_out[...] = (mixed_normed * gate).astype(BF16)
     gate_out[...] = (hidden_grad * mixed_normed * silu_slope(pre_gate)).astype(BF16)
+    for copy in leaving:
+        copy.wait()
 
 
 def prepare_kernel(
@@ -576,7 +583,7 @@
             shape((D, E), BF16),
         ),
         in_specs=[SMEM_SPEC] * 3 + [HBM_SPEC, HBM_SPEC, VMEM_SPEC],
-        out_specs=(VMEM_SPEC,) * 6,
+        out_specs=(VMEM_SPEC,) * 3 + (HBM_SPEC,) * 3,
         scratch_shapes=[
             pltpu.VMEM((E, SEQ), BF16),
             pltpu.VMEM((E, SEQ), BF16),
@@ -584,8 +591,10 @@
             pltpu.VMEM((BLK, E), BF16),
             pltpu.VMEM((NDP, 80, D), BF16),
             pltpu.VMEM((D, SEQ), BF16),
+            pltpu.VMEM((D, E), BF16),
             pltpu.SemaphoreType.DMA((4,)),
             pltpu.SemaphoreType.DMA((8,)),
+            pltpu.SemaphoreType.DMA((3,)),
         ],
         compiler_params=params(FORWARD_MB),
         cost_estimate=cost(8_000_000_000, 12_000_000),
@@ -659,45 +668,91 @@
     )(gate_grads, head_grads, weights, cotangent, own_embedded, own_terms, indices)
 
 
-def pack_kernel(proj_t, out_t, packed):
+def pack_kernel(
+    proj_t, out_t, firsts, seconds, mask_row, core_first, core_second, packed, indices, tables, own
+):
     packed[:64, :] = proj_t[...]
     packed[64:, :E] = out_t[:16, :]
     packed[64:, E:] = out_t[16:, :]
-
-
-def pack_weights(w_proj, w_out):
+    indices[...] = jnp.zeros((NBLK, 8, BLK), jnp.int32)
+    table = jnp.concatenate([core_first[...], core_second[...]], axis=0)
+    for place in range(NBLK):
+        indices[place, 0:1, :] = firsts[...]
+        indices[place, 1:2, :] = seconds[...]
+        indices[place, 2:3, 0:NBLK] = mask_row[...]
+    for place in range(NDP):
+        tables[place] = table
+    own[...] = indices[0]
+
+
+def pack_stage(w_proj, w_out, item_first, item_second, block_mask, core_first, core_second):
     return pl.pallas_call(
         pack_kernel,
-        out_shape=shape((80, D), BF16),
-        in_specs=[VMEM_SPEC] * 2,
-        out_specs=VMEM_SPEC,
+        out_shape=(
+            shape((80, D), BF16),
+            shape((NBLK, 8, BLK), jnp.int32),
+            shape((NDP, 8, D), BF16),
+            shape((8, BLK), jnp.int32),
+        ),
+        in_specs=[VMEM_SPEC] * 7,
+        out_specs=(VMEM_SPEC,) * 4,
         compiler_params=params(60),
         name="pack",
-    )(w_proj.T, w_out.T)
-
-
-def pack_indices(item_first, item_second, block_mask):
-    mask_row = jnp.pad(block_mask[0], ((0, 0), (0, BLK - NBLK)))
-    return jnp.concatenate(
-        [item_first, item_second, mask_row, jnp.zeros((5, BLK), jnp.int32)], axis=0
-    )
-
-
-def spread(values, axis, count):
-    copies = jnp.broadcast_to(values[None], (count,) + values.shape)
-    return lax.all_to_all(copies, axis, 0, 0)
+    )(w_proj.T, w_out.T, item_first, item_second, block_mask[0], core_first, core_second)
+
+
+def sum_kernel(received, copies):
+    total = jnp.sum(received[...].astype(F32), axis=0).astype(BF16)
+    for place in range(4):
+        copies[place] = total
+
+
+def sum_stage(received):
+    return pl.pallas_call(
+        sum_kernel,
+        out_shape=shape((4, 8, D), BF16),
+        in_specs=[VMEM_SPEC],
+        out_specs=VMEM_SPEC,
+        compiler_params=params(16),
+        name="sum",
+    )(received)
+
+
+def last_kernel(received, grad_first, grad_second):
+    total = jnp.sum(received[...].astype(F32), axis=0)
+    grad_first[...] = total[:4]
+    grad_second[...] = total[4:]
+
+
+def last_stage(received):
+    return pl.pallas_call(
+        last_kernel,
+        out_shape=(shape((4, D), F32), shape((4, D), F32)),
+        in_specs=[VMEM_SPEC],
+        out_specs=(VMEM_SPEC,) * 2,
+        compiler_params=params(16),
+        name="last",
+    )(received)
+
+
+NEAR = [[4 * c + h for h in range(4)] for c in range(4)]
+FAR = [[4 * c + h for c in range(4)] for h in range(4)]
+
+
+def exchange(values, axis, groups=None):
+    return lax.all_to_all(values, axis, 0, 0, axis_index_groups=groups)
 
 
 def local(
     item_first, item_second, lengths, block_mask, core_first, core_second, w_proj, w_out, cotangent
 ):
     me = lax.axis_index("ctx").astype(jnp.int32)
-    weights = lax.all_gather(pack_weights(w_proj, w_out), "dp", axis=0, tiled=True)
-    weights = weights.reshape(NDP, 80, D)
-    table = spread(jnp.concatenate([core_first, core_second], axis=0), "dp", NDP)
-    table = table.reshape(2 * ROWS, D)
-    own_indices = pack_indices(item_first, item_second, block_mask)
-    indices = spread(own_indices, "ctx", NBLK)
+    packed, index_copies, table_copies, own_indices = pack_stage(
+        w_proj, w_out, item_first, item_second, block_mask, core_first, core_second
+    )
+    weights = lax.all_gather(packed, "dp", axis=0, tiled=True).reshape(NDP, 80, D)
+    indices = exchange(index_copies, "ctx")
+    table = exchange(table_copies, "dp").reshape(2 * ROWS, D)
     mask = indices[:, 2, :NBLK]
     info = jnp.stack([me, lengths[0, 0], lengths[0, 1], me])
     inverse = 1.0 / lengths[0].astype(F32)
@@ -714,15 +769,14 @@
     pre_grads, weights_near = backward_stage(
         info, inverse, mask, keys_head, values_head, queries_head, grads, slopes, weights
     )
-    groups = [[4 * c + h for h in range(4)] for c in range(4)]
-    head_grads = lax.all_to_all(pre_grads, "ctx", 0, 0, axis_index_groups=groups)
+    head_grads = exchange(pre_grads, "ctx", NEAR)
     partial = core_stage(
         gate_grads, head_grads, weights_near, upstream, own_embedded, own_terms, own_indices
     )
-    received = lax.all_to_all(partial.reshape(NDP, 8, D), "dp", 0, 0)
-    pair_sum = jnp.sum(received.astype(F32), axis=0).astype(BF16)
-    total = jnp.sum(spread(pair_sum, "ctx", NBLK).astype(F32), axis=0)
-    return (layer_out[None], total[:4], total[4:])
+    received = exchange(partial.reshape(NDP, 8, D), "dp")
+    near_sum = exchange(sum_stage(received), "ctx", NEAR)
+    grad_first, grad_second = last_stage(exchange(sum_stage(near_sum), "ctx", FAR))
+    return (layer_out[None], grad_first, grad_second)
 
 
 def solution(mesh):

time: 207 us -> 212 us (1.024)
  blocking collectives: 61.2 us -> 90.5 us
  starting transfers between devices: 36.5 us -> 22 us
  waiting for transfers between devices: 45.9 us -> 38.4 us
  local copies, waits for them, and re-layouts: 11.4 us -> 9.2 us
    all_to_all x3 -> x5, blocking collectives: 61.2 us -> 90.5 us  [exchange(): return lax.all_to_all(values, axis, 0, 0, axis_index_groups=groups)]
    all_to_all x2 -> x1, starting transfers between devices: 25.4 us -> 9.22 us  [exchange(): return lax.all_to_all(values, axis, 0, 0, axis_index_groups=groups)]
    all_to_all x2 -> x1, waiting for transfers between devices: 24.7 us -> 14.5 us  [exchange(): return lax.all_to_all(values, axis, 0, 0, axis_index_groups=groups)]
    unnamed x36 -> x38, local copies, waits for them, and re-layouts: 7.24 us -> 7.25 us
  transfers between devices with their start and end apart: 4 -> 3, of which waited for: 4 -> 3; matrix products, arithmetic and copies ran while one was open for 4% -> 2% of each run, Pallas kernels for 7% -> 7%
where the time goes in v6:
time: 212 us; the launch traced here: 211 us
  blocking collectives  90.5 us (43%)
  waiting for transfers between devices  38.4 us (18%)
  Pallas kernels  33.1 us (16%)
  starting transfers between devices  22 us (10%)
  between operations  14.2 us (7%)
  local copies, waits for them, and re-layouts  9.2 us (4%)
  other arithmetic  3.15 us (1%)
    all_to_all x5, blocking collectives, exchange(): return lax.all_to_all(values, axis, 0, 0, axis_index_groups=groups)  90.5 us
    all_to_all x1, waiting for transfers between devices, exchange(): return lax.all_to_all(values, axis, 0, 0, axis_index_groups=groups)  14.5 us
    all_gather x1, waiting for transfers between devices, local(): lax.all_gather(packed, 'dp', axis=0, tiled=True).reshape(NDP, 80, D)  13.8 us
    all_to_all x1, starting transfers between devices, local(): grads = lax.all_to_all(grads, 'ctx', 0, 0).reshape(SEQ, HD)  12.7 us
    pallas_call x1, Pallas kernels, embed_stage(): pl.pallas_call(embed_kernel, out_shape=(shape((D, SEQ), BF16), shape((2,...  10.8 us
    all_to_all x1, waiting for transfers between devices, local(): grads = lax.all_to_all(grads, 'ctx', 0, 0).reshape(SEQ, HD)  10.2 us
    all_to_all x1, starting transfers between devices, exchange(): return lax.all_to_all(values, axis, 0, 0, axis_index_groups=groups)  9.22 us
    pallas_call x1, Pallas kernels, forward_stage(): pl.pallas_call(forward_kernel, out_shape=(shape((NBLK, BLK, HD), BF16), s...  8.36 us
  transfers between devices with their start and end apart: 3, of which 3 were waited for; matrix products, arithmetic and copies ran while one was open for 2% of the time, Pallas kernels for 7%

profile of v6, /device:TPU:1, one launch (start us, length us, event | category | flops | bytes accessed | tf_op | source)
XLA Modules:
  0.0 210.6 jit_solution(7232912900325299302)
XLA Ops:
  7.2 0.0 all-gather.2.cloned.1.call-start
  7.2 1.9 pack.1
  9.1 0.0 all-gather.2.cloned.1.call-update
  9.1 27.6 %all_to_all.35.indices = s32[16,8,128]{2,1,0:T(8,128)S(1)} all-to-all(s32[16,8,128]{2,1,0:T(8,128)} %get-tuple-element.23), channel_id=1, replica_groups=mesh['ctx'=16,'dp'=32] {'ctx'}, dimensions={0} | all-to-all | bytes 131072 | tf_op jit(solution)/shard_map/all_to_all | solution.py:743
  36.7 0.0 copy-start.11
  36.7 9.2 %all-to-all-start.1 = ((bf16[32,8,1024]{2,1,0:T(8,128)(2,1)}), bf16[32,8,1024]{2,1,0:T(8,128)(2,1)S(1)}, u32[]{:S(2)}, u32[]{:S(2)}) async-start(bf16[32,8,1024]{2,1,0:T(8,128)(2,1)} %get-tuple-element.24), calls=%async_computation.1 | async-start | bytes 1048576 | tf_op jit(solution)/shard_map/all_to_all | solution.py:743
  45.9 1.3 fusion
  47.2 1.9 pad_add_fusion.info
  49.1 1.3 divide_bitcast_fusion.inverse
  50.4 0.6 slice.12
  51.0 14.5 %all-to-all-done.1 = bf16[32,8,1024]{2,1,0:T(8,128)(2,1)S(1)} async-done(((bf16[32,8,1024]{2,1,0:T(8,128)(2,1)}), bf16[32,8,1024]{2,1,0:T(8,128)(2,1)S(1)}, u32[]{:S(2)}, u32[]{:S(2)}) %all-to-all-start.1) | async-done | bytes 524320 | tf_op jit(solution)/shard_map/all_to_all | solution.py:743
  65.5 0.0 copy-start.5
  65.5 0.0 copy-done.11
  65.5 0.8 copy-done.5
  66.3 10.8 %embed.1 = (bf16[1024,2048]{1,0:T(8,128)(2,1)}, f32[2,1024,128]{2,1,0:T(8,128)}, bf16[1024,128]{1,0:T(8,128)(2,1)}) custom-call(s32[4]{0:T(128)} %pad_add_fusion.info, s32[16,8,128]{2,1,0:T(8,128)} %copy-done.11, bf16[256,1024]{1,0:T(8,128)(2,1)} %bitcast.19), custom_call_target="tpu_custom_call" | custom-call | flops 20000000000 | bytes 6000000 | tf_op jit(solution)/shard_map/embed/pallas_call | solution.py:551
  77.1 13.8 %all-gather.2.cloned.1.call-done = bf16[2560,1024]{1,0:T(8,128)(2,1)} async-done(((bf16[80,1024]{1,0:T(8,128)(2,1)}), bf16[2560,1024]{1,0:T(8,128)(2,1)}) %all-gather.2.cloned.1.call-update) | async-done | bytes 5242896 | tf_op jit(solution)/shard_map/all_gather | solution.py:753
  90.9 0.0 copy-start.6
  90.9 0.0 copy-start.15
  90.9 8.4 %forward.1 = (bf16[16,128,128]{2,1,0:T(8,128)(2,1)}, bf16[128,512]{1,0:T(8,128)(2,1)}, bf16[128,512]{1,0:T(8,128)(2,1)}, bf16[128,2048]{1,0:T(8,128)(2,1)}, bf16...) custom-call(s32[4]{0:T(128)} %pad_add_fusion.info, f32[2]{0:T(128)} %divide_bitcast_fusion.inverse, s32[16,16]{1,0:T(8,128)} %bitcast.23, ...), custom_call_target="tpu_custom_call" | custom-call | flops 8000000000 | bytes 12000000 | tf_op jit(solution)/shard_map/forward/pallas_call | solution.py:575
  99.3 12.7 %all-to-all-start.2 = ((bf16[16,128,128]{2,1,0:T(8,128)(2,1)}), bf16[16,128,128]{2,1,0:T(8,128)(2,1)S(1)}, u32[]{:S(2)}, u32[]{:S(2)}) async-start(bf16[16,128,128]{2,1,0:T(8,128)(2,1)} %get-tuple-element.35), calls=%async_computation.2 | async-start | bytes 1048576 | tf_op jit(solution)/shard_map/all_to_all | solution.py:765
  112.0 0.0 copy-done.6
  112.0 0.0 copy-done.15
  112.0 0.0 copy-start.8
  112.0 0.9 copy-done.8
  112.9 0.0 copy-start.12
  112.9 0.8 copy-done.12
  113.8 0.0 copy-start.17
  113.8 1.2 copy-done.17
  115.0 0.0 copy-start.18
  115.0 0.9 copy-done.18
  115.9 0.0 copy-start.1
  115.9 0.0 copy-start.2
  115.9 0.0 copy-start.13
  115.9 0.0 copy-start.10
  115.9 0.0 copy-start.14
  115.9 3.6 %prepare.1 = (bf16[128,1024]{1,0:T(8,128)(2,1)}, bf16[128,2048]{1,0:T(8,128)(2,1)S(1)}, f32[512,384]{1,0:T(8,128)S(1)}) custom-call(s32[4]{0:T(128)S(1)} %copy-done.15, s32[16,8,128]{2,1,0:T(8,128)S(1)} %copy-done.12, bf16[256,1024]{1,0:T(8,128)(2,1)S(1)} %bitcast.20, bf16[1024,2048]{1,0:T(8,128)(2,1)} %get-tuple-element.25.normed_far, ...), custom_call_target="tpu_custom_call" | custom-call | flops 5000000000 | bytes 6000000 | tf_op jit(solution)/shard_map/prepare/pallas_call | solution.py:606
  119.5 0.0 copy-start.3
  119.5 0.8 copy-done.3
  120.3 0.0 copy-start
  120.3 10.2 %all-to-all-done.2 = bf16[16,128,128]{2,1,0:T(8,128)(2,1)S(1)} async-done(((bf16[16,128,128]{2,1,0:T(8,128)(2,1)}), bf16[16,128,128]{2,1,0:T(8,128)(2,1)S(1)}, u32[]{:S(2)}, u32[]{:S(2)}) %all-to-all-start.2) | async-done | bytes 524320 | tf_op jit(solution)/shard_map/all_to_all | solution.py:765
  130.5 0.0 copy-done.1
  130.5 0.0 copy-done.2
  130.5 0.0 copy-done.13
  130.5 0.0 copy-start.4
  130.5 1.0 copy-done.4
  131.5 0.0 copy-start.16
  131.5 0.7 copy-done.16
  132.2 0.0 copy-start.7
  132.2 0.0 copy-start.9
  132.2 3.7 %backward.1 = (bf16[4,128,384]{2,1,0:T(8,128)(2,1)S(1)}, bf16[32,80,1024]{2,1,0:T(8,128)(2,1)S(1)}) custom-call(s32[4]{0:T(128)S(1)} %copy-done.15, f32[2]{0:T(128)S(1)} %copy-done.16, s32[16,16]{1,0:T(8,128)S(1)} %bitcast.24, bf16[128,2048]{1,0:T(8,128)(2,1)S(1)} %copy-done.1, bf16[128,2048]{1,0:T(8,128)(2,1)S(1)} %copy-done.2, ...), custom_call_target="tpu_custom_call" | custom-call | tf_op jit(solution)/shard_map/backward/pallas_call | solution.py:643
  135.9 11.3 %all_to_all.36.head_grads = bf16[4,128,384]{2,1,0:T(8,128)(2,1)S(1)} all-to-all(bf16[4,128,384]{2,1,0:T(8,128)(2,1)S(1)} %get-tuple-element.37), channel_id=1, replica_groups={{0,32,64,96},{128,160,192,224},{256,288,320,352},{384,416,448,480},{1,3..., dimensions={0} | all-to-all | bytes 786432 | tf_op jit(solution)/shard_map/all_to_all | solution.py:743
  147.1 0.0 copy-done.10
  147.1 0.0 copy-done.14
  147.1 0.0 copy-done
  147.1 0.0 copy-done.7
  147.1 0.0 copy-done.9
  147.1 4.2 %cores.1 = bf16[256,1024]{1,0:T(8,128)(2,1)S(1)} custom-call(bf16[128,512]{1,0:T(8,128)(2,1)S(1)} %copy-done.10, bf16[4,128,384]{2,1,0:T(8,128)(2,1)S(1)} %all_to_all.36.head_grads, bf16[32,80,1024]{2,1,0:T(8,128)(2,1)S(1)} %get-tuple-element.38.weights, bf16[128,1024]{1,0:T(8,128)(2,1)S(1)} %bitcast.22, bf16[1024,128]{1,0:T(8,128)(2,1)S(1)} %copy-done.9, ...), custom_call_target="tpu_custom_call" | custom-call | tf_op jit(solution)/shard_map/cores/pallas_call | solution.py:656
  151.3 26.2 %all_to_all.37.received = bf16[32,8,1024]{2,1,0:T(8,128)(2,1)S(1)} all-to-all(bf16[32,8,1024]{2,1,0:T(8,128)(2,1)S(1)} %bitcast.18), channel_id=1, replica_groups=mesh['ctx'=16,'dp'=32] {'dp'}, dimensions={0} | all-to-all | bytes 1048576 | tf_op jit(solution)/shard_map/all_to_all | solution.py:743
  177.5 0.1 sum.2
  177.6 7.0 %all_to_all.38.received = bf16[4,8,1024]{2,1,0:T(8,128)(2,1)S(1)} all-to-all(bf16[4,8,1024]{2,1,0:T(8,128)(2,1)S(1)} %sum.2), channel_id=1, replica_groups={{0,32,64,96},{128,160,192,224},{256,288,320,352},{384,416,448,480},{1,3..., dimensions={0} | all-to-all | bytes 131072 | tf_op jit(solution)/shard_map/all_to_all | solution.py:743
  184.6 18.5 %all_to_all.39.received = bf16[4,8,1024]{2,1,0:T(8,128)(2,1)S(1)} all-to-all(bf16[4,8,1024]{2,1,0:T(8,128)(2,1)S(1)} %sum.3), channel_id=1, replica_groups={{0,128,256,384},{32,160,288,416},{64,192,320,448},{96,224,352,480},{1,1..., dimensions={0} | all-to-all | bytes 131072 | tf_op jit(solution)/shard_map/all_to_all | solution.py:743
  203.1 0.6 last.1
  (1 shorter events, 0.0 us)
Async XLA Ops:
  7.2 83.7 %all-gather.2.cloned.1.call-start = ((), (), s32[]{:S(2)}) async-start(), calls=%async_computation.7 | async-start | bytes 5406720 | tf_op jit(solution)/shard_map/all_gather | solution.py:753
  36.7 28.8 %copy-start.11 = (s32[16,8,128]{2,1,0:T(8,128)}, s32[16,8,128]{2,1,0:T(8,128)S(1)}, u32[]{:S(2)}) copy-start(s32[16,8,128]{2,1,0:T(8,128)S(1)} %all_to_all.35.indices) | copy-start | bytes 196612
  36.7 28.8 %all-to-all-start.1 = ((bf16[32,8,1024]{2,1,0:T(8,128)(2,1)}), bf16[32,8,1024]{2,1,0:T(8,128)(2,1)S(1)}, u32[]{:S(2)}, u32[]{:S(2)}) async-start(bf16[32,8,1024]{2,1,0:T(8,128)(2,1)} %get-tuple-element.24), calls=%async_computation.1 | async-start | bytes 1048576 | tf_op jit(solution)/shard_map/all_to_all | solution.py:743
  65.5 0.8 copy-start.5
  90.9 21.1 %copy-start.6 = (bf16[32,8,1024]{2,1,0:T(8,128)(2,1)S(1)}, bf16[32,8,1024]{2,1,0:T(8,128)(2,1)}, u32[]{:S(2)}) copy-start(bf16[32,8,1024]{2,1,0:T(8,128)(2,1)} %copy-done.5) | copy-start | bytes 1572868
  90.9 21.1 %copy-start.15 = (s32[4]{0:T(128)S(1)}, s32[4]{0:T(128)}, u32[]{:S(2)}) copy-start(s32[4]{0:T(128)} %pad_add_fusion.info) | copy-start | bytes 52
  99.3 31.2 %all-to-all-start.2 = ((bf16[16,128,128]{2,1,0:T(8,128)(2,1)}), bf16[16,128,128]{2,1,0:T(8,128)(2,1)S(1)}, u32[]{:S(2)}, u32[]{:S(2)}) async-start(bf16[16,128,128]{2,1,0:T(8,128)(2,1)} %get-tuple-element.35), calls=%async_computation.2 | async-start | bytes 1048576 | tf_op jit(solution)/shard_map/all_to_all | solution.py:765
  112.0 1.0 copy-start.8
  112.9 0.8 copy-start.12
  113.8 1.2 copy-start.17
  115.0 0.9 copy-start.18
  115.9 14.6 %copy-start.1 = (bf16[128,2048]{1,0:T(8,128)(2,1)S(1)}, bf16[128,2048]{1,0:T(8,128)(2,1)}, u32[]{:S(2)}) copy-start(bf16[128,2048]{1,0:T(8,128)(2,1)} %get-tuple-element.32.keys_head) | copy-start | bytes 1572868
  115.9 14.6 %copy-start.2 = (bf16[128,2048]{1,0:T(8,128)(2,1)S(1)}, bf16[128,2048]{1,0:T(8,128)(2,1)}, u32[]{:S(2)}) copy-start(bf16[128,2048]{1,0:T(8,128)(2,1)} %get-tuple-element.33.values_head) | copy-start | bytes 1572868
  115.9 14.6 %copy-start.13 = (s32[16,1,16]{2,1,0:T(1,128)S(1)}, s32[16,1,16]{2,1,0:T(1,128)}, u32[]{:S(2)}) copy-start(s32[16,1,16]{2,1,0:T(1,128)} %slice.12) | copy-start | bytes 3076
  115.9 31.2 %copy-start.10 = (bf16[128,512]{1,0:T(8,128)(2,1)S(1)}, bf16[128,512]{1,0:T(8,128)(2,1)}, u32[]{:S(2)}) copy-start(bf16[128,512]{1,0:T(8,128)(2,1)} %get-tuple-element.31.gate_grads) | copy-start | bytes 393220
  115.9 31.2 %copy-start.14 = (s32[8,128]{1,0:T(8,128)S(1)}, s32[8,128]{1,0:T(8,128)}, u32[]{:S(2)}) copy-start(s32[8,128]{1,0:T(8,128)} %get-tuple-element.40.indices) | copy-start | bytes 12292
  119.5 0.8 copy-start.3
  120.3 26.8 %copy-start = (f32[2,1024,128]{2,1,0:T(8,128)S(1)}, f32[2,1024,128]{2,1,0:T(8,128)}, u32[]{:S(2)}) copy-start(f32[2,1024,128]{2,1,0:T(8,128)} %get-tuple-element.39.own_terms) | copy-start | bytes 3145732
  130.5 1.0 copy-start.4
  131.5 0.7 copy-start.16
  132.2 14.9 %copy-start.7 = (bf16[1,128,1024]{2,1,0:T(8,128)(2,1)S(1)}, bf16[1,128,1024]{2,1,0:T(8,128)(2,1)}, u32[]{:S(2)}) copy-start(bf16[1,128,1024]{2,1,0:T(8,128)(2,1)} %param.17) | copy-start | bytes 786436
  132.2 14.9 %copy-start.9 = (bf16[1024,128]{1,0:T(8,128)(2,1)S(1)}, bf16[1024,128]{1,0:T(8,128)(2,1)}, u32[]{:S(2)}) copy-start(bf16[1024,128]{1,0:T(8,128)(2,1)} %get-tuple-element.26.own_embedded) | copy-start | bytes 786436
Sparse Core Ops, SparseCore 0:
  10.7 80.1 all-gather.1

commit v7 on v6

--- a/solution.py
+++ b/solution.py
@@ -703,14 +703,14 @@
 
 def sum_kernel(received, copies):
     total = jnp.sum(received[...].astype(F32), axis=0).astype(BF16)
-    for place in range(4):
+    for place in range(NBLK):
         copies[place] = total
 
 
 def sum_stage(received):
     return pl.pallas_call(
         sum_kernel,
-        out_shape=shape((4, 8, D), BF16),
+        out_shape=shape((NBLK, 8, D), BF16),
         in_specs=[VMEM_SPEC],
         out_specs=VMEM_SPEC,
         compiler_params=params(16),
@@ -736,7 +736,6 @@
 
 
 NEAR = [[4 * c + h for h in range(4)] for c in range(4)]
-FAR = [[4 * c + h for c in range(4)] for h in range(4)]
 
 
 def exchange(values, axis, groups=None):
@@ -774,8 +773,7 @@
         gate_grads, head_grads, weights_near, upstream, own_embedded, own_terms, own_indices
     )
     received = exchange(partial.reshape(NDP, 8, D), "dp")
-    near_sum = exchange(sum_stage(received), "ctx", NEAR)
-    grad_first, grad_second = last_stage(exchange(sum_stage(near_sum), "ctx", FAR))
+    grad_first, grad_second = last_stage(exchange(sum_stage(received), "ctx"))
     return (layer_out[None], grad_first, grad_second)
 
 

time: 212 us -> 207 us (0.976)
  blocking collectives: 90.5 us -> 86.1 us
    all_to_all x5 -> x4, blocking collectives: 90.5 us -> 86.1 us  [exchange(): return lax.all_to_all(values, axis, 0, 0, axis_index_groups=groups)]
where the time goes in v7:
time: 207 us; the launch traced here: 206 us
  blocking collectives  86.1 us (42%)
  waiting for transfers between devices  38.4 us (19%)
  Pallas kernels  33.2 us (16%)
  starting transfers between devices  21.9 us (11%)
  between operations  14.2 us (7%)
  local copies, waits for them, and re-layouts  9.2 us (4%)
  other arithmetic  3.15 us (2%)
    all_to_all x4, blocking collectives, exchange(): return lax.all_to_all(values, axis, 0, 0, axis_index_groups=groups)  86.1 us
    all_to_all x1, waiting for transfers between devices, exchange(): return lax.all_to_all(values, axis, 0, 0, axis_index_groups=groups)  14.5 us
    all_gather x1, waiting for transfers between devices, local(): lax.all_gather(packed, 'dp', axis=0, tiled=True).reshape(NDP, 80, D)  13.8 us
    all_to_all x1, starting transfers between devices, local(): grads = lax.all_to_all(grads, 'ctx', 0, 0).reshape(SEQ, HD)  12.7 us
    pallas_call x1, Pallas kernels, embed_stage(): pl.pallas_call(embed_kernel, out_shape=(shape((D, SEQ), BF16), shape((2,...  10.8 us
    all_to_all x1, waiting for transfers between devices, local(): grads = lax.all_to_all(grads, 'ctx', 0, 0).reshape(SEQ, HD)  10.1 us
    all_to_all x1, starting transfers between devices, exchange(): return lax.all_to_all(values, axis, 0, 0, axis_index_groups=groups)  9.22 us
    pallas_call x1, Pallas kernels, forward_stage(): pl.pallas_call(forward_kernel, out_shape=(shape((NBLK, BLK, HD), BF16), s...  8.36 us
  transfers between devices with their start and end apart: 3, of which 3 were waited for; matrix products, arithmetic and copies ran while one was open for 2% of the time, Pallas kernels for 7%

profile of v7, /device:TPU:1, one launch (start us, length us, event | category | flops | bytes accessed | tf_op | source)
XLA Modules:
  0.0 206.2 jit_solution(1595928316653230837)
XLA Ops:
  7.2 0.0 all-gather.2.cloned.1.call-start
  7.2 1.9 pack.1
  9.1 0.0 all-gather.2.cloned.1.call-update
  9.1 27.6 %all_to_all.30.indices = s32[16,8,128]{2,1,0:T(8,128)S(1)} all-to-all(s32[16,8,128]{2,1,0:T(8,128)} %get-tuple-element.23), channel_id=1, replica_groups=mesh['ctx'=16,'dp'=32] {'ctx'}, dimensions={0} | all-to-all | bytes 131072 | tf_op jit(solution)/shard_map/all_to_all | solution.py:742
  36.7 0.0 copy-start.11
  36.7 9.2 %all-to-all-start.1 = ((bf16[32,8,1024]{2,1,0:T(8,128)(2,1)}), bf16[32,8,1024]{2,1,0:T(8,128)(2,1)S(1)}, u32[]{:S(2)}, u32[]{:S(2)}) async-start(bf16[32,8,1024]{2,1,0:T(8,128)(2,1)} %get-tuple-element.24), calls=%async_computation.1 | async-start | bytes 1048576 | tf_op jit(solution)/shard_map/all_to_all | solution.py:742
  45.9 1.3 fusion
  47.2 1.9 pad_add_fusion.info
  49.1 1.3 divide_bitcast_fusion.inverse
  50.4 0.6 slice.12
  51.0 14.5 %all-to-all-done.1 = bf16[32,8,1024]{2,1,0:T(8,128)(2,1)S(1)} async-done(((bf16[32,8,1024]{2,1,0:T(8,128)(2,1)}), bf16[32,8,1024]{2,1,0:T(8,128)(2,1)S(1)}, u32[]{:S(2)}, u32[]{:S(2)}) %all-to-all-start.1) | async-done | bytes 524320 | tf_op jit(solution)/shard_map/all_to_all | solution.py:742
  65.5 0.0 copy-start.5
  65.5 0.0 copy-done.11
  65.5 0.8 copy-done.5
  66.3 10.8 %embed.1 = (bf16[1024,2048]{1,0:T(8,128)(2,1)}, f32[2,1024,128]{2,1,0:T(8,128)}, bf16[1024,128]{1,0:T(8,128)(2,1)}) custom-call(s32[4]{0:T(128)} %pad_add_fusion.info, s32[16,8,128]{2,1,0:T(8,128)} %copy-done.11, bf16[256,1024]{1,0:T(8,128)(2,1)} %bitcast.19), custom_call_target="tpu_custom_call" | custom-call | flops 20000000000 | bytes 6000000 | tf_op jit(solution)/shard_map/embed/pallas_call | solution.py:551
  77.1 13.8 %all-gather.2.cloned.1.call-done = bf16[2560,1024]{1,0:T(8,128)(2,1)} async-done(((bf16[80,1024]{1,0:T(8,128)(2,1)}), bf16[2560,1024]{1,0:T(8,128)(2,1)}) %all-gather.2.cloned.1.call-update) | async-done | bytes 5242896 | tf_op jit(solution)/shard_map/all_gather | solution.py:752
  90.9 0.0 copy-start.6
  90.9 0.0 copy-start.15
  90.9 8.4 %forward.1 = (bf16[16,128,128]{2,1,0:T(8,128)(2,1)}, bf16[128,512]{1,0:T(8,128)(2,1)}, bf16[128,512]{1,0:T(8,128)(2,1)}, bf16[128,2048]{1,0:T(8,128)(2,1)}, bf16...) custom-call(s32[4]{0:T(128)} %pad_add_fusion.info, f32[2]{0:T(128)} %divide_bitcast_fusion.inverse, s32[16,16]{1,0:T(8,128)} %bitcast.23, ...), custom_call_target="tpu_custom_call" | custom-call | flops 8000000000 | bytes 12000000 | tf_op jit(solution)/shard_map/forward/pallas_call | solution.py:575
  99.3 12.7 %all-to-all-start.2 = ((bf16[16,128,128]{2,1,0:T(8,128)(2,1)}), bf16[16,128,128]{2,1,0:T(8,128)(2,1)S(1)}, u32[]{:S(2)}, u32[]{:S(2)}) async-start(bf16[16,128,128]{2,1,0:T(8,128)(2,1)} %get-tuple-element.35), calls=%async_computation.2 | async-start | bytes 1048576 | tf_op jit(solution)/shard_map/all_to_all | solution.py:764
  111.9 0.0 copy-done.6
  112.0 0.0 copy-done.15
  112.0 0.0 copy-start.8
  112.0 0.9 copy-done.8
  112.9 0.0 copy-start.12
  112.9 0.8 copy-done.12
  113.8 0.0 copy-start.17
  113.8 1.2 copy-done.17
  115.0 0.0 copy-start.18
  115.0 0.9 copy-done.18
  115.9 0.0 copy-start.1
  115.9 0.0 copy-start.2
  115.9 0.0 copy-start.13
  115.9 0.0 copy-start.10
  115.9 0.0 copy-start.14
  115.9 3.6 %prepare.1 = (bf16[128,1024]{1,0:T(8,128)(2,1)}, bf16[128,2048]{1,0:T(8,128)(2,1)S(1)}, f32[512,384]{1,0:T(8,128)S(1)}) custom-call(s32[4]{0:T(128)S(1)} %copy-done.15, s32[16,8,128]{2,1,0:T(8,128)S(1)} %copy-done.12, bf16[256,1024]{1,0:T(8,128)(2,1)S(1)} %bitcast.20, bf16[1024,2048]{1,0:T(8,128)(2,1)} %get-tuple-element.25.normed_far, ...), custom_call_target="tpu_custom_call" | custom-call | flops 5000000000 | bytes 6000000 | tf_op jit(solution)/shard_map/prepare/pallas_call | solution.py:606
  119.5 0.0 copy-start.3
  119.5 0.8 copy-done.3
  120.3 0.0 copy-start
  120.3 10.1 %all-to-all-done.2 = bf16[16,128,128]{2,1,0:T(8,128)(2,1)S(1)} async-done(((bf16[16,128,128]{2,1,0:T(8,128)(2,1)}), bf16[16,128,128]{2,1,0:T(8,128)(2,1)S(1)}, u32[]{:S(2)}, u32[]{:S(2)}) %all-to-all-start.2) | async-done | bytes 524320 | tf_op jit(solution)/shard_map/all_to_all | solution.py:764
  130.4 0.0 copy-done.1
  130.4 0.0 copy-done.2
  130.4 0.0 copy-done.13
  130.4 0.0 copy-start.4
  130.4 1.0 copy-done.4
  131.5 0.0 copy-start.16
  131.5 0.7 copy-done.16
  132.2 0.0 copy-start.7
  132.2 0.0 copy-start.9
  132.2 3.7 %backward.1 = (bf16[4,128,384]{2,1,0:T(8,128)(2,1)S(1)}, bf16[32,80,1024]{2,1,0:T(8,128)(2,1)S(1)}) custom-call(s32[4]{0:T(128)S(1)} %copy-done.15, f32[2]{0:T(128)S(1)} %copy-done.16, s32[16,16]{1,0:T(8,128)S(1)} %bitcast.24, bf16[128,2048]{1,0:T(8,128)(2,1)S(1)} %copy-done.1, bf16[128,2048]{1,0:T(8,128)(2,1)S(1)} %copy-done.2, ...), custom_call_target="tpu_custom_call" | custom-call | tf_op jit(solution)/shard_map/backward/pallas_call | solution.py:643
  135.8 12.3 %all_to_all.31.head_grads = bf16[4,128,384]{2,1,0:T(8,128)(2,1)S(1)} all-to-all(bf16[4,128,384]{2,1,0:T(8,128)(2,1)S(1)} %get-tuple-element.37), channel_id=1, replica_groups={{0,32,64,96},{128,160,192,224},{256,288,320,352},{384,416,448,480},{1,3..., dimensions={0} | all-to-all | bytes 786432 | tf_op jit(solution)/shard_map/all_to_all | solution.py:742
  148.2 0.0 copy-done.10
  148.2 0.0 copy-done.14
  148.2 0.0 copy-done
  148.2 0.0 copy-done.7
  148.2 0.0 copy-done.9
  148.2 4.2 %cores.1 = bf16[256,1024]{1,0:T(8,128)(2,1)S(1)} custom-call(bf16[128,512]{1,0:T(8,128)(2,1)S(1)} %copy-done.10, bf16[4,128,384]{2,1,0:T(8,128)(2,1)S(1)} %all_to_all.31.head_grads, bf16[32,80,1024]{2,1,0:T(8,128)(2,1)S(1)} %get-tuple-element.38.weights, bf16[128,1024]{1,0:T(8,128)(2,1)S(1)} %bitcast.22, bf16[1024,128]{1,0:T(8,128)(2,1)S(1)} %copy-done.9, ...), custom_call_target="tpu_custom_call" | custom-call | tf_op jit(solution)/shard_map/cores/pallas_call | solution.py:656
  152.4 25.0 %all_to_all.32.received = bf16[32,8,1024]{2,1,0:T(8,128)(2,1)S(1)} all-to-all(bf16[32,8,1024]{2,1,0:T(8,128)(2,1)S(1)} %bitcast.18), channel_id=1, replica_groups=mesh['ctx'=16,'dp'=32] {'dp'}, dimensions={0} | all-to-all | bytes 1048576 | tf_op jit(solution)/shard_map/all_to_all | solution.py:742
  177.4 0.1 sum.1
  177.4 21.3 %all_to_all.33.received = bf16[16,8,1024]{2,1,0:T(8,128)(2,1)S(1)} all-to-all(bf16[16,8,1024]{2,1,0:T(8,128)(2,1)S(1)} %sum.1), channel_id=1, replica_groups=mesh['ctx'=16,'dp'=32] {'ctx'}, dimensions={0} | all-to-all | bytes 524288 | tf_op jit(solution)/shard_map/all_to_all | solution.py:742
  198.7 0.7 last.1
Async XLA Ops:
  7.2 83.7 %all-gather.2.cloned.1.call-start = ((), (), s32[]{:S(2)}) async-start(), calls=%async_computation.6 | async-start | bytes 5406720 | tf_op jit(solution)/shard_map/all_gather | solution.py:752
  36.7 28.8 %copy-start.11 = (s32[16,8,128]{2,1,0:T(8,128)}, s32[16,8,128]{2,1,0:T(8,128)S(1)}, u32[]{:S(2)}) copy-start(s32[16,8,128]{2,1,0:T(8,128)S(1)} %all_to_all.30.indices) | copy-start | bytes 196612
  36.7 28.8 %all-to-all-start.1 = ((bf16[32,8,1024]{2,1,0:T(8,128)(2,1)}), bf16[32,8,1024]{2,1,0:T(8,128)(2,1)S(1)}, u32[]{:S(2)}, u32[]{:S(2)}) async-start(bf16[32,8,1024]{2,1,0:T(8,128)(2,1)} %get-tuple-element.24), calls=%async_computation.1 | async-start | bytes 1048576 | tf_op jit(solution)/shard_map/all_to_all | solution.py:742
  65.5 0.8 copy-start.5
  90.9 21.1 %copy-start.6 = (bf16[32,8,1024]{2,1,0:T(8,128)(2,1)S(1)}, bf16[32,8,1024]{2,1,0:T(8,128)(2,1)}, u32[]{:S(2)}) copy-start(bf16[32,8,1024]{2,1,0:T(8,128)(2,1)} %copy-done.5) | copy-start | bytes 1572868
  90.9 21.1 %copy-start.15 = (s32[4]{0:T(128)S(1)}, s32[4]{0:T(128)}, u32[]{:S(2)}) copy-start(s32[4]{0:T(128)} %pad_add_fusion.info) | copy-start | bytes 52
  99.3 31.2 %all-to-all-start.2 = ((bf16[16,128,128]{2,1,0:T(8,128)(2,1)}), bf16[16,128,128]{2,1,0:T(8,128)(2,1)S(1)}, u32[]{:S(2)}, u32[]{:S(2)}) async-start(bf16[16,128,128]{2,1,0:T(8,128)(2,1)} %get-tuple-element.35), calls=%async_computation.2 | async-start | bytes 1048576 | tf_op jit(solution)/shard_map/all_to_all | solution.py:764
  112.0 1.0 copy-start.8
  112.9 0.8 copy-start.12
  113.8 1.2 copy-start.17
  115.0 0.9 copy-start.18
  115.9 14.5 %copy-start.1 = (bf16[128,2048]{1,0:T(8,128)(2,1)S(1)}, bf16[128,2048]{1,0:T(8,128)(2,1)}, u32[]{:S(2)}) copy-start(bf16[128,2048]{1,0:T(8,128)(2,1)} %get-tuple-element.32.keys_head) | copy-start | bytes 1572868
  115.9 14.5 %copy-start.2 = (bf16[128,2048]{1,0:T(8,128)(2,1)S(1)}, bf16[128,2048]{1,0:T(8,128)(2,1)}, u32[]{:S(2)}) copy-start(bf16[128,2048]{1,0:T(8,128)(2,1)} %get-tuple-element.33.values_head) | copy-start | bytes 1572868
  115.9 14.5 %copy-start.13 = (s32[16,1,16]{2,1,0:T(1,128)S(1)}, s32[16,1,16]{2,1,0:T(1,128)}, u32[]{:S(2)}) copy-start(s32[16,1,16]{2,1,0:T(1,128)} %slice.12) | copy-start | bytes 3076
  115.9 32.3 %copy-start.10 = (bf16[128,512]{1,0:T(8,128)(2,1)S(1)}, bf16[128,512]{1,0:T(8,128)(2,1)}, u32[]{:S(2)}) copy-start(bf16[128,512]{1,0:T(8,128)(2,1)} %get-tuple-element.31.gate_grads) | copy-start | bytes 393220
  115.9 32.3 %copy-start.14 = (s32[8,128]{1,0:T(8,128)S(1)}, s32[8,128]{1,0:T(8,128)}, u32[]{:S(2)}) copy-start(s32[8,128]{1,0:T(8,128)} %get-tuple-element.40.indices) | copy-start | bytes 12292
  119.5 0.8 copy-start.3
  120.3 27.9 %copy-start = (f32[2,1024,128]{2,1,0:T(8,128)S(1)}, f32[2,1024,128]{2,1,0:T(8,128)}, u32[]{:S(2)}) copy-start(f32[2,1024,128]{2,1,0:T(8,128)} %get-tuple-element.39.own_terms) | copy-start | bytes 3145732
  130.4 1.0 copy-start.4
  131.5 0.7 copy-start.16
  132.2 16.0 %copy-start.7 = (bf16[1,128,1024]{2,1,0:T(8,128)(2,1)S(1)}, bf16[1,128,1024]{2,1,0:T(8,128)(2,1)}, u32[]{:S(2)}) copy-start(bf16[1,128,1024]{2,1,0:T(8,128)(2,1)} %param.17) | copy-start | bytes 786436
  132.2 16.0 %copy-start.9 = (bf16[1024,128]{1,0:T(8,128)(2,1)S(1)}, bf16[1024,128]{1,0:T(8,128)(2,1)}, u32[]{:S(2)}) copy-start(bf16[1024,128]{1,0:T(8,128)(2,1)} %get-tuple-element.26.own_embedded) | copy-start | bytes 786436
Sparse Core Ops, SparseCore 0:
  10.7 80.1 all-gather.1
